TPU v7x, 32 devices: a whole 2x2x4 slice. The times are simulated.
32 devices in a mesh: col: 4 (over y, x), row: 8 (over z, core).
Axes of the slice: x: 2, y: 2, z: 4, core: 2. Of those that a mesh axis runs over, the one named last changes fastest.
Arguments:
- sigma_ret: float32 [16384, 16384], P('col', 'row'), may hold values from -0.0625 to 0.0625
- sigma_less: float32 [16384, 16384], P('col', 'row'), may hold values from -0.046875 to 0.046875
- green_less: float32 [16384, 1024], P('row', 'col'), may hold values from -6 to 6
- green_ret: float32 [1024, 16384], P(('col', 'row')), may hold values from -6 to 6
Outputs:
- collision: float32 [16384, 1024], P(('col', 'row'))
All inputs are finite; a program needn't handle non-finite values.
Results may differ from a plain program's by a relative error of at most 0.00007.
Values sent between devices are 32-bit elements; how exact they have to be, the bound alone decides.
No kernel may reach another device: no remote copies, remote signals or barrier semaphores. Data moves between devices by JAX's collectives and lax.ppermute only.
A program may use at most 192 MiB of HBM per device.

v0:
```python
import jax
import jax.numpy as jnp
from jax import lax
from jax.sharding import PartitionSpec as P


def both_terms(sigma_ret, sigma_less, lesser_panel, advanced_panel):
    highest = lax.Precision.HIGHEST
    first_term = jnp.dot(
        sigma_ret, lesser_panel, precision=highest, preferred_element_type=jnp.float32
    )
    second_term = jnp.dot(
        sigma_less, advanced_panel, precision=highest, preferred_element_type=jnp.float32
    )
    return first_term + second_term


def on_device(sigma_ret, sigma_less, green_less, green_ret):
    mirrored = lax.all_to_all(green_ret, "row", split_axis=1, concat_axis=0, tiled=True)
    green_adv = jnp.transpose(mirrored)
    lesser_whole, advanced_whole = (
        lax.all_gather(green_less, "col", axis=1, tiled=True),
        lax.all_gather(green_adv, "col", axis=1, tiled=True),
    )
    return lax.psum_scatter(
        both_terms(sigma_ret, sigma_less, lesser_whole, advanced_whole),
        "row",
        scatter_dimension=0,
        tiled=True,
    )


def solution(mesh):
    placed = (P("col", "row"), P("col", "row"), P("row", "col"), P(("col", "row"), None))
    return jax.shard_map(
        on_device, mesh=mesh, in_specs=placed, out_specs=P(("col", "row"), None), check_vma=False
    )
```

profile of v0, /device:TPU:0, one launch (start us, length us, event | category | flops | bytes accessed | tf_op | source)
XLA Modules:
  0.0 512.6 jit_solution(17424077251653518179)
XLA Ops:
  6.5 0.0 all-gather.3.cloned.1.call-start
  6.5 0.7 all-gather.3.cloned.1.call-update
  7.3 0.0 all-gather.5.cloned.1.call-start
  7.3 1.7 copy.9
  9.0 55.3 %all_to_all.19 = f32[32,8,2048]{2,0,1:T(8,128)} all-to-all(f32[32,8,2048]{2,0,1:T(8,128)S(1)} %bitcast.14), channel_id=1, replica_groups=mesh['col'=4,'row'=8] {'row'}, dimensions={1} | all-to-all | bytes 4194304 | tf_op jit(solution)/shard_map/all_to_all | solution.py:19
  64.3 0.0 all-gather.5.cloned.1.call-update
  64.4 0.0 reduce-scatter.2.cloned.1.call-start
  64.4 35.0 %all-gather.3.cloned.1.call-done = f32[2048,1024]{1,0:T(8,128)} async-done(((f32[2048,256]{1,0:T(8,128)}), f32[2048,1024]{1,0:T(8,128)}) %all-gather.3.cloned.1.call-update) | async-done | bytes 8388624 | tf_op jit(solution)/shard_map/all_gather | solution.py:22
  99.4 115.4 %fusion = f32[4096,1024]{1,0:T(8,128)} fusion(f32[4096,2048]{1,0:T(8,128)} %param.4, f32[2048,1024]{1,0:T(8,128)} %all-gather.3.cloned.1.call-done), kind=kOutput, calls=%fused_computation.2 | convolution fusion | flops 103079215104 | bytes 58720256 | tf_op jit(solution)/shard_map/dot_general | solution.py:9
  214.8 0.0 all-gather.5.cloned.1.call-done
  214.8 122.8 %convolution_add_fusion = f32[4096,1024]{1,0:T(8,128)} fusion(f32[4096,1024]{1,0:T(8,128)} %fusion, f32[4096,2048]{1,0:T(8,128)} %param.5, f32[2048,1024]{0,1:T(8,128)} %all-gather.5.cloned.1.call-done), kind=kOutput, calls=%fused_computation | convolution fusion | flops 103083409408 | bytes 75497472 | tf_op jit(solution)/shard_map/dot_general | solution.py:12
  337.6 0.0 reduce-scatter.2.cloned.1.call-update
  337.7 168.4 %reduce-scatter.2.cloned.1.call-done = f32[512,1024]{1,0:T(8,128)} async-done(((f32[4096,1024]{1,0:T(8,128)}), f32[512,1024]{1,0:T(8,128)}) %reduce-scatter.2.cloned.1.call-update) | async-done | bytes 2097168 | tf_op jit(solution)/shard_map/reduce_scatter | solution.py:25
Async XLA Ops:
  6.5 92.9 %all-gather.3.cloned.1.call-start = ((), (), s32[]{:S(2)}) async-start(), calls=%async_computation.2 | async-start | bytes 10485760 | tf_op jit(solution)/shard_map/all_gather | solution.py:22
  7.3 207.6 %all-gather.5.cloned.1.call-start = ((), (), s32[]{:S(2)}) async-start(), calls=%async_computation.3 | async-start | bytes 10485760 | tf_op jit(solution)/shard_map/all_gather | solution.py:23
  64.4 441.7 %reduce-scatter.2.cloned.1.call-start = ((), (), s32[]{:S(2)}) async-start(), calls=%async_computation.4 | async-start | bytes 18874368 | tf_op jit(solution)/shard_map/reduce_scatter | solution.py:25
Sparse Core Ops, SparseCore 0:
  9.2 90.1 all-gather.2
  101.2 87.6 all-gather.4
  337.8 168.2 reduce-scatter.1
where the time goes:
time: 513 us
  matrix products  238 us (46%)
  waiting for transfers between devices  204 us (40%)
  blocking collectives  55.3 us (11%)
  between operations  13.1 us (3%)
    reduce_scatter x1, waiting for transfers between devices, on_device(): lax.psum_scatter(both_terms(sigma_ret, sigma_less, lesser_whole, advanced...  168 us
    dot_general x1, matrix products, both_terms(): jnp.dot(sigma_less, advanced_panel, precision=highest, preferred_element_...  123 us
    dot_general x1, matrix products, both_terms(): jnp.dot(sigma_ret, lesser_panel, precision=highest, preferred_element_typ...  115 us
    all_to_all x1, blocking collectives, on_device(): lax.all_to_all(green_ret, 'row', split_axis=1, concat_axis=0, tiled=True)  55.3 us
    all_gather x1, waiting for transfers between devices, on_device(): lax.all_gather(green_less, 'col', axis=1, tiled=True)  35 us
  transfers between devices with their start and end apart: 3, of which 2 were waited for; matrix products, arithmetic and copies ran while one was open for 23% of the time, Pallas kernels for 0%

commit v1 on v0

v1 whole, which is shorter than its diff:
```python
import functools

import jax
import jax.numpy as jnp
from jax import lax
from jax.experimental import pallas as pl
from jax.experimental.pallas import tpu as pltpu
from jax.sharding import PartitionSpec as P

F32 = jnp.float32
BF16 = jnp.bfloat16


def bits_of(extent):
    assert extent & (extent - 1) == 0
    return [1 << place for place in range(extent.bit_length() - 1)]


def halving_order(extent):
    order = [0]
    for bit in reversed(bits_of(extent)):
        order = [distance | bit for distance in order] + order
    return order


def cuts(extent, parts, unit):
    edges = [extent * part // parts // unit * unit for part in range(parts)] + [extent]
    return list(zip(edges[:-1], edges[1:]))


def split(values):
    high = values.astype(BF16)
    return high, (values - high.astype(F32)).astype(BF16)


def term_kernel(mirrored, n_parts, n_added, pieces, tiles, where, sigma, *refs):
    parts, added = refs[:n_parts], refs[n_parts : n_parts + n_added]
    out, high, low = refs[n_parts + n_added : n_parts + n_added + 3]

    @pl.when(pl.program_id(0) == 0)
    def _():
        start = 0
        if mirrored:
            whole = refs[-1]
            for part in parts:
                for begin in range(0, part.shape[0], pieces):
                    distance = (start + begin) // pieces
                    place = pl.multiple_of((where[0] ^ distance) * pieces, pieces)
                    whole[pl.ds(place, pieces), :] = part[begin : begin + pieces, :]
                start += part.shape[0]
            high[...], low[...] = split(whole[...])
        else:
            for part in parts:
                rows = slice(start, start + part.shape[0])
                high[rows, :], low[rows, :] = split(part[...])
                start += part.shape[0]

    dims = (((1,), (1 if mirrored else 0,)), ((), ()))
    product = functools.partial(lax.dot_general, dimension_numbers=dims, preferred_element_type=F32)
    sigma_high, sigma_low = split(sigma[...])
    total = product(sigma_high, high[...])
    total += product(sigma_high, low[...])
    total += product(sigma_low, high[...])
    for other in added:
        total += other[...]
    out[...] = total


def term(sigma, parts, tiles, where, added, mirrored, pieces, tile, name):
    depth = sigma.shape[1]
    columns = sum(part.shape[0] for part in parts) if mirrored else parts[0].shape[1]
    held = (columns, depth) if mirrored else (depth, columns)
    steps = tiles.shape[0]
    whole = lambda shape: pl.BlockSpec(shape, lambda i, t, w: (0, 0), pipeline_mode=pl.Buffered(1))
    scratch = [pltpu.VMEM(held, BF16), pltpu.VMEM(held, BF16)]
    if mirrored:
        scratch.append(pltpu.VMEM(held, F32))
    return pl.pallas_call(
        functools.partial(term_kernel, mirrored, len(parts), len(added), pieces),
        out_shape=jax.ShapeDtypeStruct((steps * tile, columns), F32),
        grid_spec=pltpu.PrefetchScalarGridSpec(
            num_scalar_prefetch=2,
            grid=(steps,),
            in_specs=[pl.BlockSpec((tile, depth), lambda i, t, w: (t[i], 0))]
            + [whole(part.shape) for part in parts]
            + [pl.BlockSpec((tile, columns), lambda i, t, w, o=offset // tile: (i + o, 0)) for _, offset in added],
            out_specs=pl.BlockSpec((tile, columns), lambda i, t, w: (i, 0)),
            scratch_shapes=scratch,
        ),
        compiler_params=pltpu.CompilerParams(vmem_limit_bytes=40 << 20),
        cost_estimate=pl.CostEstimate(
            flops=6 * steps * tile * depth * columns,
            bytes_accessed=4 * steps * tile * (depth + columns * (1 + len(added))) + 4 * depth * columns,
            transcendentals=0,
        ),
        name=name,
    )(tiles, where, sigma, *parts, *[array for array, _ in added])


def gather_panels(own, extent, unit):
    held = {0: [own]}
    for distance in sorted(range(1, extent), key=lambda d: (bin(d).count("1"), d)):
        bits = [bit for bit in bits_of(extent) if distance & bit]
        parts = []
        for bit, (begin, end) in zip(bits, cuts(own.shape[0], len(bits), unit)):
            source = held[distance ^ bit]
            source = source[0] if len(source) == 1 else jnp.concatenate(source, axis=0)
            pairs = [(i, i ^ bit) for i in range(extent)]
            parts.append(lax.ppermute(source[begin:end], "col", pairs))
        held[distance] = parts
    return held


def on_device(sigma_ret, sigma_less, green_less, green_ret):
    n_col, n_row = lax.axis_size("col"), lax.axis_size("row")
    col, row = lax.axis_index("col"), lax.axis_index("row")
    rows, depth = sigma_ret.shape
    columns = green_less.shape[1]
    block, pieces = rows // n_row, green_ret.shape[0]
    tile = min(block, 512)

    received = []
    for distance in range(n_row):
        piece = lax.dynamic_slice(green_ret, (0, (row ^ distance) * depth), (pieces, depth))
        if distance:
            piece = lax.ppermute(piece, "row", [(i, i ^ distance) for i in range(n_row)])
        received.append(piece)
    mirrored_own = jnp.concatenate(received, axis=0)

    lesser = gather_panels(green_less, n_col, 16)
    mirrored = gather_panels(mirrored_own, n_col, pieces)

    per_block = block // tile
    order = jnp.asarray(halving_order(n_row), jnp.int32)
    tiles = (((order ^ row) * per_block)[:, None] + jnp.arange(per_block, dtype=jnp.int32)).reshape(-1)
    where = row.astype(jnp.int32).reshape(1)
    half = tiles.shape[0] // 2

    out = jnp.zeros((block, n_col * columns), F32)
    for distance in sorted(range(n_col), key=lambda d: (bin(d).count("1"), d)):
        first = term(sigma_ret, lesser[distance], tiles, where, [], False, pieces, tile, "first_term")
        second = functools.partial(term, sigma_less, mirrored[distance], mirrored=True, pieces=pieces, tile=tile)
        sent = second(tiles[:half], where, [(first, 0)], name="second_sent")
        came = lax.ppermute(sent, "row", [(i, i ^ 1) for i in range(n_row)])
        kept = second(tiles[half:], where, [(first, rows // 2)], name="second_kept")
        sums = [kept, came]
        for bit in bits_of(n_row)[1:]:
            middle = sums[0].shape[0] // 2
            sent = functools.reduce(jnp.add, [array[:middle] for array in sums])
            sums = [array[middle:] for array in sums]
            sums.append(lax.ppermute(sent, "row", [(i, i ^ bit) for i in range(n_row)]))
        final = functools.reduce(jnp.add, sums)
        out = lax.dynamic_update_slice(out, final, (0, (col ^ distance) * columns))
    return out


def solution(mesh):
    placed = (P("col", "row"), P("col", "row"), P("row", "col"), P(("col", "row"), None))
    return jax.shard_map(
        on_device, mesh=mesh, in_specs=placed, out_specs=P(("col", "row"), None), check_vma=False
    )
```

time: 513 us -> 385 us (0.75)
  matrix products: 238 us -> 0 us
  Pallas kernels: 0 us -> 171 us
  waiting for transfers between devices: 204 us -> 139 us
  blocking collectives: 55.3 us -> 0 us
  starting transfers between devices: 0.08 us -> 41.9 us
  other arithmetic: 0 us -> 21.7 us
  between operations: 13.1 us -> 0.35 us
  local copies, waits for them, and re-layouts: 1.73 us -> 9.07 us
    dot_general x2 -> x0, matrix products: 238 us -> none  [the longest x1 123 us: both_terms(): jnp.dot(sigma_less, advanced_panel, precision=highest, preferred_element_...]
    pallas_call x0 -> x12, Pallas kernels: none -> 171 us  [term(): pl.pallas_call(functools.partial(term_kernel, mirrored, len(parts), len(a...]
    reduce_scatter x1 -> x0, waiting for transfers between devices: 168 us -> none  [on_device(): lax.psum_scatter(both_terms(sigma_ret, sigma_less, lesser_whole, advanced...]
    ppermute x0 -> x27, waiting for transfers between devices: none -> 139 us  [the longest x8 107 us: on_device(): sums.append(lax.ppermute(sent, 'row', [(i, i ^ bit) for i in range(n_row)]))]
    all_to_all x1 -> x0, blocking collectives: 55.3 us -> none  [on_device(): lax.all_to_all(green_ret, 'row', split_axis=1, concat_axis=0, tiled=True)]
    ppermute x0 -> x27, starting transfers between devices: none -> 41.9 us  [the longest x8 20.5 us: on_device(): sums.append(lax.ppermute(sent, 'row', [(i, i ^ bit) for i in range(n_row)]))]
    all_gather x2 -> x0, waiting for transfers between devices: 35 us -> none  [the longest x1 35 us: on_device(): lax.all_gather(green_less, 'col', axis=1, tiled=True)]
    add x0 -> x8, other arithmetic: none -> 15.2 us  [on_device(): sent = functools.reduce(jnp.add, [array[:middle] for array in sums])]
  transfers between devices with their start and end apart: 3 -> 27, of which waited for: 2 -> 11; matrix products, arithmetic and copies ran while one was open for 23% -> 7% of each run, Pallas kernels for 0% -> 45%
where the time goes in v1:
time: 385 us; the launch traced here: 383 us
  Pallas kernels  171 us (44%)
  waiting for transfers between devices  139 us (36%)
  starting transfers between devices  41.9 us (11%)
  other arithmetic  21.7 us (6%)
  local copies, waits for them, and re-layouts  9.07 us (2%)
    pallas_call x12, Pallas kernels, term(): pl.pallas_call(functools.partial(term_kernel, mirrored, len(parts), len(a...  171 us
    ppermute x8, waiting for transfers between devices, on_device(): sums.append(lax.ppermute(sent, 'row', [(i, i ^ bit) for i in range(n_row)]))  107 us
    ppermute x7, waiting for transfers between devices, on_device(): lax.ppermute(piece, 'row', [(i, i ^ distance) for i in range(n_row)])  28 us
    ppermute x8, starting transfers between devices, on_device(): sums.append(lax.ppermute(sent, 'row', [(i, i ^ bit) for i in range(n_row)]))  20.5 us
    add x8, other arithmetic, on_device(): sent = functools.reduce(jnp.add, [array[:middle] for array in sums])  15.2 us
    ppermute x7, starting transfers between devices, on_device(): lax.ppermute(piece, 'row', [(i, i ^ distance) for i in range(n_row)])  10.8 us
    ppermute x8, starting transfers between devices, gather_panels(): parts.append(lax.ppermute(source[begin:end], 'col', pairs))  9.82 us
  transfers between devices with their start and end apart: 27, of which 11 were waited for; matrix products, arithmetic and copies ran while one was open for 7% of the time, Pallas kernels for 45%

profile of v1, /device:TPU:0, one launch (start us, length us, event | category | flops | bytes accessed | tf_op | source)
XLA Modules:
  0.0 382.6 jit_solution(9571089575736344334)
XLA Ops:
  0.0 2.9 collective-permute-start.11
  8.2 18.9 %first_term.4.refs_1_ = f32[4096,256]{1,0:T(8,128)S(1)} custom-call(s32[8]{0:T(128)S(1)} %broadcast_xor_fusion.tiles, s32[1]{0:T(128)} %bitcast.where, f32[4096,2048]{1,0:T(8,128)} %sigma.21, f32[2048,256]{1,0:T(8,128)S(1)} %copy-done.7), custom_call_target="tpu_custom_call" | custom-call | flops 12884901888 | bytes 39845888 | tf_op jit(solution)/shard_map/first_term/pallas_call | solution.py:78
  29.9 3.7 collective-permute-start.5
  33.6 20.5 %collective-permute-done.3 = f32[32,2048]{1,0:T(8,128)S(1)} collective-permute-done((f32[32,2048]{1,0:T(8,128)S(1)}, f32[32,2048]{1,0:T(8,128)S(1)}, u32[]{:S(2)}, u32[]{:S(2)}) %collective-permute-start.3) | collective-permute-done | bytes 262176 | tf_op jit(solution)/shard_map/ppermute | solution.py:126
  58.6 5.7 %collective-permute-done.6 = f32[32,2048]{1,0:T(8,128)S(1)} collective-permute-done((f32[32,2048]{1,0:T(8,128)S(1)}, f32[32,2048]{1,0:T(8,128)S(1)}, u32[]{:S(2)}, u32[]{:S(2)}) %collective-permute-start.6) | collective-permute-done | bytes 262176 | tf_op jit(solution)/shard_map/ppermute | solution.py:126
  65.4 11.2 %second_sent.4 = f32[2048,256]{1,0:T(8,128)S(1)} custom-call(s32[4]{0:T(128)S(1)} %get-tuple-element.14.tiles, s32[1]{0:T(128)} %bitcast.where, f32[4096,2048]{1,0:T(8,128)} %sigma.23, f32[256,2048]{1,0:T(8,128)S(1)} %constant_dynamic-update-slice_fusion.refs_0_, f32[4096,256]{1,0:T(8,128)S(1)} %first_term.4.refs_1_), custom_call_target="tpu_custom_call" | custom-call | flops 6442450944 | bytes 23068672 | tf_op jit(solution)/shard_map/second_sent/pallas_call | solution.py:78
  76.9 11.2 %second_kept.4 = f32[2048,256]{1,0:T(8,128)S(1)} custom-call(s32[4]{0:T(128)S(1)} %get-tuple-element.13.tiles, s32[1]{0:T(128)} %bitcast.where, f32[4096,2048]{1,0:T(8,128)} %sigma.23, f32[256,2048]{1,0:T(8,128)S(1)} %constant_dynamic-update-slice_fusion.refs_0_, f32[4096,256]{1,0:T(8,128)S(1)} %first_term.4.refs_1_), custom_call_target="tpu_custom_call" | custom-call | flops 6442450944 | bytes 23068672 | tf_op jit(solution)/shard_map/second_kept/pallas_call | solution.py:78
  95.8 19.5 %first_term.5.refs_1_ = f32[4096,256]{1,0:T(8,128)S(1)} custom-call(s32[8]{0:T(128)S(1)} %broadcast_xor_fusion.tiles, s32[1]{0:T(128)} %bitcast.where, f32[4096,2048]{1,0:T(8,128)} %sigma.21, f32[2048,256]{1,0:T(8,128)} %collective-permute-done.11.refs_0_), custom_call_target="tpu_custom_call" | custom-call | flops 12884901888 | bytes 39845888 | tf_op jit(solution)/shard_map/first_term/pallas_call | solution.py:78
  115.3 19.7 %first_term.6.refs_1_ = f32[4096,256]{1,0:T(8,128)S(1)} custom-call(s32[8]{0:T(128)S(1)} %broadcast_xor_fusion.tiles, s32[1]{0:T(128)} %bitcast.where, f32[4096,2048]{1,0:T(8,128)} %sigma.21, f32[2048,256]{1,0:T(8,128)} %collective-permute-done.16.refs_0_), custom_call_target="tpu_custom_call" | custom-call | flops 12884901888 | bytes 39845888 | tf_op jit(solution)/shard_map/first_term/pallas_call | solution.py:78
  137.4 12.1 %collective-permute-start.8 = (f32[1024,256]{1,0:T(8,128)}, f32[1024,256]{1,0:T(8,128)}, u32[]{:S(2)}, u32[]{:S(2)}) collective-permute-start(f32[1024,256]{1,0:T(8,128)} %slice_add_fusion.3), channel_id=1, source_target_pairs={{0,2},{1,3},{2,0},{3,1},{4,6},{5,7},{6,4},{7,5},{8,10},{9,11},{10,... | collective-permute-start | bytes 3145736 | tf_op jit(solution)/shard_map/ppermute | solution.py:151
  149.4 12.3 %second_sent.5 = f32[2048,256]{1,0:T(8,128)} custom-call(s32[4]{0:T(128)S(1)} %get-tuple-element.14.tiles, s32[1]{0:T(128)} %bitcast.where, f32[4096,2048]{1,0:T(8,128)} %sigma.23, f32[256,2048]{1,0:T(8,128)S(1)} %collective-permute-done.10.refs_0_, f32[4096,256]{1,0:T(8,128)S(1)} %first_term.5.refs_1_), custom_call_target="tpu_custom_call" | custom-call | flops 6442450944 | bytes 23068672 | tf_op jit(solution)/shard_map/second_sent/pallas_call | solution.py:78
  161.7 12.4 %second_sent.6 = f32[2048,256]{1,0:T(8,128)} custom-call(s32[4]{0:T(128)S(1)} %get-tuple-element.14.tiles, s32[1]{0:T(128)} %bitcast.where, f32[4096,2048]{1,0:T(8,128)} %sigma.23, f32[256,2048]{1,0:T(8,128)S(1)} %collective-permute-done.15.refs_0_, f32[4096,256]{1,0:T(8,128)S(1)} %first_term.6.refs_1_), custom_call_target="tpu_custom_call" | custom-call | flops 6442450944 | bytes 23068672 | tf_op jit(solution)/shard_map/second_sent/pallas_call | solution.py:78
  178.1 19.1 %first_term.7.refs_2_ = f32[4096,256]{1,0:T(8,128)S(1)} custom-call(s32[8]{0:T(128)S(1)} %broadcast_xor_fusion.tiles, s32[1]{0:T(128)} %bitcast.where, f32[4096,2048]{1,0:T(8,128)} %sigma.21, f32[1024,256]{1,0:T(8,128)S(1)} %copy-done.9, f32[1024,256]{1,0:T(8,128)} %collective-permute-done.23.refs_1_), custom_call_target="tpu_custom_call" | custom-call | flops 12884901888 | bytes 39845888 | tf_op jit(solution)/shard_map/first_term/pallas_call | solution.py:78
  197.2 3.7 collective-permute-done.20.refs_0_
  201.1 12.2 %second_sent.7 = f32[2048,256]{1,0:T(8,128)} custom-call(s32[4]{0:T(128)S(1)} %get-tuple-element.14.tiles, s32[1]{0:T(128)} %bitcast.where, f32[4096,2048]{1,0:T(8,128)} %sigma.23, f32[128,2048]{1,0:T(8,128)S(1)} %collective-permute-done.20.refs_0_, f32[128,2048]{1,0:T(8,128)S(1)} %collective-permute-done.21.refs_1_, f32[4096,256]{1,0:T(8,128)S(1)} %first_term.7.refs_2_), custom_call_target="tpu_custom_call" | custom-call | flops 6442450944 | bytes 23068672 | tf_op jit(solution)/shard_map/second_sent/pallas_call | solution.py:78
  213.4 11.4 %second_kept.5 = f32[2048,256]{1,0:T(8,128)S(1)} custom-call(s32[4]{0:T(128)S(1)} %get-tuple-element.13.tiles, s32[1]{0:T(128)} %bitcast.where, f32[4096,2048]{1,0:T(8,128)} %sigma.23, f32[256,2048]{1,0:T(8,128)S(1)} %collective-permute-done.10.refs_0_, f32[4096,256]{1,0:T(8,128)S(1)} %first_term.5.refs_1_), custom_call_target="tpu_custom_call" | custom-call | flops 6442450944 | bytes 23068672 | tf_op jit(solution)/shard_map/second_kept/pallas_call | solution.py:78
  224.8 11.4 %second_kept.6 = f32[2048,256]{1,0:T(8,128)S(1)} custom-call(s32[4]{0:T(128)S(1)} %get-tuple-element.13.tiles, s32[1]{0:T(128)} %bitcast.where, f32[4096,2048]{1,0:T(8,128)} %sigma.23, f32[256,2048]{1,0:T(8,128)S(1)} %copy-done.1, f32[4096,256]{1,0:T(8,128)S(1)} %first_term.6.refs_1_), custom_call_target="tpu_custom_call" | custom-call | flops 6442450944 | bytes 23068672 | tf_op jit(solution)/shard_map/second_kept/pallas_call | solution.py:78
  240.2 11.2 %second_kept.7 = f32[2048,256]{1,0:T(8,128)S(1)} custom-call(s32[4]{0:T(128)S(1)} %get-tuple-element.13.tiles, s32[1]{0:T(128)} %bitcast.where, f32[4096,2048]{1,0:T(8,128)} %sigma.23, f32[128,2048]{1,0:T(8,128)S(1)} %collective-permute-done.20.refs_0_, f32[128,2048]{1,0:T(8,128)S(1)} %collective-permute-done.21.refs_1_, f32[4096,256]{1,0:T(8,128)S(1)} %first_term.7.refs_2_), custom_call_target="tpu_custom_call" | custom-call | flops 6442450944 | bytes 23068672 | tf_op jit(solution)/shard_map/second_kept/pallas_call | solution.py:78
  262.4 2.9 collective-permute-done.9
  267.2 20.5 %collective-permute-done.13 = f32[1024,256]{1,0:T(8,128)} collective-permute-done((f32[1024,256]{1,0:T(8,128)S(1)}, f32[1024,256]{1,0:T(8,128)}, u32[]{:S(2)}, u32[]{:S(2)}) %collective-permute-start.13) | collective-permute-done | bytes 1048608 | tf_op jit(solution)/shard_map/ppermute | solution.py:151
  289.7 31.6 %collective-permute-done.18 = f32[1024,256]{1,0:T(8,128)} collective-permute-done((f32[1024,256]{1,0:T(8,128)}, f32[1024,256]{1,0:T(8,128)}, u32[]{:S(2)}, u32[]{:S(2)}) %collective-permute-start.18) | collective-permute-done | bytes 1048608 | tf_op jit(solution)/shard_map/ppermute | solution.py:151
  323.5 20.4 %collective-permute-done.25 = f32[1024,256]{1,0:T(8,128)} collective-permute-done((f32[1024,256]{1,0:T(8,128)}, f32[1024,256]{1,0:T(8,128)}, u32[]{:S(2)}, u32[]{:S(2)}) %collective-permute-start.25) | collective-permute-done | bytes 1048608 | tf_op jit(solution)/shard_map/ppermute | solution.py:151
  347.4 22.0 %collective-permute-done.19 = f32[512,256]{1,0:T(8,128)S(1)} collective-permute-done((f32[512,256]{1,0:T(8,128)S(1)}, f32[512,256]{1,0:T(8,128)S(1)}, u32[]{:S(2)}, u32[]{:S(2)}) %collective-permute-start.19) | collective-permute-done | bytes 524320 | tf_op jit(solution)/shard_map/ppermute | solution.py:151
  370.7 9.8 %collective-permute-done.26 = f32[512,256]{1,0:T(8,128)S(1)} collective-permute-done((f32[512,256]{1,0:T(8,128)S(1)}, f32[512,256]{1,0:T(8,128)S(1)}, u32[]{:S(2)}, u32[]{:S(2)}) %collective-permute-start.26) | collective-permute-done | bytes 524320 | tf_op jit(solution)/shard_map/ppermute | solution.py:151
  (93 shorter events, 56.2 us)
Async XLA Ops:
  0.0 91.9 %collective-permute-start.11 = (f32[2048,256]{1,0:T(8,128)}, f32[2048,256]{1,0:T(8,128)}, u32[]{:S(2)}, u32[]{:S(2)}) collective-permute-start(f32[2048,256]{1,0:T(8,128)} %refs_0_.1), channel_id=1, source_target_pairs={{0,8},{8,0},{16,24},{24,16},{1,9},{9,1},{17,25},{25,17},{2,10},{10... | collective-permute-start | bytes 6291464 | tf_op jit(solution)/shard_map/ppermute | solution.py:109
  2.9 85.2 %collective-permute-start.16 = (f32[2048,256]{1,0:T(8,128)}, f32[2048,256]{1,0:T(8,128)}, u32[]{:S(2)}, u32[]{:S(2)}) collective-permute-start(f32[2048,256]{1,0:T(8,128)} %refs_0_.1), channel_id=1, source_target_pairs={{0,16},{8,24},{16,0},{24,8},{1,17},{9,25},{17,1},{25,9},{2,18},{10... | collective-permute-start | bytes 6291464 | tf_op jit(solution)/shard_map/ppermute | solution.py:109
  6.3 23.4 %collective-permute-start.1 = (f32[32,2048]{1,0:T(8,128)S(1)}, f32[32,2048]{1,0:T(8,128)S(1)}, u32[]{:S(2)}, u32[]{:S(2)}) collective-permute-start(f32[32,2048]{1,0:T(8,128)S(1)} %get-tuple-element.9), channel_id=1, source_target_pairs={{0,2},{1,3},{2,0},{3,1},{4,6},{5,7},{6,4},{7,5},{8,10},{9,11},{10,... | collective-permute-start | bytes 786440 | tf_op jit(solution)/shard_map/ppermute | solution.py:126
  27.2 26.9 %collective-permute-start.3 = (f32[32,2048]{1,0:T(8,128)S(1)}, f32[32,2048]{1,0:T(8,128)S(1)}, u32[]{:S(2)}, u32[]{:S(2)}) collective-permute-start(f32[32,2048]{1,0:T(8,128)S(1)} %get-tuple-element.7), channel_id=1, source_target_pairs={{0,4},{1,5},{2,6},{3,7},{4,0},{5,1},{6,2},{7,3},{8,12},{9,13},{10,... | collective-permute-start | bytes 786440 | tf_op jit(solution)/shard_map/ppermute | solution.py:126
  29.8 28.7 %collective-permute-start.4 = (f32[32,2048]{1,0:T(8,128)S(1)}, f32[32,2048]{1,0:T(8,128)S(1)}, u32[]{:S(2)}, u32[]{:S(2)}) collective-permute-start(f32[32,2048]{1,0:T(8,128)S(1)} %get-tuple-element.6), channel_id=1, source_target_pairs={{0,5},{1,4},{2,7},{3,6},{4,1},{5,0},{6,3},{7,2},{8,13},{9,12},{10,... | collective-permute-start | bytes 786440 | tf_op jit(solution)/shard_map/ppermute | solution.py:126
  29.9 28.6 %collective-permute-start.5 = (f32[32,2048]{1,0:T(8,128)S(1)}, f32[32,2048]{1,0:T(8,128)S(1)}, u32[]{:S(2)}, u32[]{:S(2)}) collective-permute-start(f32[32,2048]{1,0:T(8,128)S(1)} %get-tuple-element.12), channel_id=1, source_target_pairs={{0,6},{1,7},{2,4},{3,5},{4,2},{5,3},{6,0},{7,1},{8,14},{9,15},{10,... | collective-permute-start | bytes 786440 | tf_op jit(solution)/shard_map/ppermute | solution.py:126
  64.3 85.1 %collective-permute-start.10 = (f32[256,2048]{1,0:T(8,128)S(1)}, f32[256,2048]{1,0:T(8,128)S(1)}, u32[]{:S(2)}, u32[]{:S(2)}) collective-permute-start(f32[256,2048]{1,0:T(8,128)S(1)} %constant_dynamic-update-slice_fusion.refs_0_), channel_id=1, source_target_pairs={{0,8},{8,0},{16,24},{24,16},{1,9},{9,1},{17,25},{25,17},{2,10},{10... | collective-permute-start | bytes 6291464 | tf_op jit(solution)/shard_map/ppermute | solution.py:109
  64.9 96.8 %collective-permute-start.15 = (f32[256,2048]{1,0:T(8,128)S(1)}, f32[256,2048]{1,0:T(8,128)S(1)}, u32[]{:S(2)}, u32[]{:S(2)}) collective-permute-start(f32[256,2048]{1,0:T(8,128)S(1)} %constant_dynamic-update-slice_fusion.refs_0_), channel_id=1, source_target_pairs={{0,16},{8,24},{16,0},{24,8},{1,17},{9,25},{17,1},{25,9},{2,18},{10... | collective-permute-start | bytes 6291464 | tf_op jit(solution)/shard_map/ppermute | solution.py:109
  76.6 58.4 %collective-permute-start.7 = (f32[2048,256]{1,0:T(8,128)S(1)}, f32[2048,256]{1,0:T(8,128)}, u32[]{:S(2)}, u32[]{:S(2)}) collective-permute-start(f32[2048,256]{1,0:T(8,128)S(1)} %second_sent.4), channel_id=1, source_target_pairs={{0,1},{1,0},{2,3},{3,2},{4,5},{5,4},{6,7},{7,6},{8,9},{9,8},{10,11... | collective-permute-start | bytes 6291464 | tf_op jit(solution)/shard_map/ppermute | solution.py:144
  90.2 84.6 %collective-permute-start.22 = (f32[1024,256]{1,0:T(8,128)S(1)}, f32[1024,256]{1,0:T(8,128)S(1)}, u32[]{:S(2)}, u32[]{:S(2)}) collective-permute-start(f32[1024,256]{1,0:T(8,128)S(1)} %slice.208), channel_id=1, source_target_pairs={{0,8},{8,0},{16,24},{24,16},{1,9},{9,1},{17,25},{25,17},{2,10},{10... | collective-permute-start | bytes 3145736 | tf_op jit(solution)/shard_map/ppermute | solution.py:109
  94.3 82.1 %collective-permute-start.23 = (f32[1024,256]{1,0:T(8,128)}, f32[1024,256]{1,0:T(8,128)}, u32[]{:S(2)}, u32[]{:S(2)}) collective-permute-start(f32[1024,256]{1,0:T(8,128)} %slice.209), channel_id=1, source_target_pairs={{0,16},{8,24},{16,0},{24,8},{1,17},{9,25},{17,1},{25,9},{2,18},{10... | collective-permute-start | bytes 3145736 | tf_op jit(solution)/shard_map/ppermute | solution.py:109
  137.4 98.8 %collective-permute-start.8 = (f32[1024,256]{1,0:T(8,128)}, f32[1024,256]{1,0:T(8,128)}, u32[]{:S(2)}, u32[]{:S(2)}) collective-permute-start(f32[1024,256]{1,0:T(8,128)} %slice_add_fusion.3), channel_id=1, source_target_pairs={{0,2},{1,3},{2,0},{3,1},{4,6},{5,7},{6,4},{7,5},{8,10},{9,11},{10,... | collective-permute-start | bytes 3145736 | tf_op jit(solution)/shard_map/ppermute | solution.py:151
  161.7 89.7 %collective-permute-start.12 = (f32[2048,256]{1,0:T(8,128)}, f32[2048,256]{1,0:T(8,128)}, u32[]{:S(2)}, u32[]{:S(2)}) collective-permute-start(f32[2048,256]{1,0:T(8,128)} %second_sent.5), channel_id=1, source_target_pairs={{0,1},{1,0},{2,3},{3,2},{4,5},{5,4},{6,7},{7,6},{8,9},{9,8},{10,11... | collective-permute-start | bytes 6291464 | tf_op jit(solution)/shard_map/ppermute | solution.py:144
  174.1 81.5 %collective-permute-start.17 = (f32[2048,256]{1,0:T(8,128)}, f32[2048,256]{1,0:T(8,128)}, u32[]{:S(2)}, u32[]{:S(2)}) collective-permute-start(f32[2048,256]{1,0:T(8,128)} %second_sent.6), channel_id=1, source_target_pairs={{0,1},{1,0},{2,3},{3,2},{4,5},{5,4},{6,7},{7,6},{8,9},{9,8},{10,11... | collective-permute-start | bytes 6291464 | tf_op jit(solution)/shard_map/ppermute | solution.py:144
  175.8 25.1 %collective-permute-start.20 = (f32[128,2048]{1,0:T(8,128)S(1)}, f32[128,2048]{1,0:T(8,128)S(1)}, u32[]{:S(2)}, u32[]{:S(2)}) collective-permute-start(f32[128,2048]{1,0:T(8,128)S(1)} %slice.206), channel_id=1, source_target_pairs={{0,8},{8,0},{16,24},{24,16},{1,9},{9,1},{17,25},{25,17},{2,10},{10... | collective-permute-start | bytes 3145736 | tf_op jit(solution)/shard_map/ppermute | solution.py:109
  176.3 24.8 %collective-permute-start.21 = (f32[128,2048]{1,0:T(8,128)S(1)}, f32[128,2048]{1,0:T(8,128)S(1)}, u32[]{:S(2)}, u32[]{:S(2)}) collective-permute-start(f32[128,2048]{1,0:T(8,128)S(1)} %slice.207), channel_id=1, source_target_pairs={{0,16},{8,24},{16,0},{24,8},{1,17},{9,25},{17,1},{25,9},{2,18},{10... | collective-permute-start | bytes 3145736 | tf_op jit(solution)/shard_map/ppermute | solution.py:109
  213.4 44.6 %collective-permute-start.24 = (f32[2048,256]{1,0:T(8,128)}, f32[2048,256]{1,0:T(8,128)}, u32[]{:S(2)}, u32[]{:S(2)}) collective-permute-start(f32[2048,256]{1,0:T(8,128)} %second_sent.7), channel_id=1, source_target_pairs={{0,1},{1,0},{2,3},{3,2},{4,5},{5,4},{6,7},{7,6},{8,9},{9,8},{10,11... | collective-permute-start | bytes 6291464 | tf_op jit(solution)/shard_map/ppermute | solution.py:144
  238.4 26.9 %collective-permute-start.9 = (f32[512,256]{1,0:T(8,128)}, f32[512,256]{1,0:T(8,128)}, u32[]{:S(2)}, u32[]{:S(2)}) collective-permute-start(f32[512,256]{1,0:T(8,128)} %slice_add_fusion.16), channel_id=1, source_target_pairs={{0,4},{1,5},{2,6},{3,7},{4,0},{5,1},{6,2},{7,3},{8,12},{9,13},{10,... | collective-permute-start | bytes 1572872 | tf_op jit(solution)/shard_map/ppermute | solution.py:151
  253.5 34.1 %collective-permute-start.13 = (f32[1024,256]{1,0:T(8,128)S(1)}, f32[1024,256]{1,0:T(8,128)}, u32[]{:S(2)}, u32[]{:S(2)}) collective-permute-start(f32[1024,256]{1,0:T(8,128)S(1)} %slice_add_fusion.2), channel_id=1, source_target_pairs={{0,2},{1,3},{2,0},{3,1},{4,6},{5,7},{6,4},{7,5},{8,10},{9,11},{10,... | collective-permute-start | bytes 3145736 | tf_op jit(solution)/shard_map/ppermute | solution.py:151
  258.0 63.4 %collective-permute-start.18 = (f32[1024,256]{1,0:T(8,128)}, f32[1024,256]{1,0:T(8,128)}, u32[]{:S(2)}, u32[]{:S(2)}) collective-permute-start(f32[1024,256]{1,0:T(8,128)} %slice_add_fusion.1), channel_id=1, source_target_pairs={{0,2},{1,3},{2,0},{3,1},{4,6},{5,7},{6,4},{7,5},{8,10},{9,11},{10,... | collective-permute-start | bytes 3145736 | tf_op jit(solution)/shard_map/ppermute | solution.py:151
  260.3 83.5 %collective-permute-start.25 = (f32[1024,256]{1,0:T(8,128)}, f32[1024,256]{1,0:T(8,128)}, u32[]{:S(2)}, u32[]{:S(2)}) collective-permute-start(f32[1024,256]{1,0:T(8,128)} %slice_add_fusion), channel_id=1, source_target_pairs={{0,2},{1,3},{2,0},{3,1},{4,6},{5,7},{6,4},{7,5},{8,10},{9,11},{10,... | collective-permute-start | bytes 3145736 | tf_op jit(solution)/shard_map/ppermute | solution.py:151
  288.9 57.1 %collective-permute-start.14 = (f32[512,256]{1,0:T(8,128)S(1)}, f32[512,256]{1,0:T(8,128)S(1)}, u32[]{:S(2)}, u32[]{:S(2)}) collective-permute-start(f32[512,256]{1,0:T(8,128)S(1)} %slice_add_fusion.12), channel_id=1, source_target_pairs={{0,4},{1,5},{2,6},{3,7},{4,0},{5,1},{6,2},{7,3},{8,12},{9,13},{10,... | collective-permute-start | bytes 1572872 | tf_op jit(solution)/shard_map/ppermute | solution.py:151
  322.6 46.7 %collective-permute-start.19 = (f32[512,256]{1,0:T(8,128)S(1)}, f32[512,256]{1,0:T(8,128)S(1)}, u32[]{:S(2)}, u32[]{:S(2)}) collective-permute-start(f32[512,256]{1,0:T(8,128)S(1)} %slice_add_fusion.8), channel_id=1, source_target_pairs={{0,4},{1,5},{2,6},{3,7},{4,0},{5,1},{6,2},{7,3},{8,12},{9,13},{10,... | collective-permute-start | bytes 1572872 | tf_op jit(solution)/shard_map/ppermute | solution.py:151
  345.2 35.3 %collective-permute-start.26 = (f32[512,256]{1,0:T(8,128)S(1)}, f32[512,256]{1,0:T(8,128)S(1)}, u32[]{:S(2)}, u32[]{:S(2)}) collective-permute-start(f32[512,256]{1,0:T(8,128)S(1)} %slice_add_fusion.4), channel_id=1, source_target_pairs={{0,4},{1,5},{2,6},{3,7},{4,0},{5,1},{6,2},{7,3},{8,12},{9,13},{10,... | collective-permute-start | bytes 1572872 | tf_op jit(solution)/shard_map/ppermute | solution.py:151
  (15 other events, 380.3 us)

commit v2 on v0

v2 whole, which is shorter than its diff:
```python
import functools

import jax
import jax.numpy as jnp
from jax import lax
from jax.experimental import pallas as pl
from jax.experimental.pallas import tpu as pltpu
from jax.sharding import PartitionSpec as P

F32 = jnp.float32
BF16 = jnp.bfloat16


def bits_of(extent):
    assert extent & (extent - 1) == 0
    return [1 << place for place in range(extent.bit_length() - 1)]


def halving_order(extent):
    order = [0]
    for bit in reversed(bits_of(extent)):
        order = [distance | bit for distance in order] + order
    return order


def split(values):
    high = values.astype(BF16)
    return high, (values - high.astype(F32)).astype(BF16)


def term_kernel(kinds, streams, n_parts, n_added, n_after, tiles, *refs):
    held, refs = [], list(refs)

    def take(count):
        taken = refs[:count]
        del refs[:count]
        return taken

    for _ in kinds:
        held.append((take(streams), take(n_parts)))
    added, _, out = take(n_added), take(n_after), take(1)[0]
    panels = [take(2) for _ in kinds]

    @pl.when(pl.program_id(0) == 0)
    def _():
        for mirrored, (_, parts), (high_panel, low_panel) in zip(kinds, held, panels):
            column = 0
            for part in parts:
                columns = slice(column, column + part.shape[0 if mirrored else 1])
                place = (columns, slice(None)) if mirrored else (slice(None), columns)
                high_panel[place], low_panel[place] = split(part[...])
                column = columns.stop

    total = None
    for mirrored, (sigma, _), (high_panel, low_panel) in zip(kinds, held, panels):
        dims = (((1,), (1 if mirrored else 0,)), ((), ()))
        halves = [split(stream[...]) for stream in sigma]
        high, low = [jnp.concatenate([half[which] for half in halves], axis=0) for which in range(2)]
        for left, right in ((high, high_panel), (high, low_panel), (low, high_panel)):
            product = lax.dot_general(left, right[...], dims, preferred_element_type=F32)
            total = product if total is None else total + product
    for other in added:
        total += other[...]
    out[...] = total


def sum_of_terms(terms, columns, tiles, added, after, tile, name):
    depth = terms[0][0].shape[1]
    n_parts = len(terms[0][1])
    near = columns // n_parts
    steps, streams = tiles.shape[0], 1
    in_specs, operands, scratch = [], [], []
    for sigma, parts, mirrored in terms:
        for j in range(streams):
            in_specs.append(pl.BlockSpec((tile // streams, depth), lambda i, t, j=j: (t[i] * streams + j, 0)))
            operands.append(sigma)
        for part, place in parts:
            shape, index = ((near, depth), (place, 0)) if mirrored else ((depth, near), (0, place))
            in_specs.append(pl.BlockSpec(shape, lambda i, t, index=index: index, pipeline_mode=pl.Buffered(1)))
            operands.append(part)
        scratch += [pltpu.VMEM((columns, depth) if mirrored else (depth, columns), BF16)] * 2
    for array, offset in added:
        in_specs.append(pl.BlockSpec((tile, columns), lambda i, t, o=offset // tile: (i + o, 0)))
        operands.append(array)
    in_specs += [pl.BlockSpec(memory_space=pl.ANY) for _ in after]
    kinds = [mirrored for _, _, mirrored in terms]
    return pl.pallas_call(
        functools.partial(term_kernel, kinds, streams, n_parts, len(added), len(after)),
        out_shape=jax.ShapeDtypeStruct((steps * tile, columns), F32),
        grid_spec=pltpu.PrefetchScalarGridSpec(
            num_scalar_prefetch=1,
            grid=(steps,),
            in_specs=in_specs,
            out_specs=pl.BlockSpec((tile, columns), lambda i, t: (i, 0)),
            scratch_shapes=scratch,
        ),
        compiler_params=pltpu.CompilerParams(vmem_limit_bytes=40 << 20),
        cost_estimate=pl.CostEstimate(
            flops=48 * len(terms) * steps * tile * depth * columns,
            bytes_accessed=4 * len(terms) * steps * tile * depth,
            transcendentals=0,
        ),
        name=name,
    )(tiles, *operands, *after)


def place_copies(sources, shapes, moves, name, after=()):
    def kernel(*refs):
        for when, source, target in moves(refs[: len(sources)], refs[len(sources) + len(after) :]):

            @pl.when(when)
            def _(source=source, target=target):
                target[...] = source[...]

    return pl.pallas_call(
        kernel,
        out_shape=[jax.ShapeDtypeStruct(shape, F32) for shape in shapes],
        in_specs=[pl.BlockSpec(memory_space=pltpu.VMEM) for _ in sources]
        + [pl.BlockSpec(memory_space=pl.ANY) for _ in after],
        out_specs=[pl.BlockSpec(memory_space=pltpu.VMEM) for _ in shapes],
        compiler_params=pltpu.CompilerParams(vmem_limit_bytes=60 << 20),
        name=name,
    )(*sources, *after)


def hold(values, after):
    return pl.pallas_call(
        lambda *refs: None,
        out_shape=jax.ShapeDtypeStruct(values.shape, values.dtype),
        in_specs=[pl.BlockSpec(memory_space=pl.ANY)] * (1 + len(after)),
        out_specs=pl.BlockSpec(memory_space=pl.ANY),
        input_output_aliases={0: 0},
        name="hold",
    )(values, *after)


def on_device(sigma_ret, sigma_less, green_less, green_ret):
    n_col, n_row = lax.axis_size("col"), lax.axis_size("row")
    col, row = lax.axis_index("col"), lax.axis_index("row")
    rows, depth = sigma_ret.shape
    columns = green_less.shape[1]
    block, pieces = rows // n_row, green_ret.shape[0]
    tile = min(block, 512)
    near = columns // 2
    chips = n_row // 2

    to_row = lambda values, distance: lax.ppermute(values, "row", [(i, i ^ distance) for i in range(n_row)])
    to_col = lambda values, distance: lax.ppermute(values, "col", [(i, i ^ distance) for i in range(n_col)])

    col_bits = bits_of(n_col)
    blocks = [[(0, 0), (0, 1)]] + [[(bit, part) for bit in col_bits] for part in range(2) if col_bits]
    far = sorted([d for d in range(n_col) if d & (d - 1)], key=lambda d: (bin(d).count("1"), d))
    blocks += [[(d, 0), (d, 1)] for d in far]

    def bring(panels, members):
        for distance, part in members:
            bit = distance & -distance if part == 0 else 1 << (distance.bit_length() - 1)
            panels[distance, part] = to_col(panels[distance ^ bit, part], bit)

    def piece(ref, owner):
        return ref.at[:, pl.ds(pl.multiple_of(owner * depth, depth), depth)]

    def rows_of(ref, place, extent):
        return ref.at[pl.ds(pl.multiple_of(place * extent, extent), extent)]

    def crossing_moves(sources, results):
        core = lax.axis_index("row") % 2
        return [
            (True, piece(sources[0], 2 * other + 1 - core), rows_of(results[0], other, pieces)) for other in range(chips)
        ]

    def pair_moves(sources, results):
        chip, core = lax.axis_index("row") // 2, lax.axis_index("row") % 2
        moves = []
        for distance in range(chips):
            other = chip ^ distance
            moves.append((True, piece(sources[0], 2 * other + core), rows_of(results[distance], core, pieces)))
            moves.append((True, rows_of(sources[1], other, pieces), rows_of(results[distance], 1 - core, pieces)))
        return moves

    def panel_moves(sources, results):
        chip, moves = lax.axis_index("row") // 2, []
        for distance in range(chips):
            other = chip ^ distance
            for half in range(2):
                target = rows_of(results[half], other % (chips // 2), 2 * pieces)
                moves.append((other // (chips // 2) == half, sources[distance], target))
        return moves

    crossing = place_copies([green_ret], [(chips * pieces, depth)], crossing_moves, "crossing")[0]
    crossing = to_row(crossing, 1)
    pairs = place_copies([green_ret, crossing], [(2 * pieces, depth)] * chips, pair_moves, "pairs")
    halves = {(0, part): green_less[:, part * near : (part + 1) * near] for part in range(2)}
    if col_bits:
        bring(halves, blocks[1])
    lesser = {(0, part): (green_less, part) if near % 128 == 0 else (halves[0, part], 0) for part in range(2)}

    order = jnp.asarray(halving_order(n_row), jnp.int32)

    def tiles_of(tile, share, shares):
        count = block // tile // shares
        within = share * count + jnp.arange(count, dtype=jnp.int32)
        return (((order ^ row) * (block // tile))[:, None] + within).reshape(-1)

    after = list(pairs[1:])

    def run(terms, members, tiles, added, tile, name):
        result = sum_of_terms(terms, near * len(members), tiles, added, after, tile, name)
        after[:] = [result]
        return result

    def first_of(members):
        return sigma_ret, [lesser.get(m) or (halves[m], 0) for m in members], False

    def second_of(members):
        return sigma_less, [(mirrored[m], 0) for m in members], True

    def run_first(place):
        return run([first_of(blocks[place])], blocks[place], tiles_of(tile, 0, 1), [], tile, "first_term")

    def run_half(place, kept, share, shares):
        members, height = blocks[place], tile // (2 if place > 1 else 1)
        tiles = tiles_of(height, share, shares)
        half = tiles.shape[0] // 2
        tiles = tiles[half:] if kept else tiles[:half]
        if place in firsts:
            added = [(firsts[place], rows // 2 if kept else 0)]
            return run([second_of(members)], members, tiles, added, height, "second_term")
        return run([first_of(members), second_of(members)], members, tiles, [], height, "both_terms")

    def halve(sums, bits):
        if not bits:
            return sums, bits
        middle = sums[0].shape[0] // 2
        sent = functools.reduce(jnp.add, [array[:middle] for array in sums])
        after.append(sent)
        return [array[middle:] for array in sums] + [to_row(sent, bits[0])], bits[1:]

    row_bits = bits_of(n_row)
    firsts, going = {0: run_first(0)}, []
    if col_bits:
        halves[0, 1] = hold(halves[0, 1], after)
        bring(halves, blocks[2])
        firsts[1] = run_first(1)

    came = [pairs[0]] + [to_row(pairs[distance], 2 * distance) for distance in range(1, chips)]
    shapes = [(columns // 2, depth)] * 2
    panels = place_copies(came, shapes, panel_moves, "mirrored", after)
    mirrored = {(0, part): panels[part] for part in range(2)}
    bring(mirrored, blocks[1] if col_bits else [])

    def relay(panels, part, after):
        for distance in far:
            bit = distance & -distance if part == 0 else 1 << (distance.bit_length() - 1)
            source = distance ^ bit, part
            if source in blocks[1] + blocks[2]:
                panels[source] = hold(panels[source], after)
            bring(panels, [(distance, part)])

    def advance(going, out):
        last = [which for which, each in enumerate(going) if each is not None and not each[2]]
        for which, each in enumerate(going):
            if each is not None and each[2]:
                going[which] = [each[0], *halve([hold(each[1][0], after), *each[1][1:]], each[2])]
        for which in last:
            (place, start), sums, _ = going[which]
            going[which] = None
            final = functools.reduce(jnp.add, [hold(sums[0], after), *sums[1:]])
            for index, (distance, part) in enumerate(blocks[place]):
                values = final[:, index * near : (index + 1) * near]
                out = lax.dynamic_update_slice(out, values, (start, (col ^ distance) * columns + part * near))
            after.append(out)
        return out

    out = jnp.zeros((block, n_col * columns), F32)
    for place, members in enumerate(blocks):
        if place == 1:
            after.extend(halves[member] for member in blocks[2])
            mirrored[0, 1] = hold(mirrored[0, 1], after)
            bring(mirrored, blocks[2])
            relay(halves, 0, after)
        if place == 2:
            relay(mirrored, 0, after)
            relay(mirrored, 1, after)
            relay(halves, 1, after)
        shares = 2 if place == len(blocks) - 1 and place > 1 else 1
        for share in range(shares):
            sent = run_half(place, False, share, shares)
            came = to_row(sent, 1)
            if place == 2:
                after.extend(halves[distance, 0] for distance in far)
            kept = run_half(place, True, share, shares)
            now = halve([kept, came], row_bits[1:])
            if place != 1:
                out = advance(going, out)
            going.append([(place, share * (block // shares)), *now])
    while any(each is not None for each in going):
        out = advance(going, out)
    return out


def solution(mesh):
    placed = (P("col", "row"), P("col", "row"), P("row", "col"), P(("col", "row"), None))
    return jax.shard_map(
        on_device, mesh=mesh, in_specs=placed, out_specs=P(("col", "row"), None), check_vma=False
    )
```

time: 513 us -> 337 us (0.66)
  matrix products: 238 us -> 0 us
  Pallas kernels: 0 us -> 185 us
  waiting for transfers between devices: 204 us -> 55 us
  blocking collectives: 55.3 us -> 0 us
  local copies, waits for them, and re-layouts: 1.73 us -> 36.7 us
  other arithmetic: 0 us -> 29.3 us
  starting transfers between devices: 0.08 us -> 29.2 us
  between operations: 13.1 us -> 0.54 us
    dot_general x2 -> x0, matrix products: 238 us -> none  [the longest x1 123 us: both_terms(): jnp.dot(sigma_less, advanced_panel, precision=highest, preferred_element_...]
    pallas_call x0 -> x31, Pallas kernels: none -> 185 us  [the longest x12 175 us: sum_of_terms(): pl.pallas_call(functools.partial(term_kernel, kinds, streams, n_parts, le...]
    reduce_scatter x1 -> x0, waiting for transfers between devices: 168 us -> none  [on_device(): lax.psum_scatter(both_terms(sigma_ret, sigma_less, lesser_whole, advanced...]
    all_to_all x1 -> x0, blocking collectives: 55.3 us -> none  [on_device(): lax.all_to_all(green_ret, 'row', split_axis=1, concat_axis=0, tiled=True)]
    ppermute x0 -> x31, waiting for transfers between devices: none -> 55 us  [the longest x19 33.8 us: on_device(): lax.ppermute(values, 'row', [(i, i ^ distance) for i in range(n_row)])]
    all_gather x2 -> x0, waiting for transfers between devices: 35 us -> none  [the longest x1 35 us: on_device(): lax.all_gather(green_less, 'col', axis=1, tiled=True)]
    unnamed x0 -> x88, local copies, waits for them, and re-layouts: none -> 31.1 us
    ppermute x0 -> x31, starting transfers between devices: none -> 29.2 us  [the longest x19 16 us: on_device(): lax.ppermute(values, 'row', [(i, i ^ distance) for i in range(n_row)])]
  transfers between devices with their start and end apart: 3 -> 31, of which waited for: 2 -> 5; matrix products, arithmetic and copies ran while one was open for 23% -> 10% of each run, Pallas kernels for 0% -> 48%
where the time goes in v2:
time: 337 us; the launch traced here: 335 us
  Pallas kernels  185 us (55%)
  waiting for transfers between devices  55 us (16%)
  local copies, waits for them, and re-layouts  36.7 us (11%)
  other arithmetic  29.3 us (9%)
  starting transfers between devices  29.2 us (9%)
    pallas_call x12, Pallas kernels, sum_of_terms(): pl.pallas_call(functools.partial(term_kernel, kinds, streams, n_parts, le...  175 us
    ppermute x19, waiting for transfers between devices, on_device(): lax.ppermute(values, 'row', [(i, i ^ distance) for i in range(n_row)])  33.8 us
    unnamed x88, local copies, waits for them, and re-layouts  31.1 us
    slice x10, other arithmetic, halve(): array[middle:]  21.7 us
    ppermute x12, waiting for transfers between devices, on_device(): lax.ppermute(values, 'col', [(i, i ^ distance) for i in range(n_col)])  21.2 us
    ppermute x19, starting transfers between devices, on_device(): lax.ppermute(values, 'row', [(i, i ^ distance) for i in range(n_row)])  16 us
    ppermute x12, starting transfers between devices, on_device(): lax.ppermute(values, 'col', [(i, i ^ distance) for i in range(n_col)])  13.2 us
    pallas_call x3, Pallas kernels, place_copies(): pl.pallas_call(kernel, out_shape=[jax.ShapeDtypeStruct(shape, F32) for sh...  9.25 us
  transfers between devices with their start and end apart: 31, of which 5 were waited for; matrix products, arithmetic and copies ran while one was open for 10% of the time, Pallas kernels for 48%

profile of v2, /device:TPU:0, one launch (start us, length us, event | category | flops | bytes accessed | tf_op | source)
XLA Modules:
  0.0 335.4 jit_solution(11350695068297495645)
XLA Ops:
  0.0 2.8 crossing.1
  10.1 3.3 pairs.1
  20.9 18.9 %first_term.2.refs_3_.refs_1_ = f32[4096,256]{1,0:T(8,128)S(1)} custom-call(s32[8]{0:T(128)S(1)} %get-tuple-element.45.tiles, f32[4096,2048]{1,0:T(8,128)} %refs_0_.27, f32[2048,256]{1,0:T(8,128)S(1)} %copy-done.21, f32[2048,256]{1,0:T(8,128)S(1)} %copy-done.21, f32[64,2048]{1,0:T(8,128)S(1)} %copy-done.31, f32[64,2048]{1,0:T(8,128)S(1)} %copy-done.30, ...), custom_call_target="tpu_custom_call" | custom-call | flops 103079215104 | bytes 33554432 | tf_op jit(solution)/shard_map/first_term/pallas_call | solution.py:87
  44.9 19.5 %first_term.3.refs_4_.refs_3_ = f32[4096,256]{1,0:T(8,128)S(1)} custom-call(s32[8]{0:T(128)S(1)} %get-tuple-element.45.tiles, f32[4096,2048]{1,0:T(8,128)} %refs_0_.27, f32[2048,128]{1,0:T(8,128)} %collective-permute-done.4.refs_1_, f32[2048,128]{1,0:T(8,128)} %collective-permute-done.5.refs_2_.refs_0_, f32[4096,256]{1,0:T(8,128)S(1)} %copy-done.18), custom_call_target="tpu_custom_call" | custom-call | flops 103079215104 | bytes 33554432 | tf_op jit(solution)/shard_map/first_term/pallas_call | solution.py:87
  66.4 3.2 mirrored.1
  79.6 11.1 %second_term.4.refs_4_ = f32[2048,256]{1,0:T(8,128)S(1)} custom-call(s32[4]{0:T(128)S(1)} %get-tuple-element.49.tiles, f32[4096,2048]{1,0:T(8,128)} %refs_3_.11, f32[128,2048]{1,0:T(8,128)S(1)} %copy-done.28, f32[128,2048]{1,0:T(8,128)S(1)} %copy-done.23, f32[4096,256]{1,0:T(8,128)S(1)} %copy-done.19, f32[4096,256]{1,0:T(8,128)S(1)} %copy-done.15), custom_call_target="tpu_custom_call" | custom-call | flops 51539607552 | bytes 16777216 | tf_op jit(solution)/shard_map/second_term/pallas_call | solution.py:87
  90.8 10.8 %second_term.5.refs_4_.refs_1_ = f32[2048,256]{1,0:T(8,128)S(1)} custom-call(s32[4]{0:T(128)S(1)} %get-tuple-element.48.tiles, f32[4096,2048]{1,0:T(8,128)} %refs_3_.11, f32[128,2048]{1,0:T(8,128)S(1)} %copy-done.28, f32[128,2048]{1,0:T(8,128)S(1)} %copy-done.23, f32[4096,256]{1,0:T(8,128)S(1)} %copy-done.20, f32[2048,256]{1,0:T(8,128)S(1)} %second_term.4.refs_4_), custom_call_target="tpu_custom_call" | custom-call | flops 51539607552 | bytes 16777216 | tf_op jit(solution)/shard_map/second_term/pallas_call | solution.py:87
  108.4 12.5 %second_term.6.refs_4_ = f32[2048,256]{1,0:T(8,128)} custom-call(s32[4]{0:T(128)S(1)} %get-tuple-element.49.tiles, f32[4096,2048]{1,0:T(8,128)} %refs_3_.11, f32[128,2048]{1,0:T(8,128)} %collective-permute-done.7.refs_1_, f32[128,2048]{1,0:T(8,128)} %collective-permute-done.8.refs_2_.refs_0_, f32[4096,256]{1,0:T(8,128)S(1)} %copy-done.16, ...), custom_call_target="tpu_custom_call" | custom-call | flops 51539607552 | bytes 16777216 | tf_op jit(solution)/shard_map/second_term/pallas_call | solution.py:87
  121.4 11.4 %second_term.7.refs_1_.refs_6_ = f32[2048,256]{1,0:T(8,128)S(1)} custom-call(s32[4]{0:T(128)S(1)} %get-tuple-element.48.tiles, f32[4096,2048]{1,0:T(8,128)} %refs_3_.11, f32[128,2048]{1,0:T(8,128)} %collective-permute-done.7.refs_1_, f32[128,2048]{1,0:T(8,128)} %collective-permute-done.8.refs_2_.refs_0_, f32[4096,256]{1,0:T(8,128)S(1)} %copy-done.16, ...), custom_call_target="tpu_custom_call" | custom-call | flops 51539607552 | bytes 16777216 | tf_op jit(solution)/shard_map/second_term/pallas_call | solution.py:87
  134.2 2.8 fusion.6
  138.8 21.6 %both_terms.6.refs_6_ = f32[2048,256]{1,0:T(8,128)} custom-call(s32[8]{0:T(128)S(1)} %slice.234.tiles, f32[4096,2048]{1,0:T(8,128)} %refs_0_.27, f32[2048,128]{1,0:T(8,128)} %hold.17.refs_1_, f32[2048,128]{1,0:T(8,128)} %collective-permute-done.10.refs_7_.refs_4_.refs_2_, f32[4096,2048]{1,0:T(8,128)} %refs_3_.11, f32[128,2048]{1,0:T(8,128)} %hold.19.refs_4_, ...), custom_call_target="tpu_custom_call" | custom-call | flops 103079215104 | bytes 33554432 | tf_op jit(solution)/shard_map/both_terms/pallas_call | solution.py:87
  165.1 21.2 %collective-permute-done.14.refs_7_.refs_1_ = f32[2048,128]{1,0:T(8,128)S(1)} collective-permute-done((f32[2048,128]{1,0:T(8,128)}, f32[2048,128]{1,0:T(8,128)S(1)}, u32[]{:S(2)}, u32[]{:S(2)}) %collective-permute-start.14) | collective-permute-done | bytes 1048608 | tf_op jit(solution)/shard_map/ppermute | solution.py:148
  188.2 20.6 %both_terms.7.refs_1_.refs_6_ = f32[2048,256]{1,0:T(8,128)S(1)} custom-call(s32[8]{0:T(128)S(1)} %slice.227.tiles, f32[4096,2048]{1,0:T(8,128)} %refs_0_.27, f32[2048,128]{1,0:T(8,128)} %hold.17.refs_1_, f32[2048,128]{1,0:T(8,128)} %collective-permute-done.10.refs_7_.refs_4_.refs_2_, f32[4096,2048]{1,0:T(8,128)} %refs_3_.11, f32[128,2048]{1,0:T(8,128)} %hold.19.refs_4_, ...), custom_call_target="tpu_custom_call" | custom-call | flops 103079215104 | bytes 33554432 | tf_op jit(solution)/shard_map/both_terms/pallas_call | solution.py:87
  208.8 3.5 %fusion.5 = (f32[1024,256]{1,0:T(8,128)}, f32[1024,256]{1,0:T(8,128)}) fusion(f32[2048,256]{1,0:T(8,128)S(1)} %both_terms.7.refs_1_.refs_6_, f32[2048,256]{1,0:T(8,128)} %collective-permute-done.15), kind=kLoop, calls=%fused_computation.44 | loop fusion | flops 262144 | bytes 5242880 | tf_op jit(solution)/shard_map/slice | solution.py:237
  216.7 3.5 %collective-permute-start.23 = (f32[512,256]{1,0:T(8,128)S(1)}, f32[512,256]{1,0:T(8,128)S(1)}, u32[]{:S(2)}, u32[]{:S(2)}) collective-permute-start(f32[512,256]{1,0:T(8,128)S(1)} %copy-done.22), channel_id=1, source_target_pairs={{0,4},{1,5},{2,6},{3,7},{4,0},{5,1},{6,2},{7,3},{8,12},{9,13},{10,... | collective-permute-start | bytes 1572872 | tf_op jit(solution)/shard_map/ppermute | solution.py:147
  222.8 12.1 %both_terms.8.refs_6_ = f32[1024,256]{1,0:T(8,128)S(1)} custom-call(s32[4]{0:T(128)S(1)} %get-tuple-element.46.tiles, f32[4096,2048]{1,0:T(8,128)} %refs_0_.27, f32[2048,128]{1,0:T(8,128)S(1)} %copy-done.25, f32[2048,128]{1,0:T(8,128)} %collective-permute-done.16.refs_2_, f32[4096,2048]{1,0:T(8,128)} %refs_3_.11, ...), custom_call_target="tpu_custom_call" | custom-call | flops 51539607552 | bytes 16777216 | tf_op jit(solution)/shard_map/both_terms/pallas_call | solution.py:87
  235.0 12.1 %both_terms.9.refs_1_.refs_6_ = f32[1024,256]{1,0:T(8,128)S(1)} custom-call(s32[4]{0:T(128)S(1)} %get-tuple-element.47.tiles, f32[4096,2048]{1,0:T(8,128)} %refs_0_.27, f32[2048,128]{1,0:T(8,128)S(1)} %copy-done.25, f32[2048,128]{1,0:T(8,128)} %collective-permute-done.16.refs_2_, f32[4096,2048]{1,0:T(8,128)} %refs_3_.11, ...), custom_call_target="tpu_custom_call" | custom-call | flops 51539607552 | bytes 16777216 | tf_op jit(solution)/shard_map/both_terms/pallas_call | solution.py:87
  250.0 7.6 %collective-permute-done.22 = f32[1024,256]{1,0:T(8,128)} collective-permute-done((f32[1024,256]{1,0:T(8,128)}, f32[1024,256]{1,0:T(8,128)}, u32[]{:S(2)}, u32[]{:S(2)}) %collective-permute-start.22) | collective-permute-done | bytes 1048608 | tf_op jit(solution)/shard_map/ppermute | solution.py:147
  263.5 3.5 %collective-permute-done.24 = f32[512,256]{1,0:T(8,128)} collective-permute-done((f32[512,256]{1,0:T(8,128)S(1)}, f32[512,256]{1,0:T(8,128)}, u32[]{:S(2)}, u32[]{:S(2)}) %collective-permute-start.24) | collective-permute-done | bytes 524320 | tf_op jit(solution)/shard_map/ppermute | solution.py:147
  270.0 12.4 %both_terms.10.refs_6_ = f32[1024,256]{1,0:T(8,128)S(1)} custom-call(s32[4]{0:T(128)S(1)} %get-tuple-element.41.tiles, f32[4096,2048]{1,0:T(8,128)} %refs_0_.27, f32[2048,128]{1,0:T(8,128)S(1)} %copy-done.26, f32[2048,128]{1,0:T(8,128)} %collective-permute-done.16.refs_2_, f32[4096,2048]{1,0:T(8,128)} %refs_3_.11, ...), custom_call_target="tpu_custom_call" | custom-call | flops 51539607552 | bytes 16777216 | tf_op jit(solution)/shard_map/both_terms/pallas_call | solution.py:87
  282.5 12.1 %both_terms.11.refs_1_ = f32[1024,256]{1,0:T(8,128)S(1)} custom-call(s32[4]{0:T(128)S(1)} %get-tuple-element.42.tiles, f32[4096,2048]{1,0:T(8,128)} %refs_0_.27, f32[2048,128]{1,0:T(8,128)S(1)} %copy-done.27, f32[2048,128]{1,0:T(8,128)} %collective-permute-done.16.refs_2_, f32[4096,2048]{1,0:T(8,128)} %refs_3_.11, ...), custom_call_target="tpu_custom_call" | custom-call | flops 51539607552 | bytes 16777216 | tf_op jit(solution)/shard_map/both_terms/pallas_call | solution.py:87
  298.7 2.9 collective-permute-start.29
  305.3 11.7 %collective-permute-done.28 = f32[512,256]{1,0:T(8,128)} collective-permute-done((f32[512,256]{1,0:T(8,128)}, f32[512,256]{1,0:T(8,128)}, u32[]{:S(2)}, u32[]{:S(2)}) %collective-permute-start.28) | collective-permute-done | bytes 524320 | tf_op jit(solution)/shard_map/ppermute | solution.py:147
  322.0 11.0 %collective-permute-done.30 = f32[256,256]{1,0:T(8,128)S(1)} collective-permute-done((f32[256,256]{1,0:T(8,128)S(1)}, f32[256,256]{1,0:T(8,128)S(1)}, u32[]{:S(2)}, u32[]{:S(2)}) %collective-permute-start.30) | collective-permute-done | bytes 262176 | tf_op jit(solution)/shard_map/ppermute | solution.py:147
  (192 shorter events, 82.6 us)
Async XLA Ops:
  4.7 37.2 %collective-permute-start.5 = (f32[2048,128]{1,0:T(8,128)}, f32[2048,128]{1,0:T(8,128)}, u32[]{:S(2)}, u32[]{:S(2)}) collective-permute-start(f32[2048,128]{1,0:T(8,128)} %get-tuple-element.22), channel_id=1, source_target_pairs={{0,16},{8,24},{16,0},{24,8},{1,17},{9,25},{17,1},{25,9},{2,18},{10... | collective-permute-start | bytes 3145736 | tf_op jit(solution)/shard_map/ppermute | solution.py:148
  7.2 35.2 %collective-permute-start.4 = (f32[2048,128]{1,0:T(8,128)}, f32[2048,128]{1,0:T(8,128)}, u32[]{:S(2)}, u32[]{:S(2)}) collective-permute-start(f32[2048,128]{1,0:T(8,128)} %get-tuple-element.22), channel_id=1, source_target_pairs={{0,8},{8,0},{16,24},{24,16},{1,9},{9,1},{17,25},{25,17},{2,10},{10... | collective-permute-start | bytes 3145736 | tf_op jit(solution)/shard_map/ppermute | solution.py:148
  13.4 53.0 %collective-permute-start.1 = (f32[64,2048]{1,0:T(8,128)}, f32[64,2048]{1,0:T(8,128)}, u32[]{:S(2)}, u32[]{:S(2)}) collective-permute-start(f32[64,2048]{1,0:T(8,128)} %get-tuple-element.12.refs_3_), channel_id=1, source_target_pairs={{0,2},{1,3},{2,0},{3,1},{4,6},{5,7},{6,4},{7,5},{8,10},{9,11},{10,... | collective-permute-start | bytes 1572872 | tf_op jit(solution)/shard_map/ppermute | solution.py:147
  15.0 51.4 %collective-permute-start.2 = (f32[64,2048]{1,0:T(8,128)}, f32[64,2048]{1,0:T(8,128)}, u32[]{:S(2)}, u32[]{:S(2)}) collective-permute-start(f32[64,2048]{1,0:T(8,128)} %get-tuple-element.13.refs_4_), channel_id=1, source_target_pairs={{0,4},{1,5},{2,6},{3,7},{4,0},{5,1},{6,2},{7,3},{8,12},{9,13},{10,... | collective-permute-start | bytes 1572872 | tf_op jit(solution)/shard_map/ppermute | solution.py:147
  17.6 48.9 %collective-permute-start.3 = (f32[64,2048]{1,0:T(8,128)}, f32[64,2048]{1,0:T(8,128)}, u32[]{:S(2)}, u32[]{:S(2)}) collective-permute-start(f32[64,2048]{1,0:T(8,128)} %get-tuple-element.14.refs_5_), channel_id=1, source_target_pairs={{0,6},{1,7},{2,4},{3,5},{4,2},{5,3},{6,0},{7,1},{8,14},{9,15},{10,... | collective-permute-start | bytes 1572872 | tf_op jit(solution)/shard_map/ppermute | solution.py:147
  41.9 62.5 %collective-permute-start.10 = (f32[2048,128]{1,0:T(8,128)}, f32[2048,128]{1,0:T(8,128)}, u32[]{:S(2)}, u32[]{:S(2)}) collective-permute-start(f32[2048,128]{1,0:T(8,128)} %hold.16), channel_id=1, source_target_pairs={{0,16},{8,24},{16,0},{24,8},{1,17},{9,25},{17,1},{25,9},{2,18},{10... | collective-permute-start | bytes 3145736 | tf_op jit(solution)/shard_map/ppermute | solution.py:148
  42.4 62.0 %collective-permute-start.6 = (f32[2048,128]{1,0:T(8,128)}, f32[2048,128]{1,0:T(8,128)}, u32[]{:S(2)}, u32[]{:S(2)}) collective-permute-start(f32[2048,128]{1,0:T(8,128)} %hold.16), channel_id=1, source_target_pairs={{0,8},{8,0},{16,24},{24,16},{1,9},{9,1},{17,25},{25,17},{2,10},{10... | collective-permute-start | bytes 3145736 | tf_op jit(solution)/shard_map/ppermute | solution.py:148
  69.6 35.7 %collective-permute-start.8 = (f32[128,2048]{1,0:T(8,128)}, f32[128,2048]{1,0:T(8,128)}, u32[]{:S(2)}, u32[]{:S(2)}) collective-permute-start(f32[128,2048]{1,0:T(8,128)} %get-tuple-element.15.refs_1_), channel_id=1, source_target_pairs={{0,16},{8,24},{16,0},{24,8},{1,17},{9,25},{17,1},{25,9},{2,18},{10... | collective-permute-start | bytes 3145736 | tf_op jit(solution)/shard_map/ppermute | solution.py:148
  71.3 34.0 %collective-permute-start.7 = (f32[128,2048]{1,0:T(8,128)}, f32[128,2048]{1,0:T(8,128)}, u32[]{:S(2)}, u32[]{:S(2)}) collective-permute-start(f32[128,2048]{1,0:T(8,128)} %get-tuple-element.15.refs_1_), channel_id=1, source_target_pairs={{0,8},{8,0},{16,24},{24,16},{1,9},{9,1},{17,25},{25,17},{2,10},{10... | collective-permute-start | bytes 3145736 | tf_op jit(solution)/shard_map/ppermute | solution.py:148
  104.4 32.6 %collective-permute-start.12 = (f32[128,2048]{1,0:T(8,128)}, f32[128,2048]{1,0:T(8,128)}, u32[]{:S(2)}, u32[]{:S(2)}) collective-permute-start(f32[128,2048]{1,0:T(8,128)} %hold.18), channel_id=1, source_target_pairs={{0,8},{8,0},{16,24},{24,16},{1,9},{9,1},{17,25},{25,17},{2,10},{10... | collective-permute-start | bytes 3145736 | tf_op jit(solution)/shard_map/ppermute | solution.py:148
  105.0 32.0 %collective-permute-start.13 = (f32[128,2048]{1,0:T(8,128)}, f32[128,2048]{1,0:T(8,128)}, u32[]{:S(2)}, u32[]{:S(2)}) collective-permute-start(f32[128,2048]{1,0:T(8,128)} %hold.18), channel_id=1, source_target_pairs={{0,16},{8,24},{16,0},{24,8},{1,17},{9,25},{17,1},{25,9},{2,18},{10... | collective-permute-start | bytes 3145736 | tf_op jit(solution)/shard_map/ppermute | solution.py:148
  160.5 26.3 %collective-permute-start.15 = (f32[2048,256]{1,0:T(8,128)}, f32[2048,256]{1,0:T(8,128)}, u32[]{:S(2)}, u32[]{:S(2)}) collective-permute-start(f32[2048,256]{1,0:T(8,128)} %both_terms.6.refs_6_), channel_id=1, source_target_pairs={{0,1},{1,0},{2,3},{3,2},{4,5},{5,4},{6,7},{7,6},{8,9},{9,8},{10,11... | collective-permute-start | bytes 6291464 | tf_op jit(solution)/shard_map/ppermute | solution.py:147
  160.5 25.8 %collective-permute-start.14 = (f32[2048,128]{1,0:T(8,128)}, f32[2048,128]{1,0:T(8,128)S(1)}, u32[]{:S(2)}, u32[]{:S(2)}) collective-permute-start(f32[2048,128]{1,0:T(8,128)} %hold.20), channel_id=1, source_target_pairs={{0,8},{8,0},{16,24},{24,16},{1,9},{9,1},{17,25},{25,17},{2,10},{10... | collective-permute-start | bytes 3145736 | tf_op jit(solution)/shard_map/ppermute | solution.py:148
  161.5 50.8 %collective-permute-start.19 = (f32[1024,256]{1,0:T(8,128)}, f32[1024,256]{1,0:T(8,128)}, u32[]{:S(2)}, u32[]{:S(2)}) collective-permute-start(f32[1024,256]{1,0:T(8,128)} %get-tuple-element.24.refs_5_.refs_2_), channel_id=1, source_target_pairs={{0,2},{1,3},{2,0},{3,1},{4,6},{5,7},{6,4},{7,5},{8,10},{9,11},{10,... | collective-permute-start | bytes 3145736 | tf_op jit(solution)/shard_map/ppermute | solution.py:147
  162.2 53.5 %collective-permute-start.20 = (f32[1024,256]{1,0:T(8,128)S(1)}, f32[1024,256]{1,0:T(8,128)}, u32[]{:S(2)}, u32[]{:S(2)}) collective-permute-start(f32[1024,256]{1,0:T(8,128)S(1)} %copy-done.10), channel_id=1, source_target_pairs={{0,2},{1,3},{2,0},{3,1},{4,6},{5,7},{6,4},{7,5},{8,10},{9,11},{10,... | collective-permute-start | bytes 3145736 | tf_op jit(solution)/shard_map/ppermute | solution.py:147
  163.6 59.2 %collective-permute-start.18 = (f32[128,2048]{1,0:T(8,128)}, f32[128,2048]{1,0:T(8,128)}, u32[]{:S(2)}, u32[]{:S(2)}) collective-permute-start(f32[128,2048]{1,0:T(8,128)} %hold.19.refs_4_), channel_id=1, source_target_pairs={{0,16},{8,24},{16,0},{24,8},{1,17},{9,25},{17,1},{25,9},{2,18},{10... | collective-permute-start | bytes 3145736 | tf_op jit(solution)/shard_map/ppermute | solution.py:148
  186.3 36.5 %collective-permute-start.16 = (f32[2048,128]{1,0:T(8,128)}, f32[2048,128]{1,0:T(8,128)}, u32[]{:S(2)}, u32[]{:S(2)}) collective-permute-start(f32[2048,128]{1,0:T(8,128)} %hold.17.refs_1_), channel_id=1, source_target_pairs={{0,16},{8,24},{16,0},{24,8},{1,17},{9,25},{17,1},{25,9},{2,18},{10... | collective-permute-start | bytes 3145736 | tf_op jit(solution)/shard_map/ppermute | solution.py:148
  186.8 35.9 %collective-permute-start.17 = (f32[128,2048]{1,0:T(8,128)}, f32[128,2048]{1,0:T(8,128)}, u32[]{:S(2)}, u32[]{:S(2)}) collective-permute-start(f32[128,2048]{1,0:T(8,128)} %hold.22), channel_id=1, source_target_pairs={{0,8},{8,0},{16,24},{24,16},{1,9},{9,1},{17,25},{25,17},{2,10},{10... | collective-permute-start | bytes 3145736 | tf_op jit(solution)/shard_map/ppermute | solution.py:148
  212.4 45.3 %collective-permute-start.22 = (f32[1024,256]{1,0:T(8,128)}, f32[1024,256]{1,0:T(8,128)}, u32[]{:S(2)}, u32[]{:S(2)}) collective-permute-start(f32[1024,256]{1,0:T(8,128)} %get-tuple-element.18.refs_2_.refs_7_), channel_id=1, source_target_pairs={{0,2},{1,3},{2,0},{3,1},{4,6},{5,7},{6,4},{7,5},{8,10},{9,11},{10,... | collective-permute-start | bytes 3145736 | tf_op jit(solution)/shard_map/ppermute | solution.py:147
  216.7 43.6 %collective-permute-start.23 = (f32[512,256]{1,0:T(8,128)S(1)}, f32[512,256]{1,0:T(8,128)S(1)}, u32[]{:S(2)}, u32[]{:S(2)}) collective-permute-start(f32[512,256]{1,0:T(8,128)S(1)} %copy-done.22), channel_id=1, source_target_pairs={{0,4},{1,5},{2,6},{3,7},{4,0},{5,1},{6,2},{7,3},{8,12},{9,13},{10,... | collective-permute-start | bytes 1572872 | tf_op jit(solution)/shard_map/ppermute | solution.py:147
  222.7 44.3 %collective-permute-start.24 = (f32[512,256]{1,0:T(8,128)S(1)}, f32[512,256]{1,0:T(8,128)}, u32[]{:S(2)}, u32[]{:S(2)}) collective-permute-start(f32[512,256]{1,0:T(8,128)S(1)} %get-tuple-element.32.refs_9_), channel_id=1, source_target_pairs={{0,4},{1,5},{2,6},{3,7},{4,0},{5,1},{6,2},{7,3},{8,12},{9,13},{10,... | collective-permute-start | bytes 1572872 | tf_op jit(solution)/shard_map/ppermute | solution.py:147
  249.3 47.4 %collective-permute-start.26 = (f32[512,256]{1,0:T(8,128)}, f32[512,256]{1,0:T(8,128)}, u32[]{:S(2)}, u32[]{:S(2)}) collective-permute-start(f32[512,256]{1,0:T(8,128)} %get-tuple-element.28.refs_2_.refs_7_), channel_id=1, source_target_pairs={{0,2},{1,3},{2,0},{3,1},{4,6},{5,7},{6,4},{7,5},{8,10},{9,11},{10,... | collective-permute-start | bytes 1572872 | tf_op jit(solution)/shard_map/ppermute | solution.py:147
  260.3 41.3 %collective-permute-start.27 = (f32[512,256]{1,0:T(8,128)}, f32[512,256]{1,0:T(8,128)}, u32[]{:S(2)}, u32[]{:S(2)}) collective-permute-start(f32[512,256]{1,0:T(8,128)} %get-tuple-element.30.refs_3_.refs_8_), channel_id=1, source_target_pairs={{0,4},{1,5},{2,6},{3,7},{4,0},{5,1},{6,2},{7,3},{8,12},{9,13},{10,... | collective-permute-start | bytes 1572872 | tf_op jit(solution)/shard_map/ppermute | solution.py:147
  298.7 20.9 %collective-permute-start.29 = (f32[256,256]{1,0:T(8,128)S(1)}, f32[256,256]{1,0:T(8,128)S(1)}, u32[]{:S(2)}, u32[]{:S(2)}) collective-permute-start(f32[256,256]{1,0:T(8,128)S(1)} %get-tuple-element.38.refs_3_), channel_id=1, source_target_pairs={{0,4},{1,5},{2,6},{3,7},{4,0},{5,1},{6,2},{7,3},{8,12},{9,13},{10,... | collective-permute-start | bytes 786440 | tf_op jit(solution)/shard_map/ppermute | solution.py:147
  (50 other events, 305.5 us)

commit v3 on v2

--- a/solution.py
+++ b/solution.py
@@ -94,7 +94,7 @@
             out_specs=pl.BlockSpec((tile, columns), lambda i, t: (i, 0)),
             scratch_shapes=scratch,
         ),
-        compiler_params=pltpu.CompilerParams(vmem_limit_bytes=40 << 20),
+        compiler_params=pltpu.CompilerParams(vmem_limit_bytes=60 << 20),
         cost_estimate=pl.CostEstimate(
             flops=48 * len(terms) * steps * tile * depth * columns,
             bytes_accessed=4 * len(terms) * steps * tile * depth,
@@ -271,6 +271,19 @@
                 out = lax.dynamic_update_slice(out, values, (start, (col ^ distance) * columns + part * near))
             after.append(out)
         return out
+
+    def halve_sums(going):
+        where, sums, bits = going[0]
+        sums = [hold(sums[0], after), *sums[1:]]
+        middle = sums[0].shape[0] // 2
+        sent = functools.reduce(jnp.add, [array[:middle] for array in sums])
+        after.append(sent)
+        return sent, [array[middle:] for array in sums]
+
+    def send_later(going, later):
+        where, _, bits = going[0]
+        sent, kept = later
+        going[0] = [where, [*kept, to_row(hold(sent, after), bits[0])], bits[1:]]
 
     out = jnp.zeros((block, n_col * columns), F32)
     for place, members in enumerate(blocks):
@@ -291,8 +304,14 @@
                 after.extend(halves[distance, 0] for distance in far)
             kept = run_half(place, True, share, shares)
             now = halve([kept, came], row_bits[1:])
-            if place != 1:
-                out = advance(going, out)
+            if place == 1:
+                later = halve_sums(going)
+            else:
+                if place == 2:
+                    send_later(going, later)
+                    going[1:] = [[each[0], *halve([hold(each[1][0], after), *each[1][1:]], each[2])] for each in going[1:]]
+                else:
+                    out = advance(going, out)
             going.append([(place, share * (block // shares)), *now])
     while any(each is not None for each in going):
         out = advance(going, out)

time: 337 us -> 317 us (0.941)
  waiting for transfers between devices: 55 us -> 30.2 us
  local copies, waits for them, and re-layouts: 36.7 us -> 19.1 us
  Pallas kernels: 185 us -> 200 us
  other arithmetic: 29.3 us -> 34.9 us
    ppermute x12, waiting for transfers between devices: 21.2 us -> 0.03 us  [on_device(): lax.ppermute(values, 'col', [(i, i ^ distance) for i in range(n_col)])]
    unnamed x88 -> x42, local copies, waits for them, and re-layouts: 31.1 us -> 10.2 us
    pallas_call x12, Pallas kernels: 175 us -> 191 us  [sum_of_terms(): pl.pallas_call(functools.partial(term_kernel, kinds, streams, n_parts, le...]
    ppermute x19, waiting for transfers between devices: 33.8 us -> 30.2 us  [on_device(): lax.ppermute(values, 'row', [(i, i ^ distance) for i in range(n_row)])]
    slice x10 -> x9, other arithmetic: 21.7 us -> 24.9 us  [halve(): array[middle:]]
  transfers between devices with their start and end apart: 31 -> 31, of which waited for: 5 -> 3; matrix products, arithmetic and copies ran while one was open for 10% -> 13% of each run, Pallas kernels for 48% -> 63%
where the time goes in v3:
time: 317 us; the launch traced here: 316 us
  Pallas kernels  200 us (63%)
  other arithmetic  34.9 us (11%)
  starting transfers between devices  30.8 us (10%)
  waiting for transfers between devices  30.2 us (10%)
  local copies, waits for them, and re-layouts  19.1 us (6%)
    pallas_call x12, Pallas kernels, sum_of_terms(): pl.pallas_call(functools.partial(term_kernel, kinds, streams, n_parts, le...  191 us
    ppermute x19, waiting for transfers between devices, on_device(): lax.ppermute(values, 'row', [(i, i ^ distance) for i in range(n_row)])  30.2 us
    slice x9, other arithmetic, halve(): array[middle:]  24.9 us
    ppermute x19, starting transfers between devices, on_device(): lax.ppermute(values, 'row', [(i, i ^ distance) for i in range(n_row)])  15.7 us
    ppermute x12, starting transfers between devices, on_device(): lax.ppermute(values, 'col', [(i, i ^ distance) for i in range(n_col)])  15.1 us
    unnamed x42, local copies, waits for them, and re-layouts  10.2 us
    pallas_call x3, Pallas kernels, place_copies(): pl.pallas_call(kernel, out_shape=[jax.ShapeDtypeStruct(shape, F32) for sh...  9.15 us
    add x5, other arithmetic, advance(): final = functools.reduce(jnp.add, [hold(sums[0], after), *sums[1:]])  7.46 us
  transfers between devices with their start and end apart: 31, of which 3 were waited for; matrix products, arithmetic and copies ran while one was open for 13% of the time, Pallas kernels for 63%

profile of v3, /device:TPU:0, one launch (start us, length us, event | category | flops | bytes accessed | tf_op | source)
XLA Modules:
  0.0 315.8 jit_solution(4818661831186820864)
XLA Ops:
  0.0 2.7 fusion.7
  2.7 2.9 collective-permute-start.4
  14.0 3.3 %pairs.1 = (f32[64,2048]{1,0:T(8,128)}, f32[64,2048]{1,0:T(8,128)}, f32[64,2048]{1,0:T(8,128)}, f32[64,2048]{1,0:T(8,128)}) custom-call(f32[32,16384]{1,0:T(8,128)} %refs_0_.15, f32[128,2048]{1,0:T(8,128)} %copy-done.14), custom_call_target="tpu_custom_call" | custom-call | tf_op jit(solution)/shard_map/pairs/pallas_call | solution.py:115
  21.7 21.2 %first_term.2.refs_3_.refs_1_ = f32[4096,256]{1,0:T(8,128)} custom-call(s32[8]{0:T(128)} %copy-done.17, f32[4096,2048]{1,0:T(8,128)} %refs_0_.27, f32[2048,256]{1,0:T(8,128)} %refs_2_.1, f32[2048,256]{1,0:T(8,128)} %refs_2_.1, f32[64,2048]{1,0:T(8,128)} %get-tuple-element.12.refs_3_, f32[64,2048]{1,0:T(8,128)} %get-tuple-element.13.refs_4_, ...), custom_call_target="tpu_custom_call" | custom-call | flops 103079215104 | bytes 33554432 | tf_op jit(solution)/shard_map/first_term/pallas_call | solution.py:87
  44.4 21.2 %first_term.3.refs_4_.refs_3_ = f32[4096,256]{1,0:T(8,128)} custom-call(s32[8]{0:T(128)} %copy-done.17, f32[4096,2048]{1,0:T(8,128)} %refs_0_.27, f32[2048,128]{1,0:T(8,128)} %collective-permute-done.4.refs_1_, f32[2048,128]{1,0:T(8,128)} %copy-done.13, f32[4096,256]{1,0:T(8,128)} %first_term.2.refs_3_.refs_1_), custom_call_target="tpu_custom_call" | custom-call | flops 103079215104 | bytes 33554432 | tf_op jit(solution)/shard_map/first_term/pallas_call | solution.py:87
  65.6 3.2 %mirrored.1 = (f32[128,2048]{1,0:T(8,128)}, f32[128,2048]{1,0:T(8,128)}) custom-call(f32[64,2048]{1,0:T(8,128)} %get-tuple-element.11.refs_0_, f32[64,2048]{1,0:T(8,128)} %collective-permute-done.1.refs_1_, f32[64,2048]{1,0:T(8,128)} %collective-permute-done.2.refs_2_, f32[64,2048]{1,0:T(8,128)} %collective-permute-done.3.refs_3_, ...), custom_call_target="tpu_custom_call" | custom-call | tf_op jit(solution)/shard_map/mirrored/pallas_call | solution.py:115
  71.3 12.9 %second_term.4.refs_4_ = f32[2048,256]{1,0:T(8,128)} custom-call(s32[4]{0:T(128)} %get-tuple-element.49.tiles, f32[4096,2048]{1,0:T(8,128)} %refs_3_.11, f32[128,2048]{1,0:T(8,128)} %get-tuple-element.15.refs_1_, f32[128,2048]{1,0:T(8,128)} %get-tuple-element.16.refs_2_.refs_0_, f32[4096,256]{1,0:T(8,128)} %first_term.2.refs_3_.refs_1_, ...), custom_call_target="tpu_custom_call" | custom-call | flops 51539607552 | bytes 16777216 | tf_op jit(solution)/shard_map/second_term/pallas_call | solution.py:87
  84.2 12.9 %second_term.5.refs_4_.refs_1_ = f32[2048,256]{1,0:T(8,128)} custom-call(s32[4]{0:T(128)} %get-tuple-element.48.tiles, f32[4096,2048]{1,0:T(8,128)} %refs_3_.11, f32[128,2048]{1,0:T(8,128)} %get-tuple-element.15.refs_1_, f32[128,2048]{1,0:T(8,128)} %get-tuple-element.16.refs_2_.refs_0_, f32[4096,256]{1,0:T(8,128)} %first_term.2.refs_3_.refs_1_, ...), custom_call_target="tpu_custom_call" | custom-call | flops 51539607552 | bytes 16777216 | tf_op jit(solution)/shard_map/second_term/pallas_call | solution.py:87
  97.1 3.5 %fusion.8 = (f32[1024,256]{1,0:T(8,128)}, f32[1024,256]{1,0:T(8,128)S(1)}) fusion(f32[2048,256]{1,0:T(8,128)} %second_term.5.refs_4_.refs_1_, f32[2048,256]{1,0:T(8,128)S(1)} %collective-permute-done.8), kind=kLoop, calls=%fused_computation.47 | loop fusion | flops 262144 | bytes 5242880 | tf_op jit(solution)/shard_map/slice | solution.py:237
  105.0 12.9 %second_term.6.refs_4_ = f32[2048,256]{1,0:T(8,128)} custom-call(s32[4]{0:T(128)} %get-tuple-element.49.tiles, f32[4096,2048]{1,0:T(8,128)} %refs_3_.11, f32[128,2048]{1,0:T(8,128)} %collective-permute-done.6.refs_1_, f32[128,2048]{1,0:T(8,128)} %collective-permute-done.7.refs_2_.refs_0_, f32[4096,256]{1,0:T(8,128)} %first_term.3.refs_4_.refs_3_, ...), custom_call_target="tpu_custom_call" | custom-call | flops 51539607552 | bytes 16777216 | tf_op jit(solution)/shard_map/second_term/pallas_call | solution.py:87
  118.5 12.9 %second_term.7.refs_1_.refs_6_ = f32[2048,256]{1,0:T(8,128)} custom-call(s32[4]{0:T(128)} %get-tuple-element.48.tiles, f32[4096,2048]{1,0:T(8,128)} %refs_3_.11, f32[128,2048]{1,0:T(8,128)} %collective-permute-done.6.refs_1_, f32[128,2048]{1,0:T(8,128)} %collective-permute-done.7.refs_2_.refs_0_, f32[4096,256]{1,0:T(8,128)} %first_term.3.refs_4_.refs_3_, ...), custom_call_target="tpu_custom_call" | custom-call | flops 51539607552 | bytes 16777216 | tf_op jit(solution)/shard_map/second_term/pallas_call | solution.py:87
  131.4 3.4 %fusion.6 = (f32[1024,256]{1,0:T(8,128)}, f32[1024,256]{1,0:T(8,128)}) fusion(f32[2048,256]{1,0:T(8,128)} %second_term.7.refs_1_.refs_6_, f32[2048,256]{1,0:T(8,128)} %collective-permute-done.11), kind=kLoop, calls=%fused_computation.45 | loop fusion | flops 262144 | bytes 5242880 | tf_op jit(solution)/shard_map/slice | solution.py:237
  140.2 22.0 %both_terms.6.refs_6_ = f32[2048,256]{1,0:T(8,128)} custom-call(s32[8]{0:T(128)} %slice.240.tiles, f32[4096,2048]{1,0:T(8,128)} %refs_0_.27, f32[2048,128]{1,0:T(8,128)} %hold.20.refs_1_, f32[2048,128]{1,0:T(8,128)} %collective-permute-done.10.refs_7_.refs_4_.refs_2_, f32[4096,2048]{1,0:T(8,128)} %refs_3_.11, f32[128,2048]{1,0:T(8,128)} %hold.23.refs_4_, ...), custom_call_target="tpu_custom_call" | custom-call | flops 103079215104 | bytes 33554432 | tf_op jit(solution)/shard_map/both_terms/pallas_call | solution.py:87
  163.8 21.8 %both_terms.7.refs_1_.refs_6_ = f32[2048,256]{1,0:T(8,128)} custom-call(s32[8]{0:T(128)} %slice.238.tiles, f32[4096,2048]{1,0:T(8,128)} %refs_0_.27, f32[2048,128]{1,0:T(8,128)} %hold.20.refs_1_, f32[2048,128]{1,0:T(8,128)} %collective-permute-done.10.refs_7_.refs_4_.refs_2_, f32[4096,2048]{1,0:T(8,128)} %refs_3_.11, f32[128,2048]{1,0:T(8,128)} %hold.23.refs_4_, ...), custom_call_target="tpu_custom_call" | custom-call | flops 103079215104 | bytes 33554432 | tf_op jit(solution)/shard_map/both_terms/pallas_call | solution.py:87
  185.6 3.8 %fusion.5 = (f32[1024,256]{1,0:T(8,128)}, f32[1024,256]{1,0:T(8,128)}) fusion(f32[2048,256]{1,0:T(8,128)} %both_terms.7.refs_1_.refs_6_, f32[2048,256]{1,0:T(8,128)S(1)} %collective-permute-done.19), kind=kLoop, calls=%fused_computation.44 | loop fusion | flops 262144 | bytes 5242880 | tf_op jit(solution)/shard_map/slice | solution.py:237
  194.7 2.6 fusion.12
  199.4 13.4 %both_terms.8.refs_6_ = f32[1024,256]{1,0:T(8,128)} custom-call(s32[4]{0:T(128)} %get-tuple-element.46.tiles, f32[4096,2048]{1,0:T(8,128)} %refs_0_.27, f32[2048,128]{1,0:T(8,128)} %collective-permute-done.12.refs_7_.refs_1_, f32[2048,128]{1,0:T(8,128)} %collective-permute-done.14.refs_2_, f32[4096,2048]{1,0:T(8,128)} %refs_3_.11, f32[128,2048]{1,0:T(8,128)} %copy-done.19, ...), custom_call_target="tpu_custom_call" | custom-call | flops 51539607552 | bytes 16777216 | tf_op jit(solution)/shard_map/both_terms/pallas_call | solution.py:87
  212.7 13.3 %both_terms.9.refs_1_.refs_6_ = f32[1024,256]{1,0:T(8,128)} custom-call(s32[4]{0:T(128)} %get-tuple-element.47.tiles, f32[4096,2048]{1,0:T(8,128)} %refs_0_.27, f32[2048,128]{1,0:T(8,128)} %collective-permute-done.12.refs_7_.refs_1_, f32[2048,128]{1,0:T(8,128)} %collective-permute-done.14.refs_2_, f32[4096,2048]{1,0:T(8,128)} %refs_3_.11, ...), custom_call_target="tpu_custom_call" | custom-call | flops 51539607552 | bytes 16777216 | tf_op jit(solution)/shard_map/both_terms/pallas_call | solution.py:87
  229.5 8.6 %collective-permute-done.22 = f32[1024,256]{1,0:T(8,128)} collective-permute-done((f32[1024,256]{1,0:T(8,128)S(1)}, f32[1024,256]{1,0:T(8,128)}, u32[]{:S(2)}, u32[]{:S(2)}) %collective-permute-start.22) | collective-permute-done | bytes 1048608 | tf_op jit(solution)/shard_map/ppermute | solution.py:147
  238.1 2.6 fusion.11
  247.1 13.6 %both_terms.10.refs_6_ = f32[1024,256]{1,0:T(8,128)} custom-call(s32[4]{0:T(128)} %get-tuple-element.41.tiles, f32[4096,2048]{1,0:T(8,128)} %refs_0_.27, f32[2048,128]{1,0:T(8,128)} %collective-permute-done.12.refs_7_.refs_1_, f32[2048,128]{1,0:T(8,128)} %collective-permute-done.14.refs_2_, f32[4096,2048]{1,0:T(8,128)} %refs_3_.11, f32[128,2048]{1,0:T(8,128)} %copy-done.19, ...), custom_call_target="tpu_custom_call" | custom-call | flops 51539607552 | bytes 16777216 | tf_op jit(solution)/shard_map/both_terms/pallas_call | solution.py:87
  260.7 13.4 %both_terms.11.refs_1_ = f32[1024,256]{1,0:T(8,128)} custom-call(s32[4]{0:T(128)} %get-tuple-element.42.tiles, f32[4096,2048]{1,0:T(8,128)} %refs_0_.27, f32[2048,128]{1,0:T(8,128)} %collective-permute-done.12.refs_7_.refs_1_, f32[2048,128]{1,0:T(8,128)} %collective-permute-done.14.refs_2_, f32[4096,2048]{1,0:T(8,128)} %refs_3_.11, f32[128,2048]{1,0:T(8,128)} %copy-done.19, ...), custom_call_target="tpu_custom_call" | custom-call | flops 51539607552 | bytes 16777216 | tf_op jit(solution)/shard_map/both_terms/pallas_call | solution.py:87
  286.6 10.3 %collective-permute-done.28 = f32[512,256]{1,0:T(8,128)} collective-permute-done((f32[512,256]{1,0:T(8,128)S(1)}, f32[512,256]{1,0:T(8,128)}, u32[]{:S(2)}, u32[]{:S(2)}) %collective-permute-start.28) | collective-permute-done | bytes 524320 | tf_op jit(solution)/shard_map/ppermute | solution.py:147
  302.0 11.3 %collective-permute-done.30 = f32[256,256]{1,0:T(8,128)S(1)} collective-permute-done((f32[256,256]{1,0:T(8,128)S(1)}, f32[256,256]{1,0:T(8,128)S(1)}, u32[]{:S(2)}, u32[]{:S(2)}) %collective-permute-start.30) | collective-permute-done | bytes 262176 | tf_op jit(solution)/shard_map/ppermute | solution.py:147
  (147 shorter events, 66.0 us)
Async XLA Ops:
  2.7 40.2 %collective-permute-start.4 = (f32[2048,128]{1,0:T(8,128)S(1)}, f32[2048,128]{1,0:T(8,128)}, u32[]{:S(2)}, u32[]{:S(2)}) collective-permute-start(f32[2048,128]{1,0:T(8,128)S(1)} %get-tuple-element.22), channel_id=1, source_target_pairs={{0,8},{8,0},{16,24},{24,16},{1,9},{9,1},{17,25},{25,17},{2,10},{10... | collective-permute-start | bytes 3145736 | tf_op jit(solution)/shard_map/ppermute | solution.py:148
  5.6 37.8 %collective-permute-start.5 = (f32[2048,128]{1,0:T(8,128)S(1)}, f32[2048,128]{1,0:T(8,128)S(1)}, u32[]{:S(2)}, u32[]{:S(2)}) collective-permute-start(f32[2048,128]{1,0:T(8,128)S(1)} %get-tuple-element.22), channel_id=1, source_target_pairs={{0,16},{8,24},{16,0},{24,8},{1,17},{9,25},{17,1},{25,9},{2,18},{10... | collective-permute-start | bytes 3145736 | tf_op jit(solution)/shard_map/ppermute | solution.py:148
  17.3 48.3 %collective-permute-start.1 = (f32[64,2048]{1,0:T(8,128)}, f32[64,2048]{1,0:T(8,128)}, u32[]{:S(2)}, u32[]{:S(2)}) collective-permute-start(f32[64,2048]{1,0:T(8,128)} %get-tuple-element.12.refs_3_), channel_id=1, source_target_pairs={{0,2},{1,3},{2,0},{3,1},{4,6},{5,7},{6,4},{7,5},{8,10},{9,11},{10,... | collective-permute-start | bytes 1572872 | tf_op jit(solution)/shard_map/ppermute | solution.py:147
  18.9 46.7 %collective-permute-start.2 = (f32[64,2048]{1,0:T(8,128)}, f32[64,2048]{1,0:T(8,128)}, u32[]{:S(2)}, u32[]{:S(2)}) collective-permute-start(f32[64,2048]{1,0:T(8,128)} %get-tuple-element.13.refs_4_), channel_id=1, source_target_pairs={{0,4},{1,5},{2,6},{3,7},{4,0},{5,1},{6,2},{7,3},{8,12},{9,13},{10,... | collective-permute-start | bytes 1572872 | tf_op jit(solution)/shard_map/ppermute | solution.py:147
  21.5 44.1 %collective-permute-start.3 = (f32[64,2048]{1,0:T(8,128)}, f32[64,2048]{1,0:T(8,128)}, u32[]{:S(2)}, u32[]{:S(2)}) collective-permute-start(f32[64,2048]{1,0:T(8,128)} %get-tuple-element.14.refs_5_), channel_id=1, source_target_pairs={{0,6},{1,7},{2,4},{3,5},{4,2},{5,3},{6,0},{7,1},{8,14},{9,15},{10,... | collective-permute-start | bytes 1572872 | tf_op jit(solution)/shard_map/ppermute | solution.py:147
  42.9 59.1 %collective-permute-start.9 = (f32[2048,128]{1,0:T(8,128)}, f32[2048,128]{1,0:T(8,128)}, u32[]{:S(2)}, u32[]{:S(2)}) collective-permute-start(f32[2048,128]{1,0:T(8,128)} %hold.17), channel_id=1, source_target_pairs={{0,8},{8,0},{16,24},{24,16},{1,9},{9,1},{17,25},{25,17},{2,10},{10... | collective-permute-start | bytes 3145736 | tf_op jit(solution)/shard_map/ppermute | solution.py:148
  43.4 58.5 %collective-permute-start.10 = (f32[2048,128]{1,0:T(8,128)}, f32[2048,128]{1,0:T(8,128)}, u32[]{:S(2)}, u32[]{:S(2)}) collective-permute-start(f32[2048,128]{1,0:T(8,128)} %hold.17), channel_id=1, source_target_pairs={{0,16},{8,24},{16,0},{24,8},{1,17},{9,25},{17,1},{25,9},{2,18},{10... | collective-permute-start | bytes 3145736 | tf_op jit(solution)/shard_map/ppermute | solution.py:148
  68.8 36.2 %collective-permute-start.7 = (f32[128,2048]{1,0:T(8,128)}, f32[128,2048]{1,0:T(8,128)}, u32[]{:S(2)}, u32[]{:S(2)}) collective-permute-start(f32[128,2048]{1,0:T(8,128)} %get-tuple-element.15.refs_1_), channel_id=1, source_target_pairs={{0,16},{8,24},{16,0},{24,8},{1,17},{9,25},{17,1},{25,9},{2,18},{10... | collective-permute-start | bytes 3145736 | tf_op jit(solution)/shard_map/ppermute | solution.py:148
  69.8 35.2 %collective-permute-start.6 = (f32[128,2048]{1,0:T(8,128)}, f32[128,2048]{1,0:T(8,128)}, u32[]{:S(2)}, u32[]{:S(2)}) collective-permute-start(f32[128,2048]{1,0:T(8,128)} %get-tuple-element.15.refs_1_), channel_id=1, source_target_pairs={{0,8},{8,0},{16,24},{24,16},{1,9},{9,1},{17,25},{25,17},{2,10},{10... | collective-permute-start | bytes 3145736 | tf_op jit(solution)/shard_map/ppermute | solution.py:148
  100.6 35.1 %collective-permute-start.13 = (f32[1024,256]{1,0:T(8,128)S(1)}, f32[1024,256]{1,0:T(8,128)}, u32[]{:S(2)}, u32[]{:S(2)}) collective-permute-start(f32[1024,256]{1,0:T(8,128)S(1)} %get-tuple-element.24.refs_5_.refs_2_), channel_id=1, source_target_pairs={{0,2},{1,3},{2,0},{3,1},{4,6},{5,7},{6,4},{7,5},{8,10},{9,11},{10,... | collective-permute-start | bytes 3145736 | tf_op jit(solution)/shard_map/ppermute | solution.py:147
  102.0 36.7 %collective-permute-start.16 = (f32[128,2048]{1,0:T(8,128)}, f32[128,2048]{1,0:T(8,128)}, u32[]{:S(2)}, u32[]{:S(2)}) collective-permute-start(f32[128,2048]{1,0:T(8,128)} %hold.22), channel_id=1, source_target_pairs={{0,8},{8,0},{16,24},{24,16},{1,9},{9,1},{17,25},{25,17},{2,10},{10... | collective-permute-start | bytes 3145736 | tf_op jit(solution)/shard_map/ppermute | solution.py:148
  103.5 36.7 %collective-permute-start.18 = (f32[128,2048]{1,0:T(8,128)}, f32[128,2048]{1,0:T(8,128)}, u32[]{:S(2)}, u32[]{:S(2)}) collective-permute-start(f32[128,2048]{1,0:T(8,128)} %hold.22), channel_id=1, source_target_pairs={{0,16},{8,24},{16,0},{24,8},{1,17},{9,25},{17,1},{25,9},{2,18},{10... | collective-permute-start | bytes 3145736 | tf_op jit(solution)/shard_map/ppermute | solution.py:148
  117.9 44.3 %collective-permute-start.12 = (f32[2048,128]{1,0:T(8,128)}, f32[2048,128]{1,0:T(8,128)}, u32[]{:S(2)}, u32[]{:S(2)}) collective-permute-start(f32[2048,128]{1,0:T(8,128)} %hold.19), channel_id=1, source_target_pairs={{0,8},{8,0},{16,24},{24,16},{1,9},{9,1},{17,25},{25,17},{2,10},{10... | collective-permute-start | bytes 3145736 | tf_op jit(solution)/shard_map/ppermute | solution.py:148
  134.8 57.0 %collective-permute-start.20 = (f32[1024,256]{1,0:T(8,128)}, f32[1024,256]{1,0:T(8,128)}, u32[]{:S(2)}, u32[]{:S(2)}) collective-permute-start(f32[1024,256]{1,0:T(8,128)} %get-tuple-element.20.refs_2_.refs_7_), channel_id=1, source_target_pairs={{0,2},{1,3},{2,0},{3,1},{4,6},{5,7},{6,4},{7,5},{8,10},{9,11},{10,... | collective-permute-start | bytes 3145736 | tf_op jit(solution)/shard_map/ppermute | solution.py:147
  138.2 59.2 %collective-permute-start.14 = (f32[2048,128]{1,0:T(8,128)}, f32[2048,128]{1,0:T(8,128)}, u32[]{:S(2)}, u32[]{:S(2)}) collective-permute-start(f32[2048,128]{1,0:T(8,128)} %hold.20.refs_1_), channel_id=1, source_target_pairs={{0,16},{8,24},{16,0},{24,8},{1,17},{9,25},{17,1},{25,9},{2,18},{10... | collective-permute-start | bytes 3145736 | tf_op jit(solution)/shard_map/ppermute | solution.py:148
  138.7 59.7 %collective-permute-start.17 = (f32[128,2048]{1,0:T(8,128)}, f32[128,2048]{1,0:T(8,128)}, u32[]{:S(2)}, u32[]{:S(2)}) collective-permute-start(f32[128,2048]{1,0:T(8,128)} %hold.23.refs_4_), channel_id=1, source_target_pairs={{0,16},{8,24},{16,0},{24,8},{1,17},{9,25},{17,1},{25,9},{2,18},{10... | collective-permute-start | bytes 3145736 | tf_op jit(solution)/shard_map/ppermute | solution.py:148
  162.2 23.4 %collective-permute-start.19 = (f32[2048,256]{1,0:T(8,128)}, f32[2048,256]{1,0:T(8,128)S(1)}, u32[]{:S(2)}, u32[]{:S(2)}) collective-permute-start(f32[2048,256]{1,0:T(8,128)} %both_terms.6.refs_6_), channel_id=1, source_target_pairs={{0,1},{1,0},{2,3},{3,2},{4,5},{5,4},{6,7},{7,6},{8,9},{9,8},{10,11... | collective-permute-start | bytes 6291464 | tf_op jit(solution)/shard_map/ppermute | solution.py:147
  162.2 36.1 %collective-permute-start.15 = (f32[128,2048]{1,0:T(8,128)}, f32[128,2048]{1,0:T(8,128)S(1)}, u32[]{:S(2)}, u32[]{:S(2)}) collective-permute-start(f32[128,2048]{1,0:T(8,128)} %hold.21), channel_id=1, source_target_pairs={{0,8},{8,0},{16,24},{24,16},{1,9},{9,1},{17,25},{25,17},{2,10},{10... | collective-permute-start | bytes 3145736 | tf_op jit(solution)/shard_map/ppermute | solution.py:148
  190.7 47.4 %collective-permute-start.22 = (f32[1024,256]{1,0:T(8,128)S(1)}, f32[1024,256]{1,0:T(8,128)}, u32[]{:S(2)}, u32[]{:S(2)}) collective-permute-start(f32[1024,256]{1,0:T(8,128)S(1)} %copy-done.7), channel_id=1, source_target_pairs={{0,2},{1,3},{2,0},{3,1},{4,6},{5,7},{6,4},{7,5},{8,10},{9,11},{10,... | collective-permute-start | bytes 3145736 | tf_op jit(solution)/shard_map/ppermute | solution.py:147
  192.8 47.9 %collective-permute-start.23 = (f32[512,256]{1,0:T(8,128)S(1)}, f32[512,256]{1,0:T(8,128)}, u32[]{:S(2)}, u32[]{:S(2)}) collective-permute-start(f32[512,256]{1,0:T(8,128)S(1)} %copy-done.5), channel_id=1, source_target_pairs={{0,4},{1,5},{2,6},{3,7},{4,0},{5,1},{6,2},{7,3},{8,12},{9,13},{10,... | collective-permute-start | bytes 1572872 | tf_op jit(solution)/shard_map/ppermute | solution.py:147
  197.4 46.7 %collective-permute-start.24 = (f32[512,256]{1,0:T(8,128)}, f32[512,256]{1,0:T(8,128)}, u32[]{:S(2)}, u32[]{:S(2)}) collective-permute-start(f32[512,256]{1,0:T(8,128)} %get-tuple-element.32.refs_8_), channel_id=1, source_target_pairs={{0,4},{1,5},{2,6},{3,7},{4,0},{5,1},{6,2},{7,3},{8,12},{9,13},{10,... | collective-permute-start | bytes 1572872 | tf_op jit(solution)/shard_map/ppermute | solution.py:147
  228.6 49.9 %collective-permute-start.26 = (f32[512,256]{1,0:T(8,128)S(1)}, f32[512,256]{1,0:T(8,128)}, u32[]{:S(2)}, u32[]{:S(2)}) collective-permute-start(f32[512,256]{1,0:T(8,128)S(1)} %get-tuple-element.28.refs_2_.refs_7_), channel_id=1, source_target_pairs={{0,2},{1,3},{2,0},{3,1},{4,6},{5,7},{6,4},{7,5},{8,10},{9,11},{10,... | collective-permute-start | bytes 1572872 | tf_op jit(solution)/shard_map/ppermute | solution.py:147
  240.7 41.6 %collective-permute-start.27 = (f32[512,256]{1,0:T(8,128)}, f32[512,256]{1,0:T(8,128)}, u32[]{:S(2)}, u32[]{:S(2)}) collective-permute-start(f32[512,256]{1,0:T(8,128)} %get-tuple-element.30.refs_3_.refs_8_), channel_id=1, source_target_pairs={{0,4},{1,5},{2,6},{3,7},{4,0},{5,1},{6,2},{7,3},{8,12},{9,13},{10,... | collective-permute-start | bytes 1572872 | tf_op jit(solution)/shard_map/ppermute | solution.py:147
  276.6 20.2 %collective-permute-start.28 = (f32[512,256]{1,0:T(8,128)S(1)}, f32[512,256]{1,0:T(8,128)}, u32[]{:S(2)}, u32[]{:S(2)}) collective-permute-start(f32[512,256]{1,0:T(8,128)S(1)} %get-tuple-element.26.refs_2_), channel_id=1, source_target_pairs={{0,2},{1,3},{2,0},{3,1},{4,6},{5,7},{6,4},{7,5},{8,10},{9,11},{10,... | collective-permute-start | bytes 1572872 | tf_op jit(solution)/shard_map/ppermute | solution.py:147
  (27 other events, 177.9 us)

commit v4 on v3

--- a/solution.py
+++ b/solution.py
@@ -188,10 +188,11 @@
         return moves
 
     crossing = place_copies([green_ret], [(chips * pieces, depth)], crossing_moves, "crossing")[0]
-    crossing = to_row(crossing, 1)
+    crossing_sent, crossing = crossing, to_row(crossing, 1)
     pairs = place_copies([green_ret, crossing], [(2 * pieces, depth)] * chips, pair_moves, "pairs")
     halves = {(0, part): green_less[:, part * near : (part + 1) * near] for part in range(2)}
     if col_bits:
+        halves[0, 0] = hold(halves[0, 0], [crossing_sent])
         bring(halves, blocks[1])
     lesser = {(0, part): (green_less, part) if near % 128 == 0 else (halves[0, part], 0) for part in range(2)}
 
@@ -257,10 +258,11 @@
                 panels[source] = hold(panels[source], after)
             bring(panels, [(distance, part)])
 
-    def advance(going, out):
+    def advance(going, out, places=None):
         last = [which for which, each in enumerate(going) if each is not None and not each[2]]
+        last = [which for which in last if places is None or which in places]
         for which, each in enumerate(going):
-            if each is not None and each[2]:
+            if each is not None and each[2] and (places is None or which in places):
                 going[which] = [each[0], *halve([hold(each[1][0], after), *each[1][1:]], each[2])]
         for which in last:
             (place, start), sums, _ = going[which]
@@ -293,6 +295,7 @@
             bring(mirrored, blocks[2])
             relay(halves, 0, after)
         if place == 2:
+            after.extend(halves[distance, 0] for distance in far)
             relay(mirrored, 0, after)
             relay(mirrored, 1, after)
             relay(halves, 1, after)
@@ -302,6 +305,9 @@
             came = to_row(sent, 1)
             if place == 2:
                 after.extend(halves[distance, 0] for distance in far)
+            if share == 1:
+                where, sums, bits = going[place - 1]
+                going[place - 1] = [where, *halve([hold(sums[0], after), *sums[1:]], bits)]
             kept = run_half(place, True, share, shares)
             now = halve([kept, came], row_bits[1:])
             if place == 1:
@@ -310,6 +316,8 @@
                 if place == 2:
                     send_later(going, later)
                     going[1:] = [[each[0], *halve([hold(each[1][0], after), *each[1][1:]], each[2])] for each in going[1:]]
+                elif shares == 2 and share == 0:
+                    out = advance(going, out, range(place - 1))
                 else:
                     out = advance(going, out)
             going.append([(place, share * (block // shares)), *now])

time: 317 us -> 339 us (1.069)
  waiting for transfers between devices: 30.2 us -> 56.8 us
  local copies, waits for them, and re-layouts: 19.1 us -> 15.2 us
    ppermute x19, waiting for transfers between devices: 30.2 us -> 44.9 us  [on_device(): lax.ppermute(values, 'row', [(i, i ^ distance) for i in range(n_row)])]
    ppermute x12, waiting for transfers between devices: 0.03 us -> 11.9 us  [on_device(): lax.ppermute(values, 'col', [(i, i ^ distance) for i in range(n_col)])]
    unnamed x42 -> x46, local copies, waits for them, and re-layouts: 10.2 us -> 7.59 us
  transfers between devices with their start and end apart: 31 -> 31, of which waited for: 3 -> 5; matrix products, arithmetic and copies ran while one was open for 13% -> 12% of each run, Pallas kernels for 63% -> 59%
where the time goes in v4:
time: 339 us; the launch traced here: 337 us
  Pallas kernels  201 us (59%)
  waiting for transfers between devices  56.8 us (17%)
  other arithmetic  35.3 us (10%)
  starting transfers between devices  29.1 us (9%)
  local copies, waits for them, and re-layouts  15.2 us (4%)
    pallas_call x12, Pallas kernels, sum_of_terms(): pl.pallas_call(functools.partial(term_kernel, kinds, streams, n_parts, le...  191 us
    ppermute x19, waiting for transfers between devices, on_device(): lax.ppermute(values, 'row', [(i, i ^ distance) for i in range(n_row)])  44.9 us
    slice x9, other arithmetic, halve(): array[middle:]  25.3 us
    ppermute x19, starting transfers between devices, on_device(): lax.ppermute(values, 'row', [(i, i ^ distance) for i in range(n_row)])  16.6 us
    ppermute x12, starting transfers between devices, on_device(): lax.ppermute(values, 'col', [(i, i ^ distance) for i in range(n_col)])  12.6 us
    ppermute x12, waiting for transfers between devices, on_device(): lax.ppermute(values, 'col', [(i, i ^ distance) for i in range(n_col)])  11.9 us
    pallas_call x3, Pallas kernels, place_copies(): pl.pallas_call(kernel, out_shape=[jax.ShapeDtypeStruct(shape, F32) for sh...  9.38 us
    unnamed x46, local copies, waits for them, and re-layouts  7.59 us
  transfers between devices with their start and end apart: 31, of which 5 were waited for; matrix products, arithmetic and copies ran while one was open for 12% of the time, Pallas kernels for 59%

profile of v4, /device:TPU:0, one launch (start us, length us, event | category | flops | bytes accessed | tf_op | source)
XLA Modules:
  0.0 337.3 jit_solution(16703832578273153152)
XLA Ops:
  11.9 3.4 pairs.1
  19.6 21.2 %first_term.2.refs_3_.refs_1_ = f32[4096,256]{1,0:T(8,128)} custom-call(s32[8]{0:T(128)} %copy-done.19, f32[4096,2048]{1,0:T(8,128)} %refs_0_.27, f32[2048,256]{1,0:T(8,128)} %refs_2_.1, f32[2048,256]{1,0:T(8,128)} %refs_2_.1, f32[64,2048]{1,0:T(8,128)} %get-tuple-element.12.refs_3_, f32[64,2048]{1,0:T(8,128)} %get-tuple-element.13.refs_4_, ...), custom_call_target="tpu_custom_call" | custom-call | flops 103079215104 | bytes 33554432 | tf_op jit(solution)/shard_map/first_term/pallas_call | solution.py:87
  42.4 21.1 %first_term.3.refs_4_.refs_3_ = f32[4096,256]{1,0:T(8,128)} custom-call(s32[8]{0:T(128)} %copy-done.19, f32[4096,2048]{1,0:T(8,128)} %refs_0_.27, f32[2048,128]{1,0:T(8,128)} %copy-done.21, f32[2048,128]{1,0:T(8,128)} %copy-done.14, f32[4096,256]{1,0:T(8,128)} %first_term.2.refs_3_.refs_1_), custom_call_target="tpu_custom_call" | custom-call | flops 103079215104 | bytes 33554432 | tf_op jit(solution)/shard_map/first_term/pallas_call | solution.py:87
  63.5 3.2 mirrored.1
  69.4 12.9 %second_term.4.refs_4_ = f32[2048,256]{1,0:T(8,128)} custom-call(s32[4]{0:T(128)} %get-tuple-element.49.tiles, f32[4096,2048]{1,0:T(8,128)} %refs_3_.11, f32[128,2048]{1,0:T(8,128)} %get-tuple-element.15.refs_1_, f32[128,2048]{1,0:T(8,128)} %get-tuple-element.16.refs_2_.refs_0_, f32[4096,256]{1,0:T(8,128)} %first_term.2.refs_3_.refs_1_, ...), custom_call_target="tpu_custom_call" | custom-call | flops 51539607552 | bytes 16777216 | tf_op jit(solution)/shard_map/second_term/pallas_call | solution.py:87
  82.2 12.9 %second_term.5.refs_4_.refs_1_ = f32[2048,256]{1,0:T(8,128)} custom-call(s32[4]{0:T(128)} %get-tuple-element.48.tiles, f32[4096,2048]{1,0:T(8,128)} %refs_3_.11, f32[128,2048]{1,0:T(8,128)} %get-tuple-element.15.refs_1_, f32[128,2048]{1,0:T(8,128)} %get-tuple-element.16.refs_2_.refs_0_, f32[4096,256]{1,0:T(8,128)} %first_term.2.refs_3_.refs_1_, ...), custom_call_target="tpu_custom_call" | custom-call | flops 51539607552 | bytes 16777216 | tf_op jit(solution)/shard_map/second_term/pallas_call | solution.py:87
  95.1 3.9 %fusion.8 = (f32[1024,256]{1,0:T(8,128)}, f32[1024,256]{1,0:T(8,128)}) fusion(f32[2048,256]{1,0:T(8,128)} %second_term.5.refs_4_.refs_1_, f32[2048,256]{1,0:T(8,128)S(1)} %collective-permute-done.8), kind=kLoop, calls=%fused_computation.47 | loop fusion | flops 262144 | bytes 5242880 | tf_op jit(solution)/shard_map/slice | solution.py:238
  103.4 12.9 %second_term.6.refs_4_ = f32[2048,256]{1,0:T(8,128)} custom-call(s32[4]{0:T(128)} %get-tuple-element.49.tiles, f32[4096,2048]{1,0:T(8,128)} %refs_3_.11, f32[128,2048]{1,0:T(8,128)} %collective-permute-done.6.refs_1_, f32[128,2048]{1,0:T(8,128)} %collective-permute-done.7.refs_2_.refs_0_, f32[4096,256]{1,0:T(8,128)} %first_term.3.refs_4_.refs_3_, ...), custom_call_target="tpu_custom_call" | custom-call | flops 51539607552 | bytes 16777216 | tf_op jit(solution)/shard_map/second_term/pallas_call | solution.py:87
  116.3 12.9 %second_term.7.refs_1_.refs_6_ = f32[2048,256]{1,0:T(8,128)} custom-call(s32[4]{0:T(128)} %get-tuple-element.48.tiles, f32[4096,2048]{1,0:T(8,128)} %refs_3_.11, f32[128,2048]{1,0:T(8,128)} %collective-permute-done.6.refs_1_, f32[128,2048]{1,0:T(8,128)} %collective-permute-done.7.refs_2_.refs_0_, f32[4096,256]{1,0:T(8,128)} %first_term.3.refs_4_.refs_3_, ...), custom_call_target="tpu_custom_call" | custom-call | flops 51539607552 | bytes 16777216 | tf_op jit(solution)/shard_map/second_term/pallas_call | solution.py:87
  129.2 3.4 fusion.6
  132.8 2.9 fusion.13
  135.7 11.9 %collective-permute-done.12.refs_4_.refs_9_.refs_7_.refs_1_ = f32[2048,128]{1,0:T(8,128)S(1)} collective-permute-done((f32[2048,128]{1,0:T(8,128)}, f32[2048,128]{1,0:T(8,128)S(1)}, u32[]{:S(2)}, u32[]{:S(2)}) %collective-permute-start.12) | collective-permute-done | bytes 1048608 | tf_op jit(solution)/shard_map/ppermute | solution.py:148
  151.5 22.0 %both_terms.6.refs_6_ = f32[2048,256]{1,0:T(8,128)} custom-call(s32[8]{0:T(128)} %slice.240.tiles, f32[4096,2048]{1,0:T(8,128)} %refs_0_.27, f32[2048,128]{1,0:T(8,128)} %hold.22.refs_1_, f32[2048,128]{1,0:T(8,128)} %collective-permute-done.10.refs_7_.refs_4_.refs_2_, f32[4096,2048]{1,0:T(8,128)} %refs_3_.11, f32[128,2048]{1,0:T(8,128)} %hold.25.refs_4_, ...), custom_call_target="tpu_custom_call" | custom-call | flops 103079215104 | bytes 33554432 | tf_op jit(solution)/shard_map/both_terms/pallas_call | solution.py:87
  173.5 21.8 %both_terms.7.refs_1_.refs_6_ = f32[2048,256]{1,0:T(8,128)} custom-call(s32[8]{0:T(128)} %slice.238.tiles, f32[4096,2048]{1,0:T(8,128)} %refs_0_.27, f32[2048,128]{1,0:T(8,128)} %hold.22.refs_1_, f32[2048,128]{1,0:T(8,128)} %collective-permute-done.10.refs_7_.refs_4_.refs_2_, f32[4096,2048]{1,0:T(8,128)} %refs_3_.11, f32[128,2048]{1,0:T(8,128)} %hold.25.refs_4_, ...), custom_call_target="tpu_custom_call" | custom-call | flops 103079215104 | bytes 33554432 | tf_op jit(solution)/shard_map/both_terms/pallas_call | solution.py:87
  195.3 3.8 %fusion.5 = (f32[1024,256]{1,0:T(8,128)}, f32[1024,256]{1,0:T(8,128)}) fusion(f32[2048,256]{1,0:T(8,128)} %both_terms.7.refs_1_.refs_6_, f32[2048,256]{1,0:T(8,128)S(1)} %collective-permute-done.19), kind=kLoop, calls=%fused_computation.44 | loop fusion | flops 262144 | bytes 5242880 | tf_op jit(solution)/shard_map/slice | solution.py:238
  207.1 13.3 %both_terms.8.refs_6_ = f32[1024,256]{1,0:T(8,128)} custom-call(s32[4]{0:T(128)} %get-tuple-element.46.tiles, f32[4096,2048]{1,0:T(8,128)} %refs_0_.27, f32[2048,128]{1,0:T(8,128)} %copy-done.7, f32[2048,128]{1,0:T(8,128)} %collective-permute-done.14.refs_2_, f32[4096,2048]{1,0:T(8,128)} %refs_3_.11, f32[128,2048]{1,0:T(8,128)} %collective-permute-done.15.refs_4_, ...), custom_call_target="tpu_custom_call" | custom-call | flops 51539607552 | bytes 16777216 | tf_op jit(solution)/shard_map/both_terms/pallas_call | solution.py:87
  220.4 13.3 %both_terms.9.refs_1_.refs_6_ = f32[1024,256]{1,0:T(8,128)} custom-call(s32[4]{0:T(128)} %get-tuple-element.47.tiles, f32[4096,2048]{1,0:T(8,128)} %refs_0_.27, f32[2048,128]{1,0:T(8,128)} %copy-done.7, f32[2048,128]{1,0:T(8,128)} %collective-permute-done.14.refs_2_, f32[4096,2048]{1,0:T(8,128)} %refs_3_.11, f32[128,2048]{1,0:T(8,128)} %collective-permute-done.15.refs_4_, ...), custom_call_target="tpu_custom_call" | custom-call | flops 51539607552 | bytes 16777216 | tf_op jit(solution)/shard_map/both_terms/pallas_call | solution.py:87
  237.1 16.2 %collective-permute-done.22 = f32[512,256]{1,0:T(8,128)} collective-permute-done((f32[512,256]{1,0:T(8,128)S(1)}, f32[512,256]{1,0:T(8,128)}, u32[]{:S(2)}, u32[]{:S(2)}) %collective-permute-start.22) | collective-permute-done | bytes 524320 | tf_op jit(solution)/shard_map/ppermute | solution.py:147
  259.5 13.6 %both_terms.10.refs_1_.refs_6_ = f32[1024,256]{1,0:T(8,128)} custom-call(s32[4]{0:T(128)} %get-tuple-element.42.tiles, f32[4096,2048]{1,0:T(8,128)} %refs_0_.27, f32[2048,128]{1,0:T(8,128)} %copy-done.7, f32[2048,128]{1,0:T(8,128)} %collective-permute-done.14.refs_2_, f32[4096,2048]{1,0:T(8,128)} %refs_3_.11, f32[128,2048]{1,0:T(8,128)} %collective-permute-done.15.refs_4_, ...), custom_call_target="tpu_custom_call" | custom-call | flops 51539607552 | bytes 16777216 | tf_op jit(solution)/shard_map/both_terms/pallas_call | solution.py:87
  275.7 13.3 %both_terms.11.refs_1_ = f32[1024,256]{1,0:T(8,128)} custom-call(s32[4]{0:T(128)} %get-tuple-element.41.tiles, f32[4096,2048]{1,0:T(8,128)} %refs_0_.27, f32[2048,128]{1,0:T(8,128)} %copy-done.7, f32[2048,128]{1,0:T(8,128)} %collective-permute-done.14.refs_2_, f32[4096,2048]{1,0:T(8,128)} %refs_3_.11, f32[128,2048]{1,0:T(8,128)} %collective-permute-done.15.refs_4_, ...), custom_call_target="tpu_custom_call" | custom-call | flops 51539607552 | bytes 16777216 | tf_op jit(solution)/shard_map/both_terms/pallas_call | solution.py:87
  291.6 3.0 collective-permute-start.28
  297.3 5.2 %collective-permute-done.27 = f32[512,256]{1,0:T(8,128)} collective-permute-done((f32[512,256]{1,0:T(8,128)}, f32[512,256]{1,0:T(8,128)}, u32[]{:S(2)}, u32[]{:S(2)}) %collective-permute-start.27) | collective-permute-done | bytes 524320 | tf_op jit(solution)/shard_map/ppermute | solution.py:147
  306.2 13.0 %collective-permute-done.28 = f32[512,256]{1,0:T(8,128)} collective-permute-done((f32[512,256]{1,0:T(8,128)S(1)}, f32[512,256]{1,0:T(8,128)}, u32[]{:S(2)}, u32[]{:S(2)}) %collective-permute-start.28) | collective-permute-done | bytes 524320 | tf_op jit(solution)/shard_map/ppermute | solution.py:147
  324.3 10.5 %collective-permute-done.30 = f32[256,256]{1,0:T(8,128)S(1)} collective-permute-done((f32[256,256]{1,0:T(8,128)S(1)}, f32[256,256]{1,0:T(8,128)S(1)}, u32[]{:S(2)}, u32[]{:S(2)}) %collective-permute-start.30) | collective-permute-done | bytes 262176 | tf_op jit(solution)/shard_map/ppermute | solution.py:147
  (152 shorter events, 65.6 us)
Async XLA Ops:
  4.7 36.1 %collective-permute-start.5 = (f32[2048,128]{1,0:T(8,128)}, f32[2048,128]{1,0:T(8,128)S(1)}, u32[]{:S(2)}, u32[]{:S(2)}) collective-permute-start(f32[2048,128]{1,0:T(8,128)} %hold.18), channel_id=1, source_target_pairs={{0,16},{8,24},{16,0},{24,8},{1,17},{9,25},{17,1},{25,9},{2,18},{10... | collective-permute-start | bytes 3145736 | tf_op jit(solution)/shard_map/ppermute | solution.py:148
  7.2 34.2 %collective-permute-start.4 = (f32[2048,128]{1,0:T(8,128)}, f32[2048,128]{1,0:T(8,128)S(1)}, u32[]{:S(2)}, u32[]{:S(2)}) collective-permute-start(f32[2048,128]{1,0:T(8,128)} %hold.18), channel_id=1, source_target_pairs={{0,8},{8,0},{16,24},{24,16},{1,9},{9,1},{17,25},{25,17},{2,10},{10... | collective-permute-start | bytes 3145736 | tf_op jit(solution)/shard_map/ppermute | solution.py:148
  15.3 48.3 %collective-permute-start.1 = (f32[64,2048]{1,0:T(8,128)}, f32[64,2048]{1,0:T(8,128)}, u32[]{:S(2)}, u32[]{:S(2)}) collective-permute-start(f32[64,2048]{1,0:T(8,128)} %get-tuple-element.12.refs_3_), channel_id=1, source_target_pairs={{0,2},{1,3},{2,0},{3,1},{4,6},{5,7},{6,4},{7,5},{8,10},{9,11},{10,... | collective-permute-start | bytes 1572872 | tf_op jit(solution)/shard_map/ppermute | solution.py:147
  16.8 46.7 %collective-permute-start.2 = (f32[64,2048]{1,0:T(8,128)}, f32[64,2048]{1,0:T(8,128)}, u32[]{:S(2)}, u32[]{:S(2)}) collective-permute-start(f32[64,2048]{1,0:T(8,128)} %get-tuple-element.13.refs_4_), channel_id=1, source_target_pairs={{0,4},{1,5},{2,6},{3,7},{4,0},{5,1},{6,2},{7,3},{8,12},{9,13},{10,... | collective-permute-start | bytes 1572872 | tf_op jit(solution)/shard_map/ppermute | solution.py:147
  19.4 44.1 %collective-permute-start.3 = (f32[64,2048]{1,0:T(8,128)}, f32[64,2048]{1,0:T(8,128)}, u32[]{:S(2)}, u32[]{:S(2)}) collective-permute-start(f32[64,2048]{1,0:T(8,128)} %get-tuple-element.14.refs_5_), channel_id=1, source_target_pairs={{0,6},{1,7},{2,4},{3,5},{4,2},{5,3},{6,0},{7,1},{8,14},{9,15},{10,... | collective-permute-start | bytes 1572872 | tf_op jit(solution)/shard_map/ppermute | solution.py:147
  40.8 58.1 %collective-permute-start.10 = (f32[2048,128]{1,0:T(8,128)}, f32[2048,128]{1,0:T(8,128)}, u32[]{:S(2)}, u32[]{:S(2)}) collective-permute-start(f32[2048,128]{1,0:T(8,128)} %hold.19), channel_id=1, source_target_pairs={{0,16},{8,24},{16,0},{24,8},{1,17},{9,25},{17,1},{25,9},{2,18},{10... | collective-permute-start | bytes 3145736 | tf_op jit(solution)/shard_map/ppermute | solution.py:148
  41.4 57.6 %collective-permute-start.9 = (f32[2048,128]{1,0:T(8,128)}, f32[2048,128]{1,0:T(8,128)}, u32[]{:S(2)}, u32[]{:S(2)}) collective-permute-start(f32[2048,128]{1,0:T(8,128)} %hold.19), channel_id=1, source_target_pairs={{0,8},{8,0},{16,24},{24,16},{1,9},{9,1},{17,25},{25,17},{2,10},{10... | collective-permute-start | bytes 3145736 | tf_op jit(solution)/shard_map/ppermute | solution.py:148
  66.8 36.1 %collective-permute-start.7 = (f32[128,2048]{1,0:T(8,128)}, f32[128,2048]{1,0:T(8,128)}, u32[]{:S(2)}, u32[]{:S(2)}) collective-permute-start(f32[128,2048]{1,0:T(8,128)} %get-tuple-element.15.refs_1_), channel_id=1, source_target_pairs={{0,16},{8,24},{16,0},{24,8},{1,17},{9,25},{17,1},{25,9},{2,18},{10... | collective-permute-start | bytes 3145736 | tf_op jit(solution)/shard_map/ppermute | solution.py:148
  68.3 35.1 %collective-permute-start.6 = (f32[128,2048]{1,0:T(8,128)}, f32[128,2048]{1,0:T(8,128)}, u32[]{:S(2)}, u32[]{:S(2)}) collective-permute-start(f32[128,2048]{1,0:T(8,128)} %get-tuple-element.15.refs_1_), channel_id=1, source_target_pairs={{0,8},{8,0},{16,24},{24,16},{1,9},{9,1},{17,25},{25,17},{2,10},{10... | collective-permute-start | bytes 3145736 | tf_op jit(solution)/shard_map/ppermute | solution.py:148
  99.0 52.5 %collective-permute-start.18 = (f32[128,2048]{1,0:T(8,128)}, f32[128,2048]{1,0:T(8,128)}, u32[]{:S(2)}, u32[]{:S(2)}) collective-permute-start(f32[128,2048]{1,0:T(8,128)} %hold.24), channel_id=1, source_target_pairs={{0,16},{8,24},{16,0},{24,8},{1,17},{9,25},{17,1},{25,9},{2,18},{10... | collective-permute-start | bytes 3145736 | tf_op jit(solution)/shard_map/ppermute | solution.py:148
  99.6 51.4 %collective-permute-start.16 = (f32[128,2048]{1,0:T(8,128)}, f32[128,2048]{1,0:T(8,128)}, u32[]{:S(2)}, u32[]{:S(2)}) collective-permute-start(f32[128,2048]{1,0:T(8,128)} %hold.24), channel_id=1, source_target_pairs={{0,8},{8,0},{16,24},{24,16},{1,9},{9,1},{17,25},{25,17},{2,10},{10... | collective-permute-start | bytes 3145736 | tf_op jit(solution)/shard_map/ppermute | solution.py:148
  100.5 32.3 %collective-permute-start.13 = (f32[1024,256]{1,0:T(8,128)S(1)}, f32[1024,256]{1,0:T(8,128)S(1)}, u32[]{:S(2)}, u32[]{:S(2)}) collective-permute-start(f32[1024,256]{1,0:T(8,128)S(1)} %copy-done.6), channel_id=1, source_target_pairs={{0,2},{1,3},{2,0},{3,1},{4,6},{5,7},{6,4},{7,5},{8,10},{9,11},{10,... | collective-permute-start | bytes 3145736 | tf_op jit(solution)/shard_map/ppermute | solution.py:147
  102.9 44.7 %collective-permute-start.12 = (f32[2048,128]{1,0:T(8,128)}, f32[2048,128]{1,0:T(8,128)S(1)}, u32[]{:S(2)}, u32[]{:S(2)}) collective-permute-start(f32[2048,128]{1,0:T(8,128)} %hold.21), channel_id=1, source_target_pairs={{0,8},{8,0},{16,24},{24,16},{1,9},{9,1},{17,25},{25,17},{2,10},{10... | collective-permute-start | bytes 3145736 | tf_op jit(solution)/shard_map/ppermute | solution.py:148
  132.6 68.9 %collective-permute-start.20 = (f32[1024,256]{1,0:T(8,128)}, f32[1024,256]{1,0:T(8,128)}, u32[]{:S(2)}, u32[]{:S(2)}) collective-permute-start(f32[1024,256]{1,0:T(8,128)} %get-tuple-element.20.refs_2_.refs_7_), channel_id=1, source_target_pairs={{0,2},{1,3},{2,0},{3,1},{4,6},{5,7},{6,4},{7,5},{8,10},{9,11},{10,... | collective-permute-start | bytes 3145736 | tf_op jit(solution)/shard_map/ppermute | solution.py:147
  148.5 57.5 %collective-permute-start.15 = (f32[128,2048]{1,0:T(8,128)}, f32[128,2048]{1,0:T(8,128)}, u32[]{:S(2)}, u32[]{:S(2)}) collective-permute-start(f32[128,2048]{1,0:T(8,128)} %hold.23), channel_id=1, source_target_pairs={{0,8},{8,0},{16,24},{24,16},{1,9},{9,1},{17,25},{25,17},{2,10},{10... | collective-permute-start | bytes 3145736 | tf_op jit(solution)/shard_map/ppermute | solution.py:148
  149.5 57.6 %collective-permute-start.14 = (f32[2048,128]{1,0:T(8,128)}, f32[2048,128]{1,0:T(8,128)}, u32[]{:S(2)}, u32[]{:S(2)}) collective-permute-start(f32[2048,128]{1,0:T(8,128)} %hold.22.refs_1_), channel_id=1, source_target_pairs={{0,16},{8,24},{16,0},{24,8},{1,17},{9,25},{17,1},{25,9},{2,18},{10... | collective-permute-start | bytes 3145736 | tf_op jit(solution)/shard_map/ppermute | solution.py:148
  151.0 56.1 %collective-permute-start.17 = (f32[128,2048]{1,0:T(8,128)}, f32[128,2048]{1,0:T(8,128)}, u32[]{:S(2)}, u32[]{:S(2)}) collective-permute-start(f32[128,2048]{1,0:T(8,128)} %hold.25.refs_4_), channel_id=1, source_target_pairs={{0,16},{8,24},{16,0},{24,8},{1,17},{9,25},{17,1},{25,9},{2,18},{10... | collective-permute-start | bytes 3145736 | tf_op jit(solution)/shard_map/ppermute | solution.py:148
  199.1 74.0 %collective-permute-start.24 = (f32[1024,256]{1,0:T(8,128)}, f32[1024,256]{1,0:T(8,128)}, u32[]{:S(2)}, u32[]{:S(2)}) collective-permute-start(f32[1024,256]{1,0:T(8,128)} %get-tuple-element.18.refs_2_.refs_7_), channel_id=1, source_target_pairs={{0,2},{1,3},{2,0},{3,1},{4,6},{5,7},{6,4},{7,5},{8,10},{9,11},{10,... | collective-permute-start | bytes 3145736 | tf_op jit(solution)/shard_map/ppermute | solution.py:147
  204.2 52.3 %collective-permute-start.23 = (f32[512,256]{1,0:T(8,128)}, f32[512,256]{1,0:T(8,128)}, u32[]{:S(2)}, u32[]{:S(2)}) collective-permute-start(f32[512,256]{1,0:T(8,128)} %get-tuple-element.32.refs_8_), channel_id=1, source_target_pairs={{0,4},{1,5},{2,6},{3,7},{4,0},{5,1},{6,2},{7,3},{8,12},{9,13},{10,... | collective-permute-start | bytes 1572872 | tf_op jit(solution)/shard_map/ppermute | solution.py:147
  206.0 47.3 %collective-permute-start.22 = (f32[512,256]{1,0:T(8,128)S(1)}, f32[512,256]{1,0:T(8,128)}, u32[]{:S(2)}, u32[]{:S(2)}) collective-permute-start(f32[512,256]{1,0:T(8,128)S(1)} %copy-done.5), channel_id=1, source_target_pairs={{0,4},{1,5},{2,6},{3,7},{4,0},{5,1},{6,2},{7,3},{8,12},{9,13},{10,... | collective-permute-start | bytes 1572872 | tf_op jit(solution)/shard_map/ppermute | solution.py:147
  236.3 58.3 %collective-permute-start.26 = (f32[512,256]{1,0:T(8,128)S(1)}, f32[512,256]{1,0:T(8,128)}, u32[]{:S(2)}, u32[]{:S(2)}) collective-permute-start(f32[512,256]{1,0:T(8,128)S(1)} %get-tuple-element.28.refs_2_.refs_7_), channel_id=1, source_target_pairs={{0,2},{1,3},{2,0},{3,1},{4,6},{5,7},{6,4},{7,5},{8,10},{9,11},{10,... | collective-permute-start | bytes 1572872 | tf_op jit(solution)/shard_map/ppermute | solution.py:147
  275.7 26.7 %collective-permute-start.27 = (f32[512,256]{1,0:T(8,128)}, f32[512,256]{1,0:T(8,128)}, u32[]{:S(2)}, u32[]{:S(2)}) collective-permute-start(f32[512,256]{1,0:T(8,128)} %get-tuple-element.30.refs_7_), channel_id=1, source_target_pairs={{0,4},{1,5},{2,6},{3,7},{4,0},{5,1},{6,2},{7,3},{8,12},{9,13},{10,... | collective-permute-start | bytes 1572872 | tf_op jit(solution)/shard_map/ppermute | solution.py:147
  291.6 27.6 %collective-permute-start.28 = (f32[512,256]{1,0:T(8,128)S(1)}, f32[512,256]{1,0:T(8,128)}, u32[]{:S(2)}, u32[]{:S(2)}) collective-permute-start(f32[512,256]{1,0:T(8,128)S(1)} %get-tuple-element.26.refs_2_), channel_id=1, source_target_pairs={{0,2},{1,3},{2,0},{3,1},{4,6},{5,7},{6,4},{7,5},{8,10},{9,11},{10,... | collective-permute-start | bytes 1572872 | tf_op jit(solution)/shard_map/ppermute | solution.py:147
  296.6 25.3 %collective-permute-start.29 = (f32[256,256]{1,0:T(8,128)S(1)}, f32[256,256]{1,0:T(8,128)S(1)}, u32[]{:S(2)}, u32[]{:S(2)}) collective-permute-start(f32[256,256]{1,0:T(8,128)S(1)} %get-tuple-element.38.refs_3_), channel_id=1, source_target_pairs={{0,4},{1,5},{2,6},{3,7},{4,0},{5,1},{6,2},{7,3},{8,12},{9,13},{10,... | collective-permute-start | bytes 786440 | tf_op jit(solution)/shard_map/ppermute | solution.py:147
  (29 other events, 195.4 us)

commit v5 on v3

--- a/solution.py
+++ b/solution.py
@@ -188,10 +188,11 @@
         return moves
 
     crossing = place_copies([green_ret], [(chips * pieces, depth)], crossing_moves, "crossing")[0]
-    crossing = to_row(crossing, 1)
+    crossing_sent, crossing = crossing, to_row(crossing, 1)
     pairs = place_copies([green_ret, crossing], [(2 * pieces, depth)] * chips, pair_moves, "pairs")
     halves = {(0, part): green_less[:, part * near : (part + 1) * near] for part in range(2)}
     if col_bits:
+        halves[0, 0] = hold(halves[0, 0], [crossing_sent])
         bring(halves, blocks[1])
     lesser = {(0, part): (green_less, part) if near % 128 == 0 else (halves[0, part], 0) for part in range(2)}
 
@@ -302,6 +303,8 @@
             came = to_row(sent, 1)
             if place == 2:
                 after.extend(halves[distance, 0] for distance in far)
+            if share == 1:
+                out = advance(going, out)
             kept = run_half(place, True, share, shares)
             now = halve([kept, came], row_bits[1:])
             if place == 1:
@@ -310,7 +313,7 @@
                 if place == 2:
                     send_later(going, later)
                     going[1:] = [[each[0], *halve([hold(each[1][0], after), *each[1][1:]], each[2])] for each in going[1:]]
-                else:
+                elif shares == 1 or share == 1:
                     out = advance(going, out)
             going.append([(place, share * (block // shares)), *now])
     while any(each is not None for each in going):

time: 317 us -> 311 us (0.981)
  transfers between devices with their start and end apart: 31 -> 31, of which waited for: 3 -> 4; matrix products, arithmetic and copies ran while one was open for 13% -> 13% of each run, Pallas kernels for 63% -> 64%
where the time goes in v5:
time: 311 us; the launch traced here: 310 us
  Pallas kernels  201 us (65%)
  other arithmetic  34.2 us (11%)
  starting transfers between devices  30 us (10%)
  waiting for transfers between devices  27.8 us (9%)
  local copies, waits for them, and re-layouts  16.9 us (5%)
    pallas_call x12, Pallas kernels, sum_of_terms(): pl.pallas_call(functools.partial(term_kernel, kinds, streams, n_parts, le...  191 us
    ppermute x19, waiting for transfers between devices, on_device(): lax.ppermute(values, 'row', [(i, i ^ distance) for i in range(n_row)])  27.7 us
    slice x9, other arithmetic, halve(): array[middle:]  24.5 us
    ppermute x19, starting transfers between devices, on_device(): lax.ppermute(values, 'row', [(i, i ^ distance) for i in range(n_row)])  15.6 us
    ppermute x12, starting transfers between devices, on_device(): lax.ppermute(values, 'col', [(i, i ^ distance) for i in range(n_col)])  14.4 us
    pallas_call x3, Pallas kernels, place_copies(): pl.pallas_call(kernel, out_shape=[jax.ShapeDtypeStruct(shape, F32) for sh...  9.41 us
    unnamed x42, local copies, waits for them, and re-layouts  7.92 us
    add x5, other arithmetic, advance(): final = functools.reduce(jnp.add, [hold(sums[0], after), *sums[1:]])  7.14 us
  transfers between devices with their start and end apart: 31, of which 4 were waited for; matrix products, arithmetic and copies ran while one was open for 13% of the time, Pallas kernels for 64%

profile of v5, /device:TPU:0, one launch (start us, length us, event | category | flops | bytes accessed | tf_op | source)
XLA Modules:
  0.0 309.8 jit_solution(1184457089425021850)
XLA Ops:
  0.0 2.8 crossing.1.refs_1_
  4.7 2.5 collective-permute-start.4
  12.8 3.3 %pairs.1 = (f32[64,2048]{1,0:T(8,128)}, f32[64,2048]{1,0:T(8,128)}, f32[64,2048]{1,0:T(8,128)}, f32[64,2048]{1,0:T(8,128)}) custom-call(f32[32,16384]{1,0:T(8,128)} %refs_0_.15, f32[128,2048]{1,0:T(8,128)} %copy-done.11), custom_call_target="tpu_custom_call" | custom-call | tf_op jit(solution)/shard_map/pairs/pallas_call | solution.py:115
  17.7 2.6 collective-permute-start.2
  20.5 21.2 %first_term.2.refs_3_.refs_1_ = f32[4096,256]{1,0:T(8,128)} custom-call(s32[8]{0:T(128)} %copy-done.17, f32[4096,2048]{1,0:T(8,128)} %refs_0_.27, f32[2048,256]{1,0:T(8,128)} %refs_2_.1, f32[2048,256]{1,0:T(8,128)} %refs_2_.1, f32[64,2048]{1,0:T(8,128)} %get-tuple-element.12.refs_3_, f32[64,2048]{1,0:T(8,128)} %get-tuple-element.13.refs_4_, ...), custom_call_target="tpu_custom_call" | custom-call | flops 103079215104 | bytes 33554432 | tf_op jit(solution)/shard_map/first_term/pallas_call | solution.py:87
  43.2 21.2 %first_term.3.refs_4_.refs_3_ = f32[4096,256]{1,0:T(8,128)} custom-call(s32[8]{0:T(128)} %copy-done.17, f32[4096,2048]{1,0:T(8,128)} %refs_0_.27, f32[2048,128]{1,0:T(8,128)} %collective-permute-done.4.refs_1_, f32[2048,128]{1,0:T(8,128)} %copy-done.10, f32[4096,256]{1,0:T(8,128)} %first_term.2.refs_3_.refs_1_), custom_call_target="tpu_custom_call" | custom-call | flops 103079215104 | bytes 33554432 | tf_op jit(solution)/shard_map/first_term/pallas_call | solution.py:87
  64.4 3.3 %mirrored.1 = (f32[128,2048]{1,0:T(8,128)}, f32[128,2048]{1,0:T(8,128)}) custom-call(f32[64,2048]{1,0:T(8,128)} %get-tuple-element.11.refs_0_, f32[64,2048]{1,0:T(8,128)} %collective-permute-done.1.refs_1_, f32[64,2048]{1,0:T(8,128)} %collective-permute-done.2.refs_2_, f32[64,2048]{1,0:T(8,128)} %collective-permute-done.3.refs_3_, ...), custom_call_target="tpu_custom_call" | custom-call | tf_op jit(solution)/shard_map/mirrored/pallas_call | solution.py:115
  70.3 12.9 %second_term.4.refs_4_ = f32[2048,256]{1,0:T(8,128)} custom-call(s32[4]{0:T(128)} %get-tuple-element.49.tiles, f32[4096,2048]{1,0:T(8,128)} %refs_3_.11, f32[128,2048]{1,0:T(8,128)} %get-tuple-element.15.refs_1_, f32[128,2048]{1,0:T(8,128)} %get-tuple-element.16.refs_2_.refs_0_, f32[4096,256]{1,0:T(8,128)} %first_term.2.refs_3_.refs_1_, ...), custom_call_target="tpu_custom_call" | custom-call | flops 51539607552 | bytes 16777216 | tf_op jit(solution)/shard_map/second_term/pallas_call | solution.py:87
  83.2 12.9 %second_term.5.refs_4_.refs_1_ = f32[2048,256]{1,0:T(8,128)} custom-call(s32[4]{0:T(128)} %get-tuple-element.48.tiles, f32[4096,2048]{1,0:T(8,128)} %refs_3_.11, f32[128,2048]{1,0:T(8,128)} %get-tuple-element.15.refs_1_, f32[128,2048]{1,0:T(8,128)} %get-tuple-element.16.refs_2_.refs_0_, f32[4096,256]{1,0:T(8,128)} %first_term.2.refs_3_.refs_1_, ...), custom_call_target="tpu_custom_call" | custom-call | flops 51539607552 | bytes 16777216 | tf_op jit(solution)/shard_map/second_term/pallas_call | solution.py:87
  96.1 3.5 %fusion.8 = (f32[1024,256]{1,0:T(8,128)}, f32[1024,256]{1,0:T(8,128)S(1)}) fusion(f32[2048,256]{1,0:T(8,128)} %second_term.5.refs_4_.refs_1_, f32[2048,256]{1,0:T(8,128)S(1)} %collective-permute-done.8), kind=kLoop, calls=%fused_computation.47 | loop fusion | flops 262144 | bytes 5242880 | tf_op jit(solution)/shard_map/slice | solution.py:238
  103.4 12.9 %second_term.6.refs_4_ = f32[2048,256]{1,0:T(8,128)} custom-call(s32[4]{0:T(128)} %get-tuple-element.49.tiles, f32[4096,2048]{1,0:T(8,128)} %refs_3_.11, f32[128,2048]{1,0:T(8,128)} %collective-permute-done.6.refs_1_, f32[128,2048]{1,0:T(8,128)} %collective-permute-done.7.refs_2_.refs_0_, f32[4096,256]{1,0:T(8,128)} %first_term.3.refs_4_.refs_3_, ...), custom_call_target="tpu_custom_call" | custom-call | flops 51539607552 | bytes 16777216 | tf_op jit(solution)/shard_map/second_term/pallas_call | solution.py:87
  116.9 12.9 %second_term.7.refs_1_.refs_6_ = f32[2048,256]{1,0:T(8,128)} custom-call(s32[4]{0:T(128)} %get-tuple-element.48.tiles, f32[4096,2048]{1,0:T(8,128)} %refs_3_.11, f32[128,2048]{1,0:T(8,128)} %collective-permute-done.6.refs_1_, f32[128,2048]{1,0:T(8,128)} %collective-permute-done.7.refs_2_.refs_0_, f32[4096,256]{1,0:T(8,128)} %first_term.3.refs_4_.refs_3_, ...), custom_call_target="tpu_custom_call" | custom-call | flops 51539607552 | bytes 16777216 | tf_op jit(solution)/shard_map/second_term/pallas_call | solution.py:87
  129.8 3.4 %fusion.6 = (f32[1024,256]{1,0:T(8,128)}, f32[1024,256]{1,0:T(8,128)}) fusion(f32[2048,256]{1,0:T(8,128)} %second_term.7.refs_1_.refs_6_, f32[2048,256]{1,0:T(8,128)} %collective-permute-done.11), kind=kLoop, calls=%fused_computation.45 | loop fusion | flops 262144 | bytes 5242880 | tf_op jit(solution)/shard_map/slice | solution.py:238
  138.6 22.0 %both_terms.6.refs_6_ = f32[2048,256]{1,0:T(8,128)} custom-call(s32[8]{0:T(128)} %slice.241.tiles, f32[4096,2048]{1,0:T(8,128)} %refs_0_.27, f32[2048,128]{1,0:T(8,128)} %hold.22.refs_1_, f32[2048,128]{1,0:T(8,128)} %collective-permute-done.10.refs_7_.refs_4_.refs_2_, f32[4096,2048]{1,0:T(8,128)} %refs_3_.11, f32[128,2048]{1,0:T(8,128)} %hold.25.refs_4_, ...), custom_call_target="tpu_custom_call" | custom-call | flops 103079215104 | bytes 33554432 | tf_op jit(solution)/shard_map/both_terms/pallas_call | solution.py:87
  162.2 21.8 %both_terms.7.refs_1_.refs_6_ = f32[2048,256]{1,0:T(8,128)} custom-call(s32[8]{0:T(128)} %slice.239.tiles, f32[4096,2048]{1,0:T(8,128)} %refs_0_.27, f32[2048,128]{1,0:T(8,128)} %hold.22.refs_1_, f32[2048,128]{1,0:T(8,128)} %collective-permute-done.10.refs_7_.refs_4_.refs_2_, f32[4096,2048]{1,0:T(8,128)} %refs_3_.11, f32[128,2048]{1,0:T(8,128)} %hold.25.refs_4_, ...), custom_call_target="tpu_custom_call" | custom-call | flops 103079215104 | bytes 33554432 | tf_op jit(solution)/shard_map/both_terms/pallas_call | solution.py:87
  184.0 3.8 %fusion.5 = (f32[1024,256]{1,0:T(8,128)}, f32[1024,256]{1,0:T(8,128)}) fusion(f32[2048,256]{1,0:T(8,128)} %both_terms.7.refs_1_.refs_6_, f32[2048,256]{1,0:T(8,128)S(1)} %collective-permute-done.19), kind=kLoop, calls=%fused_computation.44 | loop fusion | flops 262144 | bytes 5242880 | tf_op jit(solution)/shard_map/slice | solution.py:238
  190.9 2.6 fusion.11
  195.5 13.3 %both_terms.8.refs_6_ = f32[1024,256]{1,0:T(8,128)} custom-call(s32[4]{0:T(128)} %get-tuple-element.43.tiles, f32[4096,2048]{1,0:T(8,128)} %refs_0_.27, f32[2048,128]{1,0:T(8,128)} %collective-permute-done.12.refs_7_.refs_1_, f32[2048,128]{1,0:T(8,128)} %collective-permute-done.14.refs_2_, f32[4096,2048]{1,0:T(8,128)} %refs_3_.11, f32[128,2048]{1,0:T(8,128)} %copy-done.19, ...), custom_call_target="tpu_custom_call" | custom-call | flops 51539607552 | bytes 16777216 | tf_op jit(solution)/shard_map/both_terms/pallas_call | solution.py:87
  208.9 13.3 %both_terms.9.refs_6_ = f32[1024,256]{1,0:T(8,128)} custom-call(s32[4]{0:T(128)} %get-tuple-element.44.tiles, f32[4096,2048]{1,0:T(8,128)} %refs_0_.27, f32[2048,128]{1,0:T(8,128)} %collective-permute-done.12.refs_7_.refs_1_, f32[2048,128]{1,0:T(8,128)} %collective-permute-done.14.refs_2_, f32[4096,2048]{1,0:T(8,128)} %refs_3_.11, f32[128,2048]{1,0:T(8,128)} %copy-done.19, ...), custom_call_target="tpu_custom_call" | custom-call | flops 51539607552 | bytes 16777216 | tf_op jit(solution)/shard_map/both_terms/pallas_call | solution.py:87
  225.6 13.6 %both_terms.10.refs_1_.refs_6_ = f32[1024,256]{1,0:T(8,128)} custom-call(s32[4]{0:T(128)} %get-tuple-element.42.tiles, f32[4096,2048]{1,0:T(8,128)} %refs_0_.27, f32[2048,128]{1,0:T(8,128)} %collective-permute-done.12.refs_7_.refs_1_, f32[2048,128]{1,0:T(8,128)} %collective-permute-done.14.refs_2_, f32[4096,2048]{1,0:T(8,128)} %refs_3_.11, ...), custom_call_target="tpu_custom_call" | custom-call | flops 51539607552 | bytes 16777216 | tf_op jit(solution)/shard_map/both_terms/pallas_call | solution.py:87
  244.1 5.9 %collective-permute-done.23 = f32[512,256]{1,0:T(8,128)S(1)} collective-permute-done((f32[512,256]{1,0:T(8,128)S(1)}, f32[512,256]{1,0:T(8,128)S(1)}, u32[]{:S(2)}, u32[]{:S(2)}) %collective-permute-start.23) | collective-permute-done | bytes 524320 | tf_op jit(solution)/shard_map/ppermute | solution.py:147
  259.1 13.4 %both_terms.11.refs_1_ = f32[1024,256]{1,0:T(8,128)} custom-call(s32[4]{0:T(128)} %get-tuple-element.41.tiles, f32[4096,2048]{1,0:T(8,128)} %refs_0_.27, f32[2048,128]{1,0:T(8,128)} %collective-permute-done.12.refs_7_.refs_1_, f32[2048,128]{1,0:T(8,128)} %collective-permute-done.14.refs_2_, f32[4096,2048]{1,0:T(8,128)} %refs_3_.11, f32[128,2048]{1,0:T(8,128)} %copy-done.19, ...), custom_call_target="tpu_custom_call" | custom-call | flops 51539607552 | bytes 16777216 | tf_op jit(solution)/shard_map/both_terms/pallas_call | solution.py:87
  283.7 7.1 %collective-permute-done.29 = f32[512,256]{1,0:T(8,128)} collective-permute-done((f32[512,256]{1,0:T(8,128)S(1)}, f32[512,256]{1,0:T(8,128)}, u32[]{:S(2)}, u32[]{:S(2)}) %collective-permute-start.29) | collective-permute-done | bytes 524320 | tf_op jit(solution)/shard_map/ppermute | solution.py:147
  293.4 13.9 %collective-permute-done.30 = f32[256,256]{1,0:T(8,128)S(1)} collective-permute-done((f32[256,256]{1,0:T(8,128)S(1)}, f32[256,256]{1,0:T(8,128)S(1)}, u32[]{:S(2)}, u32[]{:S(2)}) %collective-permute-start.30) | collective-permute-done | bytes 262176 | tf_op jit(solution)/shard_map/ppermute | solution.py:147
  (148 shorter events, 63.5 us)
Async XLA Ops:
  4.7 37.1 %collective-permute-start.4 = (f32[2048,128]{1,0:T(8,128)}, f32[2048,128]{1,0:T(8,128)}, u32[]{:S(2)}, u32[]{:S(2)}) collective-permute-start(f32[2048,128]{1,0:T(8,128)} %hold.18), channel_id=1, source_target_pairs={{0,8},{8,0},{16,24},{24,16},{1,9},{9,1},{17,25},{25,17},{2,10},{10... | collective-permute-start | bytes 3145736 | tf_op jit(solution)/shard_map/ppermute | solution.py:148
  7.2 35.1 %collective-permute-start.5 = (f32[2048,128]{1,0:T(8,128)}, f32[2048,128]{1,0:T(8,128)S(1)}, u32[]{:S(2)}, u32[]{:S(2)}) collective-permute-start(f32[2048,128]{1,0:T(8,128)} %hold.18), channel_id=1, source_target_pairs={{0,16},{8,24},{16,0},{24,8},{1,17},{9,25},{17,1},{25,9},{2,18},{10... | collective-permute-start | bytes 3145736 | tf_op jit(solution)/shard_map/ppermute | solution.py:148
  16.1 48.3 %collective-permute-start.1 = (f32[64,2048]{1,0:T(8,128)}, f32[64,2048]{1,0:T(8,128)}, u32[]{:S(2)}, u32[]{:S(2)}) collective-permute-start(f32[64,2048]{1,0:T(8,128)} %get-tuple-element.12.refs_3_), channel_id=1, source_target_pairs={{0,2},{1,3},{2,0},{3,1},{4,6},{5,7},{6,4},{7,5},{8,10},{9,11},{10,... | collective-permute-start | bytes 1572872 | tf_op jit(solution)/shard_map/ppermute | solution.py:147
  17.7 46.7 %collective-permute-start.2 = (f32[64,2048]{1,0:T(8,128)}, f32[64,2048]{1,0:T(8,128)}, u32[]{:S(2)}, u32[]{:S(2)}) collective-permute-start(f32[64,2048]{1,0:T(8,128)} %get-tuple-element.13.refs_4_), channel_id=1, source_target_pairs={{0,4},{1,5},{2,6},{3,7},{4,0},{5,1},{6,2},{7,3},{8,12},{9,13},{10,... | collective-permute-start | bytes 1572872 | tf_op jit(solution)/shard_map/ppermute | solution.py:147
  20.3 44.1 %collective-permute-start.3 = (f32[64,2048]{1,0:T(8,128)}, f32[64,2048]{1,0:T(8,128)}, u32[]{:S(2)}, u32[]{:S(2)}) collective-permute-start(f32[64,2048]{1,0:T(8,128)} %get-tuple-element.14.refs_5_), channel_id=1, source_target_pairs={{0,6},{1,7},{2,4},{3,5},{4,2},{5,3},{6,0},{7,1},{8,14},{9,15},{10,... | collective-permute-start | bytes 1572872 | tf_op jit(solution)/shard_map/ppermute | solution.py:147
  41.7 58.8 %collective-permute-start.9 = (f32[2048,128]{1,0:T(8,128)}, f32[2048,128]{1,0:T(8,128)}, u32[]{:S(2)}, u32[]{:S(2)}) collective-permute-start(f32[2048,128]{1,0:T(8,128)} %hold.19), channel_id=1, source_target_pairs={{0,8},{8,0},{16,24},{24,16},{1,9},{9,1},{17,25},{25,17},{2,10},{10... | collective-permute-start | bytes 3145736 | tf_op jit(solution)/shard_map/ppermute | solution.py:148
  42.3 58.2 %collective-permute-start.10 = (f32[2048,128]{1,0:T(8,128)}, f32[2048,128]{1,0:T(8,128)}, u32[]{:S(2)}, u32[]{:S(2)}) collective-permute-start(f32[2048,128]{1,0:T(8,128)} %hold.19), channel_id=1, source_target_pairs={{0,16},{8,24},{16,0},{24,8},{1,17},{9,25},{17,1},{25,9},{2,18},{10... | collective-permute-start | bytes 3145736 | tf_op jit(solution)/shard_map/ppermute | solution.py:148
  67.7 35.7 %collective-permute-start.7 = (f32[128,2048]{1,0:T(8,128)}, f32[128,2048]{1,0:T(8,128)}, u32[]{:S(2)}, u32[]{:S(2)}) collective-permute-start(f32[128,2048]{1,0:T(8,128)} %get-tuple-element.15.refs_1_), channel_id=1, source_target_pairs={{0,16},{8,24},{16,0},{24,8},{1,17},{9,25},{17,1},{25,9},{2,18},{10... | collective-permute-start | bytes 3145736 | tf_op jit(solution)/shard_map/ppermute | solution.py:148
  68.8 34.7 %collective-permute-start.6 = (f32[128,2048]{1,0:T(8,128)}, f32[128,2048]{1,0:T(8,128)}, u32[]{:S(2)}, u32[]{:S(2)}) collective-permute-start(f32[128,2048]{1,0:T(8,128)} %get-tuple-element.15.refs_1_), channel_id=1, source_target_pairs={{0,8},{8,0},{16,24},{24,16},{1,9},{9,1},{17,25},{25,17},{2,10},{10... | collective-permute-start | bytes 3145736 | tf_op jit(solution)/shard_map/ppermute | solution.py:148
  99.6 34.6 %collective-permute-start.13 = (f32[1024,256]{1,0:T(8,128)S(1)}, f32[1024,256]{1,0:T(8,128)}, u32[]{:S(2)}, u32[]{:S(2)}) collective-permute-start(f32[1024,256]{1,0:T(8,128)S(1)} %get-tuple-element.24.refs_5_.refs_2_), channel_id=1, source_target_pairs={{0,2},{1,3},{2,0},{3,1},{4,6},{5,7},{6,4},{7,5},{8,10},{9,11},{10,... | collective-permute-start | bytes 3145736 | tf_op jit(solution)/shard_map/ppermute | solution.py:147
  100.6 36.9 %collective-permute-start.16 = (f32[128,2048]{1,0:T(8,128)}, f32[128,2048]{1,0:T(8,128)}, u32[]{:S(2)}, u32[]{:S(2)}) collective-permute-start(f32[128,2048]{1,0:T(8,128)} %hold.24), channel_id=1, source_target_pairs={{0,8},{8,0},{16,24},{24,16},{1,9},{9,1},{17,25},{25,17},{2,10},{10... | collective-permute-start | bytes 3145736 | tf_op jit(solution)/shard_map/ppermute | solution.py:148
  101.9 36.7 %collective-permute-start.18 = (f32[128,2048]{1,0:T(8,128)}, f32[128,2048]{1,0:T(8,128)}, u32[]{:S(2)}, u32[]{:S(2)}) collective-permute-start(f32[128,2048]{1,0:T(8,128)} %hold.24), channel_id=1, source_target_pairs={{0,16},{8,24},{16,0},{24,8},{1,17},{9,25},{17,1},{25,9},{2,18},{10... | collective-permute-start | bytes 3145736 | tf_op jit(solution)/shard_map/ppermute | solution.py:148
  116.3 44.3 %collective-permute-start.12 = (f32[2048,128]{1,0:T(8,128)}, f32[2048,128]{1,0:T(8,128)}, u32[]{:S(2)}, u32[]{:S(2)}) collective-permute-start(f32[2048,128]{1,0:T(8,128)} %hold.21), channel_id=1, source_target_pairs={{0,8},{8,0},{16,24},{24,16},{1,9},{9,1},{17,25},{25,17},{2,10},{10... | collective-permute-start | bytes 3145736 | tf_op jit(solution)/shard_map/ppermute | solution.py:148
  133.2 55.7 %collective-permute-start.20 = (f32[1024,256]{1,0:T(8,128)}, f32[1024,256]{1,0:T(8,128)}, u32[]{:S(2)}, u32[]{:S(2)}) collective-permute-start(f32[1024,256]{1,0:T(8,128)} %get-tuple-element.20.refs_2_.refs_7_), channel_id=1, source_target_pairs={{0,2},{1,3},{2,0},{3,1},{4,6},{5,7},{6,4},{7,5},{8,10},{9,11},{10,... | collective-permute-start | bytes 3145736 | tf_op jit(solution)/shard_map/ppermute | solution.py:147
  136.6 56.9 %collective-permute-start.14 = (f32[2048,128]{1,0:T(8,128)}, f32[2048,128]{1,0:T(8,128)}, u32[]{:S(2)}, u32[]{:S(2)}) collective-permute-start(f32[2048,128]{1,0:T(8,128)} %hold.22.refs_1_), channel_id=1, source_target_pairs={{0,16},{8,24},{16,0},{24,8},{1,17},{9,25},{17,1},{25,9},{2,18},{10... | collective-permute-start | bytes 3145736 | tf_op jit(solution)/shard_map/ppermute | solution.py:148
  137.4 57.1 %collective-permute-start.17 = (f32[128,2048]{1,0:T(8,128)}, f32[128,2048]{1,0:T(8,128)}, u32[]{:S(2)}, u32[]{:S(2)}) collective-permute-start(f32[128,2048]{1,0:T(8,128)} %hold.25.refs_4_), channel_id=1, source_target_pairs={{0,16},{8,24},{16,0},{24,8},{1,17},{9,25},{17,1},{25,9},{2,18},{10... | collective-permute-start | bytes 3145736 | tf_op jit(solution)/shard_map/ppermute | solution.py:148
  160.6 33.9 %collective-permute-start.15 = (f32[128,2048]{1,0:T(8,128)}, f32[128,2048]{1,0:T(8,128)S(1)}, u32[]{:S(2)}, u32[]{:S(2)}) collective-permute-start(f32[128,2048]{1,0:T(8,128)} %hold.23), channel_id=1, source_target_pairs={{0,8},{8,0},{16,24},{24,16},{1,9},{9,1},{17,25},{25,17},{2,10},{10... | collective-permute-start | bytes 3145736 | tf_op jit(solution)/shard_map/ppermute | solution.py:148
  187.8 51.8 %collective-permute-start.22 = (f32[1024,256]{1,0:T(8,128)}, f32[1024,256]{1,0:T(8,128)}, u32[]{:S(2)}, u32[]{:S(2)}) collective-permute-start(f32[1024,256]{1,0:T(8,128)} %get-tuple-element.18.refs_2_.refs_7_), channel_id=1, source_target_pairs={{0,2},{1,3},{2,0},{3,1},{4,6},{5,7},{6,4},{7,5},{8,10},{9,11},{10,... | collective-permute-start | bytes 3145736 | tf_op jit(solution)/shard_map/ppermute | solution.py:147
  188.9 63.7 %collective-permute-start.24 = (f32[512,256]{1,0:T(8,128)}, f32[512,256]{1,0:T(8,128)}, u32[]{:S(2)}, u32[]{:S(2)}) collective-permute-start(f32[512,256]{1,0:T(8,128)} %hold.30), channel_id=1, source_target_pairs={{0,4},{1,5},{2,6},{3,7},{4,0},{5,1},{6,2},{7,3},{8,12},{9,13},{10,... | collective-permute-start | bytes 1572872 | tf_op jit(solution)/shard_map/ppermute | solution.py:147
  193.5 62.5 %collective-permute-start.25 = (f32[512,256]{1,0:T(8,128)}, f32[512,256]{1,0:T(8,128)}, u32[]{:S(2)}, u32[]{:S(2)}) collective-permute-start(f32[512,256]{1,0:T(8,128)} %get-tuple-element.30.refs_8_), channel_id=1, source_target_pairs={{0,4},{1,5},{2,6},{3,7},{4,0},{5,1},{6,2},{7,3},{8,12},{9,13},{10,... | collective-permute-start | bytes 1572872 | tf_op jit(solution)/shard_map/ppermute | solution.py:147
  224.7 25.3 %collective-permute-start.23 = (f32[512,256]{1,0:T(8,128)S(1)}, f32[512,256]{1,0:T(8,128)S(1)}, u32[]{:S(2)}, u32[]{:S(2)}) collective-permute-start(f32[512,256]{1,0:T(8,128)S(1)} %get-tuple-element.32.refs_7_), channel_id=1, source_target_pairs={{0,2},{1,3},{2,0},{3,1},{4,6},{5,7},{6,4},{7,5},{8,10},{9,11},{10,... | collective-permute-start | bytes 1572872 | tf_op jit(solution)/shard_map/ppermute | solution.py:147
  239.3 33.2 %collective-permute-start.26 = (f32[1024,256]{1,0:T(8,128)}, f32[1024,256]{1,0:T(8,128)}, u32[]{:S(2)}, u32[]{:S(2)}) collective-permute-start(f32[1024,256]{1,0:T(8,128)} %both_terms.10.refs_1_.refs_6_), channel_id=1, source_target_pairs={{0,1},{1,0},{2,3},{3,2},{4,5},{5,4},{6,7},{7,6},{8,9},{9,8},{10,11... | collective-permute-start | bytes 3145736 | tf_op jit(solution)/shard_map/ppermute | solution.py:147
  242.1 33.7 %collective-permute-start.27 = (f32[512,256]{1,0:T(8,128)S(1)}, f32[512,256]{1,0:T(8,128)S(1)}, u32[]{:S(2)}, u32[]{:S(2)}) collective-permute-start(f32[512,256]{1,0:T(8,128)S(1)} %get-tuple-element.28.refs_2_.refs_7_), channel_id=1, source_target_pairs={{0,4},{1,5},{2,6},{3,7},{4,0},{5,1},{6,2},{7,3},{8,12},{9,13},{10,... | collective-permute-start | bytes 1572872 | tf_op jit(solution)/shard_map/ppermute | solution.py:147
  252.0 27.7 %collective-permute-start.28 = (f32[256,256]{1,0:T(8,128)S(1)}, f32[256,256]{1,0:T(8,128)}, u32[]{:S(2)}, u32[]{:S(2)}) collective-permute-start(f32[256,256]{1,0:T(8,128)S(1)} %get-tuple-element.38.refs_3_.refs_8_), channel_id=1, source_target_pairs={{0,4},{1,5},{2,6},{3,7},{4,0},{5,1},{6,2},{7,3},{8,12},{9,13},{10,... | collective-permute-start | bytes 786440 | tf_op jit(solution)/shard_map/ppermute | solution.py:147
  (27 other events, 209.6 us)

commit v6 on v5

--- a/solution.py
+++ b/solution.py
@@ -258,10 +258,11 @@
                 panels[source] = hold(panels[source], after)
             bring(panels, [(distance, part)])
 
-    def advance(going, out):
+    def advance(going, out, places=None):
         last = [which for which, each in enumerate(going) if each is not None and not each[2]]
+        last = [which for which in last if places is None or which in places]
         for which, each in enumerate(going):
-            if each is not None and each[2]:
+            if each is not None and each[2] and (places is None or which in places):
                 going[which] = [each[0], *halve([hold(each[1][0], after), *each[1][1:]], each[2])]
         for which in last:
             (place, start), sums, _ = going[which]
@@ -304,7 +305,7 @@
             if place == 2:
                 after.extend(halves[distance, 0] for distance in far)
             if share == 1:
-                out = advance(going, out)
+                out = advance(going, out, range(place))
             kept = run_half(place, True, share, shares)
             now = halve([kept, came], row_bits[1:])
             if place == 1:

time: 311 us -> 305 us (0.981)
  waiting for transfers between devices: 27.8 us -> 22.1 us
    ppermute x19, waiting for transfers between devices: 27.7 us -> 22 us  [on_device(): lax.ppermute(values, 'row', [(i, i ^ distance) for i in range(n_row)])]
    unnamed x42 -> x40, local copies, waits for them, and re-layouts: 7.92 us -> 8.53 us
  transfers between devices with their start and end apart: 31 -> 31, of which waited for: 4 -> 2; matrix products, arithmetic and copies ran while one was open for 13% -> 14% of each run, Pallas kernels for 64% -> 65%
where the time goes in v6:
time: 305 us; the launch traced here: 304 us
  Pallas kernels  201 us (66%)
  other arithmetic  34.5 us (11%)
  starting transfers between devices  30.3 us (10%)
  waiting for transfers between devices  22.1 us (7%)
  local copies, waits for them, and re-layouts  16.1 us (5%)
    pallas_call x12, Pallas kernels, sum_of_terms(): pl.pallas_call(functools.partial(term_kernel, kinds, streams, n_parts, le...  191 us
    slice x9, other arithmetic, halve(): array[middle:]  24.5 us
    ppermute x19, waiting for transfers between devices, on_device(): lax.ppermute(values, 'row', [(i, i ^ distance) for i in range(n_row)])  22 us
    ppermute x19, starting transfers between devices, on_device(): lax.ppermute(values, 'row', [(i, i ^ distance) for i in range(n_row)])  15.9 us
    ppermute x12, starting transfers between devices, on_device(): lax.ppermute(values, 'col', [(i, i ^ distance) for i in range(n_col)])  14.4 us
    pallas_call x3, Pallas kernels, place_copies(): pl.pallas_call(kernel, out_shape=[jax.ShapeDtypeStruct(shape, F32) for sh...  9.44 us
    unnamed x40, local copies, waits for them, and re-layouts  8.53 us
    add x5, other arithmetic, advance(): final = functools.reduce(jnp.add, [hold(sums[0], after), *sums[1:]])  7.53 us
  transfers between devices with their start and end apart: 31, of which 2 were waited for; matrix products, arithmetic and copies ran while one was open for 14% of the time, Pallas kernels for 65%

profile of v6, /device:TPU:0, one launch (start us, length us, event | category | flops | bytes accessed | tf_op | source)
XLA Modules:
  0.0 304.0 jit_solution(7469278258314001667)
XLA Ops:
  0.0 2.8 crossing.1.refs_1_
  4.7 2.5 collective-permute-start.4
  12.8 3.3 %pairs.1 = (f32[64,2048]{1,0:T(8,128)}, f32[64,2048]{1,0:T(8,128)}, f32[64,2048]{1,0:T(8,128)}, f32[64,2048]{1,0:T(8,128)}) custom-call(f32[32,16384]{1,0:T(8,128)} %refs_0_.15, f32[128,2048]{1,0:T(8,128)} %copy-done.13), custom_call_target="tpu_custom_call" | custom-call | tf_op jit(solution)/shard_map/pairs/pallas_call | solution.py:115
  17.8 2.6 collective-permute-start.2
  20.6 21.2 %first_term.2.refs_3_.refs_1_ = f32[4096,256]{1,0:T(8,128)} custom-call(s32[8]{0:T(128)} %copy-done.16, f32[4096,2048]{1,0:T(8,128)} %refs_0_.27, f32[2048,256]{1,0:T(8,128)} %refs_2_.1, f32[2048,256]{1,0:T(8,128)} %refs_2_.1, f32[64,2048]{1,0:T(8,128)} %get-tuple-element.12.refs_3_, f32[64,2048]{1,0:T(8,128)} %get-tuple-element.13.refs_4_, ...), custom_call_target="tpu_custom_call" | custom-call | flops 103079215104 | bytes 33554432 | tf_op jit(solution)/shard_map/first_term/pallas_call | solution.py:87
  43.3 21.2 %first_term.3.refs_4_.refs_3_ = f32[4096,256]{1,0:T(8,128)} custom-call(s32[8]{0:T(128)} %copy-done.16, f32[4096,2048]{1,0:T(8,128)} %refs_0_.27, f32[2048,128]{1,0:T(8,128)} %collective-permute-done.4.refs_1_, f32[2048,128]{1,0:T(8,128)} %copy-done.12, f32[4096,256]{1,0:T(8,128)} %first_term.2.refs_3_.refs_1_), custom_call_target="tpu_custom_call" | custom-call | flops 103079215104 | bytes 33554432 | tf_op jit(solution)/shard_map/first_term/pallas_call | solution.py:87
  64.5 3.3 %mirrored.1 = (f32[128,2048]{1,0:T(8,128)}, f32[128,2048]{1,0:T(8,128)}) custom-call(f32[64,2048]{1,0:T(8,128)} %get-tuple-element.11.refs_0_, f32[64,2048]{1,0:T(8,128)} %collective-permute-done.1.refs_1_, f32[64,2048]{1,0:T(8,128)} %collective-permute-done.2.refs_2_, f32[64,2048]{1,0:T(8,128)} %collective-permute-done.3.refs_3_, ...), custom_call_target="tpu_custom_call" | custom-call | tf_op jit(solution)/shard_map/mirrored/pallas_call | solution.py:115
  70.3 12.9 %second_term.4.refs_4_ = f32[2048,256]{1,0:T(8,128)} custom-call(s32[4]{0:T(128)} %get-tuple-element.49.tiles, f32[4096,2048]{1,0:T(8,128)} %refs_3_.11, f32[128,2048]{1,0:T(8,128)} %get-tuple-element.15.refs_1_, f32[128,2048]{1,0:T(8,128)} %get-tuple-element.16.refs_2_.refs_0_, f32[4096,256]{1,0:T(8,128)} %first_term.2.refs_3_.refs_1_, ...), custom_call_target="tpu_custom_call" | custom-call | flops 51539607552 | bytes 16777216 | tf_op jit(solution)/shard_map/second_term/pallas_call | solution.py:87
  83.3 12.9 %second_term.5.refs_4_.refs_1_ = f32[2048,256]{1,0:T(8,128)} custom-call(s32[4]{0:T(128)} %get-tuple-element.48.tiles, f32[4096,2048]{1,0:T(8,128)} %refs_3_.11, f32[128,2048]{1,0:T(8,128)} %get-tuple-element.15.refs_1_, f32[128,2048]{1,0:T(8,128)} %get-tuple-element.16.refs_2_.refs_0_, f32[4096,256]{1,0:T(8,128)} %first_term.2.refs_3_.refs_1_, ...), custom_call_target="tpu_custom_call" | custom-call | flops 51539607552 | bytes 16777216 | tf_op jit(solution)/shard_map/second_term/pallas_call | solution.py:87
  96.1 3.5 %fusion.8 = (f32[1024,256]{1,0:T(8,128)}, f32[1024,256]{1,0:T(8,128)S(1)}) fusion(f32[2048,256]{1,0:T(8,128)} %second_term.5.refs_4_.refs_1_, f32[2048,256]{1,0:T(8,128)S(1)} %collective-permute-done.8), kind=kLoop, calls=%fused_computation.47 | loop fusion | flops 262144 | bytes 5242880 | tf_op jit(solution)/shard_map/slice | solution.py:238
  103.5 12.9 %second_term.6.refs_4_ = f32[2048,256]{1,0:T(8,128)} custom-call(s32[4]{0:T(128)} %get-tuple-element.49.tiles, f32[4096,2048]{1,0:T(8,128)} %refs_3_.11, f32[128,2048]{1,0:T(8,128)} %collective-permute-done.6.refs_1_, f32[128,2048]{1,0:T(8,128)} %collective-permute-done.7.refs_2_.refs_0_, f32[4096,256]{1,0:T(8,128)} %first_term.3.refs_4_.refs_3_, ...), custom_call_target="tpu_custom_call" | custom-call | flops 51539607552 | bytes 16777216 | tf_op jit(solution)/shard_map/second_term/pallas_call | solution.py:87
  117.0 12.9 %second_term.7.refs_1_.refs_6_ = f32[2048,256]{1,0:T(8,128)} custom-call(s32[4]{0:T(128)} %get-tuple-element.48.tiles, f32[4096,2048]{1,0:T(8,128)} %refs_3_.11, f32[128,2048]{1,0:T(8,128)} %collective-permute-done.6.refs_1_, f32[128,2048]{1,0:T(8,128)} %collective-permute-done.7.refs_2_.refs_0_, f32[4096,256]{1,0:T(8,128)} %first_term.3.refs_4_.refs_3_, ...), custom_call_target="tpu_custom_call" | custom-call | flops 51539607552 | bytes 16777216 | tf_op jit(solution)/shard_map/second_term/pallas_call | solution.py:87
  129.9 3.4 %fusion.6 = (f32[1024,256]{1,0:T(8,128)}, f32[1024,256]{1,0:T(8,128)}) fusion(f32[2048,256]{1,0:T(8,128)} %second_term.7.refs_1_.refs_6_, f32[2048,256]{1,0:T(8,128)} %collective-permute-done.11), kind=kLoop, calls=%fused_computation.45 | loop fusion | flops 262144 | bytes 5242880 | tf_op jit(solution)/shard_map/slice | solution.py:238
  138.7 22.0 %both_terms.6.refs_6_ = f32[2048,256]{1,0:T(8,128)} custom-call(s32[8]{0:T(128)} %slice.241.tiles, f32[4096,2048]{1,0:T(8,128)} %refs_0_.27, f32[2048,128]{1,0:T(8,128)} %hold.22.refs_1_, f32[2048,128]{1,0:T(8,128)} %collective-permute-done.10.refs_7_.refs_4_.refs_2_, f32[4096,2048]{1,0:T(8,128)} %refs_3_.11, f32[128,2048]{1,0:T(8,128)} %hold.25.refs_4_, ...), custom_call_target="tpu_custom_call" | custom-call | flops 103079215104 | bytes 33554432 | tf_op jit(solution)/shard_map/both_terms/pallas_call | solution.py:87
  162.2 21.8 %both_terms.7.refs_1_.refs_6_ = f32[2048,256]{1,0:T(8,128)} custom-call(s32[8]{0:T(128)} %slice.239.tiles, f32[4096,2048]{1,0:T(8,128)} %refs_0_.27, f32[2048,128]{1,0:T(8,128)} %hold.22.refs_1_, f32[2048,128]{1,0:T(8,128)} %collective-permute-done.10.refs_7_.refs_4_.refs_2_, f32[4096,2048]{1,0:T(8,128)} %refs_3_.11, f32[128,2048]{1,0:T(8,128)} %hold.25.refs_4_, ...), custom_call_target="tpu_custom_call" | custom-call | flops 103079215104 | bytes 33554432 | tf_op jit(solution)/shard_map/both_terms/pallas_call | solution.py:87
  184.0 3.9 %fusion.5 = (f32[1024,256]{1,0:T(8,128)}, f32[1024,256]{1,0:T(8,128)}) fusion(f32[2048,256]{1,0:T(8,128)} %both_terms.7.refs_1_.refs_6_, f32[2048,256]{1,0:T(8,128)S(1)} %collective-permute-done.19), kind=kLoop, calls=%fused_computation.44 | loop fusion | flops 262144 | bytes 5242880 | tf_op jit(solution)/shard_map/slice | solution.py:238
  190.9 2.6 fusion.12
  195.6 13.3 %both_terms.8.refs_6_ = f32[1024,256]{1,0:T(8,128)} custom-call(s32[4]{0:T(128)} %get-tuple-element.43.tiles, f32[4096,2048]{1,0:T(8,128)} %refs_0_.27, f32[2048,128]{1,0:T(8,128)} %collective-permute-done.12.refs_7_.refs_1_, f32[2048,128]{1,0:T(8,128)} %collective-permute-done.14.refs_2_, f32[4096,2048]{1,0:T(8,128)} %refs_3_.11, f32[128,2048]{1,0:T(8,128)} %copy-done.18, ...), custom_call_target="tpu_custom_call" | custom-call | flops 51539607552 | bytes 16777216 | tf_op jit(solution)/shard_map/both_terms/pallas_call | solution.py:87
  208.9 13.3 %both_terms.9.refs_6_ = f32[1024,256]{1,0:T(8,128)} custom-call(s32[4]{0:T(128)} %get-tuple-element.44.tiles, f32[4096,2048]{1,0:T(8,128)} %refs_0_.27, f32[2048,128]{1,0:T(8,128)} %collective-permute-done.12.refs_7_.refs_1_, f32[2048,128]{1,0:T(8,128)} %collective-permute-done.14.refs_2_, f32[4096,2048]{1,0:T(8,128)} %refs_3_.11, f32[128,2048]{1,0:T(8,128)} %copy-done.18, ...), custom_call_target="tpu_custom_call" | custom-call | flops 51539607552 | bytes 16777216 | tf_op jit(solution)/shard_map/both_terms/pallas_call | solution.py:87
  222.3 2.5 fusion.10
  225.6 13.6 %both_terms.10.refs_1_.refs_6_ = f32[1024,256]{1,0:T(8,128)} custom-call(s32[4]{0:T(128)} %get-tuple-element.42.tiles, f32[4096,2048]{1,0:T(8,128)} %refs_0_.27, f32[2048,128]{1,0:T(8,128)} %collective-permute-done.12.refs_7_.refs_1_, f32[2048,128]{1,0:T(8,128)} %collective-permute-done.14.refs_2_, f32[4096,2048]{1,0:T(8,128)} %refs_3_.11, ...), custom_call_target="tpu_custom_call" | custom-call | flops 51539607552 | bytes 16777216 | tf_op jit(solution)/shard_map/both_terms/pallas_call | solution.py:87
  250.5 13.3 %both_terms.11.refs_1_ = f32[1024,256]{1,0:T(8,128)} custom-call(s32[4]{0:T(128)} %get-tuple-element.41.tiles, f32[4096,2048]{1,0:T(8,128)} %refs_0_.27, f32[2048,128]{1,0:T(8,128)} %collective-permute-done.12.refs_7_.refs_1_, f32[2048,128]{1,0:T(8,128)} %collective-permute-done.14.refs_2_, f32[4096,2048]{1,0:T(8,128)} %refs_3_.11, f32[128,2048]{1,0:T(8,128)} %copy-done.18, ...), custom_call_target="tpu_custom_call" | custom-call | flops 51539607552 | bytes 16777216 | tf_op jit(solution)/shard_map/both_terms/pallas_call | solution.py:87
  274.3 11.4 %collective-permute-done.28 = f32[512,256]{1,0:T(8,128)} collective-permute-done((f32[512,256]{1,0:T(8,128)S(1)}, f32[512,256]{1,0:T(8,128)}, u32[]{:S(2)}, u32[]{:S(2)}) %collective-permute-start.28) | collective-permute-done | bytes 524320 | tf_op jit(solution)/shard_map/ppermute | solution.py:147
  290.9 10.6 %collective-permute-done.30 = f32[256,256]{1,0:T(8,128)S(1)} collective-permute-done((f32[256,256]{1,0:T(8,128)S(1)}, f32[256,256]{1,0:T(8,128)S(1)}, u32[]{:S(2)}, u32[]{:S(2)}) %collective-permute-start.30) | collective-permute-done | bytes 262176 | tf_op jit(solution)/shard_map/ppermute | solution.py:147
  (146 shorter events, 60.2 us)
Async XLA Ops:
  4.7 37.1 %collective-permute-start.4 = (f32[2048,128]{1,0:T(8,128)}, f32[2048,128]{1,0:T(8,128)}, u32[]{:S(2)}, u32[]{:S(2)}) collective-permute-start(f32[2048,128]{1,0:T(8,128)} %hold.18), channel_id=1, source_target_pairs={{0,8},{8,0},{16,24},{24,16},{1,9},{9,1},{17,25},{25,17},{2,10},{10... | collective-permute-start | bytes 3145736 | tf_op jit(solution)/shard_map/ppermute | solution.py:148
  7.2 35.1 %collective-permute-start.5 = (f32[2048,128]{1,0:T(8,128)}, f32[2048,128]{1,0:T(8,128)S(1)}, u32[]{:S(2)}, u32[]{:S(2)}) collective-permute-start(f32[2048,128]{1,0:T(8,128)} %hold.18), channel_id=1, source_target_pairs={{0,16},{8,24},{16,0},{24,8},{1,17},{9,25},{17,1},{25,9},{2,18},{10... | collective-permute-start | bytes 3145736 | tf_op jit(solution)/shard_map/ppermute | solution.py:148
  16.2 48.3 %collective-permute-start.1 = (f32[64,2048]{1,0:T(8,128)}, f32[64,2048]{1,0:T(8,128)}, u32[]{:S(2)}, u32[]{:S(2)}) collective-permute-start(f32[64,2048]{1,0:T(8,128)} %get-tuple-element.12.refs_3_), channel_id=1, source_target_pairs={{0,2},{1,3},{2,0},{3,1},{4,6},{5,7},{6,4},{7,5},{8,10},{9,11},{10,... | collective-permute-start | bytes 1572872 | tf_op jit(solution)/shard_map/ppermute | solution.py:147
  17.8 46.7 %collective-permute-start.2 = (f32[64,2048]{1,0:T(8,128)}, f32[64,2048]{1,0:T(8,128)}, u32[]{:S(2)}, u32[]{:S(2)}) collective-permute-start(f32[64,2048]{1,0:T(8,128)} %get-tuple-element.13.refs_4_), channel_id=1, source_target_pairs={{0,4},{1,5},{2,6},{3,7},{4,0},{5,1},{6,2},{7,3},{8,12},{9,13},{10,... | collective-permute-start | bytes 1572872 | tf_op jit(solution)/shard_map/ppermute | solution.py:147
  20.3 44.1 %collective-permute-start.3 = (f32[64,2048]{1,0:T(8,128)}, f32[64,2048]{1,0:T(8,128)}, u32[]{:S(2)}, u32[]{:S(2)}) collective-permute-start(f32[64,2048]{1,0:T(8,128)} %get-tuple-element.14.refs_5_), channel_id=1, source_target_pairs={{0,6},{1,7},{2,4},{3,5},{4,2},{5,3},{6,0},{7,1},{8,14},{9,15},{10,... | collective-permute-start | bytes 1572872 | tf_op jit(solution)/shard_map/ppermute | solution.py:147
  41.8 58.8 %collective-permute-start.9 = (f32[2048,128]{1,0:T(8,128)}, f32[2048,128]{1,0:T(8,128)}, u32[]{:S(2)}, u32[]{:S(2)}) collective-permute-start(f32[2048,128]{1,0:T(8,128)} %hold.19), channel_id=1, source_target_pairs={{0,8},{8,0},{16,24},{24,16},{1,9},{9,1},{17,25},{25,17},{2,10},{10... | collective-permute-start | bytes 3145736 | tf_op jit(solution)/shard_map/ppermute | solution.py:148
  42.3 58.3 %collective-permute-start.10 = (f32[2048,128]{1,0:T(8,128)}, f32[2048,128]{1,0:T(8,128)}, u32[]{:S(2)}, u32[]{:S(2)}) collective-permute-start(f32[2048,128]{1,0:T(8,128)} %hold.19), channel_id=1, source_target_pairs={{0,16},{8,24},{16,0},{24,8},{1,17},{9,25},{17,1},{25,9},{2,18},{10... | collective-permute-start | bytes 3145736 | tf_op jit(solution)/shard_map/ppermute | solution.py:148
  67.8 35.7 %collective-permute-start.7 = (f32[128,2048]{1,0:T(8,128)}, f32[128,2048]{1,0:T(8,128)}, u32[]{:S(2)}, u32[]{:S(2)}) collective-permute-start(f32[128,2048]{1,0:T(8,128)} %get-tuple-element.15.refs_1_), channel_id=1, source_target_pairs={{0,16},{8,24},{16,0},{24,8},{1,17},{9,25},{17,1},{25,9},{2,18},{10... | collective-permute-start | bytes 3145736 | tf_op jit(solution)/shard_map/ppermute | solution.py:148
  68.9 34.6 %collective-permute-start.6 = (f32[128,2048]{1,0:T(8,128)}, f32[128,2048]{1,0:T(8,128)}, u32[]{:S(2)}, u32[]{:S(2)}) collective-permute-start(f32[128,2048]{1,0:T(8,128)} %get-tuple-element.15.refs_1_), channel_id=1, source_target_pairs={{0,8},{8,0},{16,24},{24,16},{1,9},{9,1},{17,25},{25,17},{2,10},{10... | collective-permute-start | bytes 3145736 | tf_op jit(solution)/shard_map/ppermute | solution.py:148
  99.6 34.5 %collective-permute-start.13 = (f32[1024,256]{1,0:T(8,128)S(1)}, f32[1024,256]{1,0:T(8,128)}, u32[]{:S(2)}, u32[]{:S(2)}) collective-permute-start(f32[1024,256]{1,0:T(8,128)S(1)} %get-tuple-element.24.refs_5_.refs_2_), channel_id=1, source_target_pairs={{0,2},{1,3},{2,0},{3,1},{4,6},{5,7},{6,4},{7,5},{8,10},{9,11},{10,... | collective-permute-start | bytes 3145736 | tf_op jit(solution)/shard_map/ppermute | solution.py:147
  100.6 36.9 %collective-permute-start.16 = (f32[128,2048]{1,0:T(8,128)}, f32[128,2048]{1,0:T(8,128)}, u32[]{:S(2)}, u32[]{:S(2)}) collective-permute-start(f32[128,2048]{1,0:T(8,128)} %hold.24), channel_id=1, source_target_pairs={{0,8},{8,0},{16,24},{24,16},{1,9},{9,1},{17,25},{25,17},{2,10},{10... | collective-permute-start | bytes 3145736 | tf_op jit(solution)/shard_map/ppermute | solution.py:148
  102.0 36.7 %collective-permute-start.18 = (f32[128,2048]{1,0:T(8,128)}, f32[128,2048]{1,0:T(8,128)}, u32[]{:S(2)}, u32[]{:S(2)}) collective-permute-start(f32[128,2048]{1,0:T(8,128)} %hold.24), channel_id=1, source_target_pairs={{0,16},{8,24},{16,0},{24,8},{1,17},{9,25},{17,1},{25,9},{2,18},{10... | collective-permute-start | bytes 3145736 | tf_op jit(solution)/shard_map/ppermute | solution.py:148
  116.4 44.3 %collective-permute-start.12 = (f32[2048,128]{1,0:T(8,128)}, f32[2048,128]{1,0:T(8,128)}, u32[]{:S(2)}, u32[]{:S(2)}) collective-permute-start(f32[2048,128]{1,0:T(8,128)} %hold.21), channel_id=1, source_target_pairs={{0,8},{8,0},{16,24},{24,16},{1,9},{9,1},{17,25},{25,17},{2,10},{10... | collective-permute-start | bytes 3145736 | tf_op jit(solution)/shard_map/ppermute | solution.py:148
  133.3 55.7 %collective-permute-start.20 = (f32[1024,256]{1,0:T(8,128)}, f32[1024,256]{1,0:T(8,128)}, u32[]{:S(2)}, u32[]{:S(2)}) collective-permute-start(f32[1024,256]{1,0:T(8,128)} %get-tuple-element.20.refs_2_.refs_7_), channel_id=1, source_target_pairs={{0,2},{1,3},{2,0},{3,1},{4,6},{5,7},{6,4},{7,5},{8,10},{9,11},{10,... | collective-permute-start | bytes 3145736 | tf_op jit(solution)/shard_map/ppermute | solution.py:147
  136.6 56.9 %collective-permute-start.14 = (f32[2048,128]{1,0:T(8,128)}, f32[2048,128]{1,0:T(8,128)}, u32[]{:S(2)}, u32[]{:S(2)}) collective-permute-start(f32[2048,128]{1,0:T(8,128)} %hold.22.refs_1_), channel_id=1, source_target_pairs={{0,16},{8,24},{16,0},{24,8},{1,17},{9,25},{17,1},{25,9},{2,18},{10... | collective-permute-start | bytes 3145736 | tf_op jit(solution)/shard_map/ppermute | solution.py:148
  137.5 57.1 %collective-permute-start.17 = (f32[128,2048]{1,0:T(8,128)}, f32[128,2048]{1,0:T(8,128)}, u32[]{:S(2)}, u32[]{:S(2)}) collective-permute-start(f32[128,2048]{1,0:T(8,128)} %hold.25.refs_4_), channel_id=1, source_target_pairs={{0,16},{8,24},{16,0},{24,8},{1,17},{9,25},{17,1},{25,9},{2,18},{10... | collective-permute-start | bytes 3145736 | tf_op jit(solution)/shard_map/ppermute | solution.py:148
  160.7 23.4 %collective-permute-start.19 = (f32[2048,256]{1,0:T(8,128)}, f32[2048,256]{1,0:T(8,128)S(1)}, u32[]{:S(2)}, u32[]{:S(2)}) collective-permute-start(f32[2048,256]{1,0:T(8,128)} %both_terms.6.refs_6_), channel_id=1, source_target_pairs={{0,1},{1,0},{2,3},{3,2},{4,5},{5,4},{6,7},{7,6},{8,9},{9,8},{10,11... | collective-permute-start | bytes 6291464 | tf_op jit(solution)/shard_map/ppermute | solution.py:147
  160.7 33.9 %collective-permute-start.15 = (f32[128,2048]{1,0:T(8,128)}, f32[128,2048]{1,0:T(8,128)S(1)}, u32[]{:S(2)}, u32[]{:S(2)}) collective-permute-start(f32[128,2048]{1,0:T(8,128)} %hold.23), channel_id=1, source_target_pairs={{0,8},{8,0},{16,24},{24,16},{1,9},{9,1},{17,25},{25,17},{2,10},{10... | collective-permute-start | bytes 3145736 | tf_op jit(solution)/shard_map/ppermute | solution.py:148
  187.9 51.8 %collective-permute-start.22 = (f32[1024,256]{1,0:T(8,128)}, f32[1024,256]{1,0:T(8,128)}, u32[]{:S(2)}, u32[]{:S(2)}) collective-permute-start(f32[1024,256]{1,0:T(8,128)} %get-tuple-element.18.refs_2_.refs_7_), channel_id=1, source_target_pairs={{0,2},{1,3},{2,0},{3,1},{4,6},{5,7},{6,4},{7,5},{8,10},{9,11},{10,... | collective-permute-start | bytes 3145736 | tf_op jit(solution)/shard_map/ppermute | solution.py:147
  189.0 55.1 %collective-permute-start.23 = (f32[512,256]{1,0:T(8,128)}, f32[512,256]{1,0:T(8,128)}, u32[]{:S(2)}, u32[]{:S(2)}) collective-permute-start(f32[512,256]{1,0:T(8,128)} %hold.29), channel_id=1, source_target_pairs={{0,4},{1,5},{2,6},{3,7},{4,0},{5,1},{6,2},{7,3},{8,12},{9,13},{10,... | collective-permute-start | bytes 1572872 | tf_op jit(solution)/shard_map/ppermute | solution.py:147
  193.6 53.9 %collective-permute-start.24 = (f32[512,256]{1,0:T(8,128)}, f32[512,256]{1,0:T(8,128)}, u32[]{:S(2)}, u32[]{:S(2)}) collective-permute-start(f32[512,256]{1,0:T(8,128)} %get-tuple-element.32.refs_8_), channel_id=1, source_target_pairs={{0,4},{1,5},{2,6},{3,7},{4,0},{5,1},{6,2},{7,3},{8,12},{9,13},{10,... | collective-permute-start | bytes 1572872 | tf_op jit(solution)/shard_map/ppermute | solution.py:147
  224.7 42.5 %collective-permute-start.26 = (f32[512,256]{1,0:T(8,128)S(1)}, f32[512,256]{1,0:T(8,128)}, u32[]{:S(2)}, u32[]{:S(2)}) collective-permute-start(f32[512,256]{1,0:T(8,128)S(1)} %get-tuple-element.28.refs_7_), channel_id=1, source_target_pairs={{0,2},{1,3},{2,0},{3,1},{4,6},{5,7},{6,4},{7,5},{8,10},{9,11},{10,... | collective-permute-start | bytes 1572872 | tf_op jit(solution)/shard_map/ppermute | solution.py:147
  239.2 24.6 %collective-permute-start.25 = (f32[1024,256]{1,0:T(8,128)}, f32[1024,256]{1,0:T(8,128)}, u32[]{:S(2)}, u32[]{:S(2)}) collective-permute-start(f32[1024,256]{1,0:T(8,128)} %both_terms.10.refs_1_.refs_6_), channel_id=1, source_target_pairs={{0,1},{1,0},{2,3},{3,2},{4,5},{5,4},{6,7},{7,6},{8,9},{9,8},{10,11... | collective-permute-start | bytes 3145736 | tf_op jit(solution)/shard_map/ppermute | solution.py:147
  242.2 27.8 %collective-permute-start.27 = (f32[512,256]{1,0:T(8,128)S(1)}, f32[512,256]{1,0:T(8,128)}, u32[]{:S(2)}, u32[]{:S(2)}) collective-permute-start(f32[512,256]{1,0:T(8,128)S(1)} %get-tuple-element.30.refs_2_.refs_7_), channel_id=1, source_target_pairs={{0,4},{1,5},{2,6},{3,7},{4,0},{5,1},{6,2},{7,3},{8,12},{9,13},{10,... | collective-permute-start | bytes 1572872 | tf_op jit(solution)/shard_map/ppermute | solution.py:147
  (26 other events, 195.7 us)
